TPU v7x, 128 devices: a whole 4x4x4 slice. The times are simulated.
128 devices in a mesh: dp: 8 (over x, z_hi), sq: 8 (over z_lo, y), hd: 2 (over core).
Axes of the slice: x: 4, y: 4, z: 4 (z_hi: 2, z_lo: 2; z = z_hi * 2 + z_lo), core: 2. Of those that a mesh axis runs over, the one named last changes fastest.
Arguments:
- inputs: bfloat16 [8, 2048, 1536], P('dp', ('sq', 'hd')), may hold values from -6 to 6
- norm_gain: float32 [1536], replicated, may hold values from 0.5 to 1.5
- w_query: bfloat16 [1536, 1536], P(('sq', 'hd')), may hold values from -0.15625 to 0.15625
- w_key: bfloat16 [1536, 512], P(('sq', 'hd')), may hold values from -0.15625 to 0.15625
- w_value: bfloat16 [1536, 512], P(('sq', 'hd')), may hold values from -0.15625 to 0.15625
- w_out: bfloat16 [1536, 1536], P(('sq', 'hd')), may hold values from -0.625 to 0.625
- query_gain: float32 [64], replicated, may hold values from 0.5 to 1.5
- key_gain: float32 [64], replicated, may hold values from 0.5 to 1.5
- ffn_gain: float32 [1536], replicated, may hold values from 0.5 to 1.5
- w_gate: bfloat16 [1536, 6912], P(('sq', 'hd')), may hold values from -0.15625 to 0.15625
- w_up: bfloat16 [1536, 6912], P(('sq', 'hd')), may hold values from -0.15625 to 0.15625
- w_down: bfloat16 [6912, 1536], P(('sq', 'hd')), may hold values from -0.078125 to 0.078125
- cotangent: bfloat16 [8, 2048, 1536], P('dp', ('sq', 'hd')), may hold values from -6 to 6
Outputs:
- output: bfloat16 [8, 2048, 1536], P('dp', ('sq', 'hd'))
- input_grad: float32 [8, 2048, 1536], P('dp', ('sq', 'hd'))
- norm_gain_grad: float32 [1536], replicated
- w_query_grad: float32 [1536, 1536], P(('sq', 'hd'))
- w_key_grad: float32 [1536, 512], P(('sq', 'hd'))
- w_value_grad: float32 [1536, 512], P(('sq', 'hd'))
- w_out_grad: float32 [1536, 1536], P(('sq', 'hd'))
- query_gain_grad: float32 [64], replicated
- key_gain_grad: float32 [64], replicated
- ffn_gain_grad: float32 [1536], replicated
- w_gate_grad: float32 [1536, 6912], P(('sq', 'hd'))
- w_up_grad: float32 [1536, 6912], P(('sq', 'hd'))
- w_down_grad: float32 [6912, 1536], P(('sq', 'hd'))
All inputs are finite; a program needn't handle non-finite values.
Results may differ from a plain program's by a relative error of at most 0.025.
Values may be sent and summed in bfloat16 or wider, within the bound.
No kernel may reach another device: no remote copies, remote signals or barrier semaphores. Data moves between devices by JAX's collectives and lax.ppermute only.
A program may use at most 256 MiB of HBM per device.

v0:
```python
import jax
import jax.numpy as jnp
from jax import lax
from jax.sharding import PartitionSpec as P

HQ = 24
HK = 8
HS = 64


EPSILON = 1e-05
ROPE_BASE = 1000000.0
SCORE_SCALE = 0.125
MASKED = -1e30


def rms_forward(values, gain):
    factor = lax.rsqrt(jnp.mean(values * values, axis=-1, keepdims=True) + EPSILON)
    return values * factor * gain


def rms_backward(values, gain, grad_out):
    factor = lax.rsqrt(jnp.mean(values * values, axis=-1, keepdims=True) + EPSILON)
    normal = values * factor
    scaled = grad_out * gain
    grad_in = factor * (scaled - normal * jnp.mean(scaled * normal, axis=-1, keepdims=True))
    grad_gain = jnp.sum((grad_out * normal).reshape(-1, values.shape[-1]), axis=0)
    return (grad_in, grad_gain)


def rope_tables(positions, width):
    half = width // 2
    freqs = ROPE_BASE ** (-jnp.arange(half, dtype=jnp.float32) * 2.0 / width)
    angles = positions[:, None].astype(jnp.float32) * freqs[None, :]
    return (jnp.cos(angles)[:, None, :], jnp.sin(angles)[:, None, :])


def rotate(values, cosine, sine):
    half = values.shape[-1] // 2
    first = values[..., :half]
    second = values[..., half:]
    return jnp.concatenate(
        [first * cosine - second * sine, second * cosine + first * sine], axis=-1
    )


def unrotate(grads, cosine, sine):
    half = grads.shape[-1] // 2
    first = grads[..., :half]
    second = grads[..., half:]
    return jnp.concatenate(
        [first * cosine + second * sine, second * cosine - first * sine], axis=-1
    )


def fold_rows(inputs, weight_shard):
    return jnp.dot(
        inputs,
        lax.all_gather(weight_shard, ("sq", "hd"), axis=0, tiled=True),
        preferred_element_type=jnp.float32,
    )


def map_rows(grads, weight_shard):
    return lax.dot_general(
        grads,
        lax.all_gather(weight_shard, ("sq", "hd"), axis=0, tiled=True),
        (((1,), (1,)), ((), ())),
        preferred_element_type=jnp.float32,
    )


def weight_terms(inputs, grads):
    return lax.psum_scatter(
        lax.dot_general(
            inputs, grads, (((0,), (0,)), ((), ())), preferred_element_type=jnp.float32
        ).astype(jnp.bfloat16),
        ("sq", "hd"),
        scatter_dimension=0,
        tiled=True,
    ).astype(jnp.float32)


def column_terms(inputs, grads):
    return weight_terms(inputs, grads)


def on_device(
    inputs,
    norm_gain,
    w_query,
    w_key,
    w_value,
    w_out,
    query_gain,
    key_gain,
    ffn_gain,
    w_gate,
    w_up,
    w_down,
    cotangent,
):
    hd_count = lax.axis_size("hd")
    tokens = inputs[0]
    tok_rows = tokens.shape[0]
    block_len = tok_rows * hd_count
    query_local = HQ // hd_count
    kv_local = HK // hd_count
    group = HQ // HK
    query_width = HQ * HS
    kv_width = HK * HS
    ffn_width = w_gate.shape[1]
    tokens32 = tokens.astype(jnp.float32)
    normed = rms_forward(tokens32, norm_gain).astype(jnp.bfloat16)
    w_joint = jnp.concatenate([w_query, w_key, w_value], axis=1)
    joint = fold_rows(normed, w_joint)
    query_lin = (
        joint[:, :query_width].astype(jnp.bfloat16).reshape(tok_rows, hd_count, query_local * HS)
    )
    key_lin = (
        joint[:, query_width : query_width + kv_width]
        .astype(jnp.bfloat16)
        .reshape(tok_rows, hd_count, kv_local * HS)
    )
    value_lin = (
        joint[:, query_width + kv_width :]
        .astype(jnp.bfloat16)
        .reshape(tok_rows, hd_count, kv_local * HS)
    )
    query_heads, key_heads, value_heads = (
        lax.all_to_all(query_lin, "hd", split_axis=1, concat_axis=0, tiled=True),
        lax.all_to_all(key_lin, "hd", split_axis=1, concat_axis=0, tiled=True),
        lax.all_to_all(value_lin, "hd", split_axis=1, concat_axis=0, tiled=True),
    )
    block_index = lax.axis_index("sq")
    positions = block_index * block_len + jnp.arange(block_len, dtype=jnp.int32)
    cosine, sine = rope_tables(positions, HS)
    query32 = query_heads.reshape(block_len, query_local, HS).astype(jnp.float32)
    key32 = key_heads.reshape(block_len, kv_local, HS).astype(jnp.float32)
    query_rot = (
        rotate(rms_forward(query32, query_gain), cosine, sine)
        .astype(jnp.bfloat16)
        .reshape(block_len, kv_local, group, HS)
    )
    key_rot = (
        rotate(rms_forward(key32, key_gain), cosine, sine)
        .astype(jnp.bfloat16)
        .reshape(block_len, kv_local * HS)
    )
    value_flat = value_heads.reshape(block_len, kv_local * HS)
    key_whole, value_whole = (
        lax.all_gather(key_rot, "sq", axis=0, tiled=True),
        lax.all_gather(value_flat, "sq", axis=0, tiled=True),
    )
    last_block = block_index + 1

    def block_scores(index, key_source):
        key_block = lax.dynamic_slice_in_dim(key_source, index * block_len, block_len, 0).reshape(
            block_len, kv_local, HS
        )
        scores = (
            jnp.einsum("qhgd,khd->hgqk", query_rot, key_block, preferred_element_type=jnp.float32)
            * SCORE_SCALE
        )
        key_pos = index * block_len + jnp.arange(block_len, dtype=jnp.int32)
        return jnp.where(positions[:, None] >= key_pos[None, :], scores, MASKED)

    def peak_step(index, carry):
        peak, total = carry
        scores = block_scores(index, key_whole)
        new_peak = jnp.maximum(peak, jnp.max(scores, axis=-1))
        total = total * jnp.exp(peak - new_peak) + jnp.sum(
            jnp.exp(scores - new_peak[..., None]), axis=-1
        )
        return (new_peak, total)

    start_peak = jnp.full((kv_local, group, block_len), MASKED, jnp.float32)
    peak, total = lax.fori_loop(0, last_block, peak_step, (start_peak, jnp.zeros_like(start_peak)))
    log_total = peak + jnp.log(total)

    def output_step(index, carry):
        result, extra = carry
        weights = jnp.exp(block_scores(index, key_whole) - log_total[..., None])
        rounded = weights.astype(jnp.bfloat16)
        leftover = (weights - rounded.astype(jnp.float32)).astype(jnp.bfloat16)
        value_block = lax.dynamic_slice_in_dim(
            value_whole, index * block_len, block_len, 0
        ).reshape(block_len, kv_local, HS)
        result = result + jnp.einsum(
            "hgqk,khd->qhgd", rounded, value_block, preferred_element_type=jnp.float32
        )
        extra = extra + jnp.einsum(
            "hgqk,khd->qhgd", leftover, value_block, preferred_element_type=jnp.float32
        )
        return (result, extra)

    empty_out = jnp.zeros((block_len, kv_local, group, HS), jnp.float32)
    result, extra = lax.fori_loop(0, last_block, output_step, (empty_out, empty_out))
    attn_full = result + extra
    attn_heads = result.astype(jnp.bfloat16).reshape(block_len, 1, query_local * HS)
    attended = lax.all_to_all(attn_heads, "hd", split_axis=0, concat_axis=1, tiled=True).reshape(
        tok_rows, query_width
    )
    middle = tokens32 + fold_rows(attended, w_out)
    ffn_in = rms_forward(middle, ffn_gain).astype(jnp.bfloat16)
    w_joint_ffn = jnp.concatenate([w_gate, w_up], axis=1)
    gate_up = fold_rows(ffn_in, w_joint_ffn)
    gate = gate_up[:, :ffn_width]
    up_val = gate_up[:, ffn_width:]
    hidden = (jax.nn.silu(gate) * up_val).astype(jnp.bfloat16)
    output = (middle + fold_rows(hidden, w_down)).astype(jnp.bfloat16)
    out_grad = cotangent[0]
    hidden_grad = map_rows(out_grad, w_down)
    grad_down = column_terms(hidden, out_grad)
    sigmoid = jax.nn.sigmoid(gate)
    gate_grad = hidden_grad * up_val * sigmoid * (1.0 + gate * (1.0 - sigmoid))
    up_grad = hidden_grad * gate * sigmoid
    joint_ffn_grad = jnp.concatenate([gate_grad, up_grad], axis=1).astype(jnp.bfloat16)
    ffn_in_grad = map_rows(joint_ffn_grad, w_joint_ffn)
    grad_ffn = weight_terms(ffn_in, joint_ffn_grad)
    middle_part, ffn_gain_part = rms_backward(middle, ffn_gain, ffn_in_grad)
    middle_grad = out_grad.astype(jnp.float32) + middle_part
    branch_grad = middle_grad.astype(jnp.bfloat16)
    attended_grad = map_rows(branch_grad, w_out)
    grad_out = column_terms(attended, branch_grad)
    attended_send = attended_grad.astype(jnp.bfloat16).reshape(tok_rows, hd_count, query_local * HS)
    head_grad = lax.all_to_all(
        attended_send, "hd", split_axis=1, concat_axis=0, tiled=True
    ).reshape(block_len, kv_local, group, HS)
    delta = jnp.sum(head_grad.astype(jnp.float32) * attn_full, axis=-1).transpose(1, 2, 0)
    key_back, value_back = (
        lax.all_gather(key_rot, "sq", axis=0, tiled=True),
        lax.all_gather(value_flat, "sq", axis=0, tiled=True),
    )

    def grad_step(index, carry):
        query_grad, key_term, value_term = carry
        weights = jnp.exp(block_scores(index, key_back) - log_total[..., None])
        rounded = weights.astype(jnp.bfloat16)
        key_block = lax.dynamic_slice_in_dim(key_back, index * block_len, block_len, 0).reshape(
            block_len, kv_local, HS
        )
        value_block = lax.dynamic_slice_in_dim(value_back, index * block_len, block_len, 0).reshape(
            block_len, kv_local, HS
        )
        value_part = jnp.einsum(
            "hgqk,qhgd->khd", rounded, head_grad, preferred_element_type=jnp.float32
        )
        prob_grad = jnp.einsum(
            "qhgd,khd->hgqk", head_grad, value_block, preferred_element_type=jnp.float32
        )
        score_grad = (weights * (prob_grad - delta[..., None])).astype(jnp.bfloat16)
        query_grad = (
            query_grad
            + jnp.einsum(
                "hgqk,khd->qhgd", score_grad, key_block, preferred_element_type=jnp.float32
            )
            * SCORE_SCALE
        )
        key_part = (
            jnp.einsum("hgqk,qhgd->khd", score_grad, query_rot, preferred_element_type=jnp.float32)
            * SCORE_SCALE
        )
        key_term = lax.dynamic_update_slice_in_dim(
            key_term, key_part.reshape(block_len, kv_local * HS), index * block_len, 0
        )
        value_term = lax.dynamic_update_slice_in_dim(
            value_term, value_part.reshape(block_len, kv_local * HS), index * block_len, 0
        )
        return (query_grad, key_term, value_term)

    whole_terms = jnp.zeros((key_back.shape[0], kv_local * HS), jnp.float32)
    query_grad, key_term, value_term = lax.fori_loop(
        0, last_block, grad_step, (empty_out, whole_terms, whole_terms)
    )
    key_sum, value_sum = (
        lax.psum_scatter(
            key_term.astype(jnp.bfloat16), "sq", scatter_dimension=0, tiled=True
        ).astype(jnp.float32),
        lax.psum_scatter(
            value_term.astype(jnp.bfloat16), "sq", scatter_dimension=0, tiled=True
        ).astype(jnp.float32),
    )
    query_turned = unrotate(query_grad.reshape(block_len, query_local, HS), cosine, sine)
    query_lin_grad, query_gain_part = rms_backward(query32, query_gain, query_turned)
    key_turned = unrotate(key_sum.reshape(block_len, kv_local, HS), cosine, sine)
    key_lin_grad, key_gain_part = rms_backward(key32, key_gain, key_turned)
    query_send = query_lin_grad.astype(jnp.bfloat16).reshape(block_len, 1, query_local * HS)
    key_send = key_lin_grad.astype(jnp.bfloat16).reshape(block_len, 1, kv_local * HS)
    value_send = value_sum.astype(jnp.bfloat16).reshape(block_len, 1, kv_local * HS)
    query_back, key_back_grad, value_back_grad = (
        lax.all_to_all(query_send, "hd", split_axis=0, concat_axis=1, tiled=True),
        lax.all_to_all(key_send, "hd", split_axis=0, concat_axis=1, tiled=True),
        lax.all_to_all(value_send, "hd", split_axis=0, concat_axis=1, tiled=True),
    )
    joint_grad = jnp.concatenate(
        [
            query_back.reshape(tok_rows, query_width),
            key_back_grad.reshape(tok_rows, kv_width),
            value_back_grad.reshape(tok_rows, kv_width),
        ],
        axis=1,
    )
    normed_grad = map_rows(joint_grad, w_joint)
    grad_joint = weight_terms(normed, joint_grad)
    input_part, norm_gain_part = rms_backward(tokens32, norm_gain, normed_grad)
    input_grad = middle_grad + input_part
    norm_gain_grad, query_gain_grad, key_gain_grad, ffn_gain_grad = lax.psum(
        (norm_gain_part, query_gain_part, key_gain_part, ffn_gain_part), ("dp", "sq", "hd")
    )
    grad_joint, grad_out, grad_ffn, grad_down = (
        lax.psum(grad_joint.astype(jnp.bfloat16), "dp").astype(jnp.float32),
        lax.psum(grad_out.astype(jnp.bfloat16), "dp").astype(jnp.float32),
        lax.psum(grad_ffn.astype(jnp.bfloat16), "dp").astype(jnp.float32),
        lax.psum(grad_down.astype(jnp.bfloat16), "dp").astype(jnp.float32),
    )
    return (
        output[None],
        input_grad[None],
        norm_gain_grad,
        grad_joint[:, :query_width],
        grad_joint[:, query_width : query_width + kv_width],
        grad_joint[:, query_width + kv_width :],
        grad_out,
        query_gain_grad,
        key_gain_grad,
        ffn_gain_grad,
        grad_ffn[:, :ffn_width],
        grad_ffn[:, ffn_width:],
        grad_down,
    )


def solution(mesh):
    return jax.shard_map(
        on_device,
        mesh=mesh,
        in_specs=(
            P("dp", ("sq", "hd"), None),
            P(),
            P(("sq", "hd"), None),
            P(("sq", "hd"), None),
            P(("sq", "hd"), None),
            P(("sq", "hd"), None),
            P(),
            P(),
            P(),
            P(("sq", "hd"), None),
            P(("sq", "hd"), None),
            P(("sq", "hd"), None),
            P("dp", ("sq", "hd"), None),
        ),
        out_specs=(
            P("dp", ("sq", "hd"), None),
            P("dp", ("sq", "hd"), None),
            P(),
            P(("sq", "hd"), None),
            P(("sq", "hd"), None),
            P(("sq", "hd"), None),
            P(("sq", "hd"), None),
            P(),
            P(),
            P(),
            P(("sq", "hd"), None),
            P(("sq", "hd"), None),
            P(("sq", "hd"), None),
        ),
        check_vma=False,
    )
```

profile of v0, /device:TPU:0, one launch (start us, length us, event | category | flops | bytes accessed | tf_op | source)
XLA Modules:
  0.0 1465.6 jit_solution(12250674595962186203)
XLA Ops:
  10.6 51.9 %all-gather.7.cloned.1.call-done = bf16[1536,2560]{1,0:T(8,128)(2,1)} async-done(((bf16[96,2560]{1,0:T(8,128)(2,1)}), bf16[1536,2560]{1,0:T(8,128)(2,1)}) %all-gather.7.cloned.1.call-update) | async-done | bytes 7864336 | tf_op jit(solution)/shard_map/all_gather | solution.py:59
  62.5 4.7 convolution_convert_fusion.4
  67.2 4.0 all_to_all.108
  73.3 3.8 all_to_all.109
  82.3 4.0 all_to_all.110
  89.5 22.0 %all-gather.11.cloned.1.call-done = bf16[2048,256]{0,1:T(8,128)(2,1)} async-done(((bf16[256,256]{0,1:T(8,128)(2,1)}), bf16[2048,256]{0,1:T(8,128)(2,1)}) %all-gather.11.cloned.1.call-update) | async-done | bytes 1048592 | tf_op jit(solution)/shard_map/all_gather | solution.py:152
  114.0 38.7 %all-gather.9.cloned.1.call-done = bf16[2048,256]{0,1:T(8,128)(2,1)} async-done(((bf16[256,256]{0,1:T(8,128)(2,1)}), bf16[2048,256]{0,1:T(8,128)(2,1)}) %all-gather.9.cloned.1.call-update) | async-done | bytes 1048592 | tf_op jit(solution)/shard_map/all_gather | solution.py:153
  164.3 6.1 all_to_all.111
  174.5 20.1 %all-gather.13.cloned.1.call-done = bf16[1536,1536]{1,0:T(8,128)(2,1)} async-done(((bf16[96,1536]{1,0:T(8,128)(2,1)}), bf16[1536,1536]{1,0:T(8,128)(2,1)}) %all-gather.13.cloned.1.call-update) | async-done | bytes 4718608 | tf_op jit(solution)/shard_map/all_gather | solution.py:59
  197.9 211.3 %all-gather.15.cloned.1.call-done = bf16[1536,13824]{1,0:T(8,128)(2,1)} async-done(((bf16[96,13824]{1,0:T(8,128)(2,1)}), bf16[1536,13824]{1,0:T(8,128)(2,1)}) %all-gather.15.cloned.1.call-update) | async-done | bytes 42467344 | tf_op jit(solution)/shard_map/all_gather | solution.py:59
  409.2 19.5 %fusion.82 = f32[128,13824]{1,0:T(8,128)} fusion(bf16[1536,13824]{1,0:T(8,128)(2,1)} %all-gather.15.cloned.1.call-done, f32[128,1536]{1,0:T(8,128)S(1)} %get-tuple-element.361, f32[1536]{0:T(1024)S(1)} %copy-done.24, f32[128]{0:T(128)S(1)} %add_rsqrt_fusion.2), kind=kOutput, calls=%fused_computation.161 | convolution fusion | flops 5436407808 | bytes 50338304 | tf_op jit(solution)/shard_map/dot_general | solution.py:57
  428.7 95.5 %all-gather.17.cloned.1.call-done = bf16[6912,1536]{1,0:T(8,128)(2,1)} async-done(((bf16[432,1536]{1,0:T(8,128)(2,1)}), bf16[6912,1536]{1,0:T(8,128)(2,1)}) %all-gather.17.cloned.1.call-update) | async-done | bytes 21233680 | tf_op jit(solution)/shard_map/all_gather | solution.py:59
  524.2 14.3 multiply_convert_fusion.1
  538.4 19.7 %multiply_reduce_fusion = (f32[1536]{0:T(1024)}, f32[128]{0:T(128)S(1)}, f32[128,1536]{1,0:T(8,128)S(1)}) fusion(f32[128,1536]{1,0:T(8,128)S(1)} %get-tuple-element.361, f32[128]{0:T(128)S(1)} %add_rsqrt_fusion.2, f32[1536]{0:T(1024)S(1)} %copy-done.24, bf16[1536,13824]{1,0:T(8,128)(2,1)} %all-gather.15.cloned.1.call-done, ...), kind=kOutput, calls=%fused_computation.98 | convolution fusion | flops 5444073984 | bytes 47592448 | tf_op jit(solution)/shard_map/dot_general | solution.py:65
  558.4 4.3 convolution_convert_fusion.5
  562.7 5.2 all_to_all.112
  576.2 7.8 while.43
  584.7 4.8 convolution_convert_fusion.3
  601.0 4.0 all_to_all.113
  605.8 71.7 %reduce-scatter.9.cloned.1.call-done = bf16[256,256]{1,0:T(8,128)(2,1)} async-done(((bf16[2048,256]{1,0:T(8,128)(2,1)}), bf16[256,256]{1,0:T(8,128)(2,1)}) %reduce-scatter.9.cloned.1.call-update) | async-done | bytes 131088 | tf_op jit(solution)/shard_map/reduce_scatter | solution.py:280
  679.1 3.8 all_to_all.114
  683.2 34.6 %reduce-scatter.7.cloned.1.call-done = bf16[256,256]{0,1:T(8,128)(2,1)} async-done(((bf16[2048,256]{0,1:T(8,128)(2,1)}), bf16[256,256]{0,1:T(8,128)(2,1)}) %reduce-scatter.7.cloned.1.call-update) | async-done | bytes 131088 | tf_op jit(solution)/shard_map/reduce_scatter | solution.py:277
  724.2 5.6 convolution_convert_fusion.2
  730.8 11.8 convolution_convert_fusion.1
  743.2 19.3 %convolution_convert_fusion = bf16[1536,13824]{1,0:T(8,128)(2,1)} fusion(bf16[128,6912]{1,0:T(8,128)(2,1)} %get-tuple-element.334, bf16[128,6912]{1,0:T(8,128)(2,1)} %get-tuple-element.333, f32[128,1536]{1,0:T(8,128)S(1)} %get-tuple-element.361, f32[1536]{0:T(1024)S(1)} %copy-done.24, f32[128]{0:T(128)S(1)} %copy-done.42), kind=kOutput, calls=%fused_computation.59 | convolution fusion | flops 5464719360 | bytes 46799360 | tf_op jit(solution)/shard_map/dot_general | solution.py:75
  762.5 24.4 %reduce-scatter.13.cloned.1.call-done = bf16[96,1536]{1,0:T(8,128)(2,1)} async-done(((bf16[1536,1536]{1,0:T(8,128)(2,1)}), bf16[96,1536]{1,0:T(8,128)(2,1)}) %reduce-scatter.13.cloned.1.call-update) | async-done | bytes 294928 | tf_op jit(solution)/shard_map/reduce_scatter | solution.py:74
  786.9 74.7 %reduce-scatter.11.cloned.1.call-done = bf16[96,2560]{1,0:T(8,128)(2,1)} async-done(((bf16[1536,2560]{1,0:T(8,128)(2,1)}), bf16[96,2560]{1,0:T(8,128)(2,1)}) %reduce-scatter.11.cloned.1.call-update) | async-done | bytes 491536 | tf_op jit(solution)/shard_map/reduce_scatter | solution.py:74
  861.6 121.7 %reduce-scatter.17.cloned.1.call-done = bf16[432,1536]{1,0:T(8,128)(2,1)} async-done(((bf16[6912,1536]{1,0:T(8,128)(2,1)}), bf16[432,1536]{1,0:T(8,128)(2,1)}) %reduce-scatter.17.cloned.1.call-update) | async-done | bytes 1327120 | tf_op jit(solution)/shard_map/reduce_scatter | solution.py:74
  983.4 228.7 %reduce-scatter.15.cloned.1.call-done = bf16[96,13824]{1,0:T(8,128)(2,1)} async-done(((bf16[1536,13824]{1,0:T(8,128)(2,1)}), bf16[96,13824]{1,0:T(8,128)(2,1)}) %reduce-scatter.15.cloned.1.call-update) | async-done | bytes 2654224 | tf_op jit(solution)/shard_map/reduce_scatter | solution.py:74
  1227.9 10.8 fusion.44
  1239.6 6.2 fusion.57
  1245.8 201.9 %all-reduce = (f32[1536]{0:T(1024)}, f32[64]{0:T(128)}, f32[64]{0:T(128)}, f32[1536]{0:T(1024)}) all-reduce(f32[1536]{0:T(1024)S(1)} %get-tuple-element.255, f32[64]{0:T(128)S(1)} %fusion.46, f32[64]{0:T(128)S(1)} %fusion.63, f32[1536]{0:T(1024)S(1)} %copy-done.50), channel_id=1, replica_groups=mesh['dp'=8,'sq'=8,'hd'=2] {'dp','sq','hd'}, use_global_device_ids=true, to_apply=%region_20.21 | all-reduce | flops 3200 | bytes 25600 | tf_op jit(solution)/shard_map/psum | solution.py:308
  (279 shorter events, 107.7 us)
Async XLA Ops:
  7.2 55.3 %all-gather.7.cloned.1.call-start = ((), (), s32[]{:S(2)}) async-start(), calls=%async_computation.14 | async-start | bytes 8355840 | tf_op jit(solution)/shard_map/all_gather | solution.py:59
  9.1 102.4 %all-gather.11.cloned.1.call-start = ((), (), s32[]{:S(2)}) async-start(), calls=%async_computation.16 | async-start | bytes 1179648 | tf_op jit(solution)/shard_map/all_gather | solution.py:152
  10.4 56.8 %copy-start.47 = (f32[128]{0:T(128)}, f32[128]{0:T(128)S(1)}, u32[]{:S(2)}) copy-start(f32[128]{0:T(128)S(1)} %add_rsqrt_fusion.3) | copy-start | bytes 1540
  10.6 61.9 %copy-start.25 = (f32[256,32]{0,1:T(8,128)}, f32[256,32]{0,1:T(8,128)S(1)}, u32[]{:S(2)}) copy-start(f32[256,32]{0,1:T(8,128)S(1)} %get-tuple-element.358) | copy-start | bytes 98308
  10.6 61.9 %copy-start.29 = (f32[256,32]{0,1:T(8,128)}, f32[256,32]{0,1:T(8,128)S(1)}, u32[]{:S(2)}) copy-start(f32[256,32]{0,1:T(8,128)S(1)} %get-tuple-element.359) | copy-start | bytes 98308
  10.6 61.8 %copy-start.51 = (f32[64]{0:T(128)S(1)}, f32[64]{0:T(128)}, u32[]{:S(2)}) copy-start(f32[64]{0:T(128)} %param.26) | copy-start | bytes 772
  72.4 517.9 %copy-start.43 = (f32[256,4]{0,1:T(4,128)}, f32[256,4]{0,1:T(4,128)S(1)}, u32[]{:S(2)}) copy-start(f32[256,4]{0,1:T(4,128)S(1)} %add_rsqrt_fusion.1) | copy-start | bytes 12292
  73.2 79.5 %all-gather.9.cloned.1.call-start = ((), (), s32[]{:S(2)}) async-start(), calls=%async_computation.15 | async-start | bytes 1179648 | tf_op jit(solution)/shard_map/all_gather | solution.py:153
  77.9 116.6 %all-gather.13.cloned.1.call-start = ((), (), s32[]{:S(2)}) async-start(), calls=%async_computation.17 | async-start | bytes 5013504 | tf_op jit(solution)/shard_map/all_gather | solution.py:59
  78.5 330.7 %all-gather.15.cloned.1.call-start = ((), (), s32[]{:S(2)}) async-start(), calls=%async_computation.18 | async-start | bytes 45121536 | tf_op jit(solution)/shard_map/all_gather | solution.py:59
  81.6 442.6 %all-gather.17.cloned.1.call-start = ((), (), s32[]{:S(2)}) async-start(), calls=%async_computation.19 | async-start | bytes 22560768 | tf_op jit(solution)/shard_map/all_gather | solution.py:59
  82.2 595.3 %reduce-scatter.9.cloned.1.call-start = ((), (), s32[]{:S(2)}) async-start(), calls=%async_computation.21 | async-start | bytes 1179648 | tf_op jit(solution)/shard_map/reduce_scatter | solution.py:280
  194.6 214.7 %copy-start.24 = (f32[1536]{0:T(1024)S(1)}, f32[1536]{0:T(1024)}, u32[]{:S(2)}) copy-start(f32[1536]{0:T(1024)} %param.27) | copy-start | bytes 18436
  197.9 360.2 %copy-start.41 = (f32[128]{0:T(128)}, f32[128]{0:T(128)S(1)}, u32[]{:S(2)}) copy-start(f32[128]{0:T(128)S(1)} %add_rsqrt_fusion.2) | copy-start | bytes 1540
  583.9 133.9 %reduce-scatter.7.cloned.1.call-start = ((), (), s32[]{:S(2)}) async-start(), calls=%async_computation.20 | async-start | bytes 1179648 | tf_op jit(solution)/shard_map/reduce_scatter | solution.py:277
  584.7 202.2 %reduce-scatter.13.cloned.1.call-start = ((), (), s32[]{:S(2)}) async-start(), calls=%async_computation.23 | async-start | bytes 5013504 | tf_op jit(solution)/shard_map/reduce_scatter | solution.py:74
  589.5 272.1 %reduce-scatter.11.cloned.1.call-start = ((), (), s32[]{:S(2)}) async-start(), calls=%async_computation.22 | async-start | bytes 8355840 | tf_op jit(solution)/shard_map/reduce_scatter | solution.py:74
  601.0 117.7 %copy-start.28 = (f32[256,32]{0,1:T(8,128)S(1)}, f32[256,32]{0,1:T(8,128)}, u32[]{:S(2)}) copy-start(f32[256,32]{0,1:T(8,128)} %copy-done.25) | copy-start | bytes 98308
  601.0 117.7 %copy-start.32 = (f32[256,32]{0,1:T(8,128)S(1)}, f32[256,32]{0,1:T(8,128)}, u32[]{:S(2)}) copy-start(f32[256,32]{0,1:T(8,128)} %copy-done.29) | copy-start | bytes 98308
  605.1 113.7 %copy-start.44 = (f32[256,4]{0,1:T(4,128)S(1)}, f32[256,4]{0,1:T(4,128)}, u32[]{:S(2)}) copy-start(f32[256,4]{0,1:T(4,128)} %copy-done.43) | copy-start | bytes 12292
  605.1 113.7 %copy-start.52 = (f32[64]{0:T(128)S(1)}, f32[64]{0:T(128)}, u32[]{:S(2)}) copy-start(f32[64]{0:T(128)} %param.26) | copy-start | bytes 772
  605.5 113.7 %copy-start.22 = (f32[128,2,1,256]{3,0,1,2:T(8,128)S(1)}, f32[128,2,1,256]{3,0,1,2:T(8,128)}, u32[]{:S(2)}) copy-start(f32[128,2,1,256]{3,0,1,2:T(8,128)} %get-tuple-element.356) | copy-start | bytes 786436
  605.5 113.7 %copy-start.23 = (f32[256,1,256]{2,0,1:T(8,128)S(1)}, f32[256,1,256]{2,0,1:T(8,128)}, u32[]{:S(2)}) copy-start(f32[256,1,256]{2,0,1:T(8,128)} %copy.182) | copy-start | bytes 786436
  605.5 113.7 %copy-start.55 = (f32[256]{0:T(256)S(1)}, f32[256]{0:T(256)}, u32[]{:S(2)}) copy-start(f32[256]{0:T(256)} %mul.611) | copy-start | bytes 3076
  605.8 118.4 %copy-start.18 = (bf16[128,2,1,768]{0,3,1,2:T(8,128)(2,1)}, bf16[128,2,1,768]{0,3,1,2:T(8,128)(2,1)S(1)}, u32[]{:S(2)}) copy-start(bf16[128,2,1,768]{0,3,1,2:T(8,128)(2,1)S(1)} %copy.178) | copy-start | bytes 1179652
  683.1 41.1 %copy-start.40 = (f32[1536]{0:T(1024)S(1)}, f32[1536]{0:T(1024)}, u32[]{:S(2)}) copy-start(f32[1536]{0:T(1024)} %param.20) | copy-start | bytes 18436
  683.2 46.6 %copy-start.35 = (bf16[128,2,1,256]{0,3,1,2:T(8,128)(2,1)}, bf16[128,2,1,256]{0,3,1,2:T(8,128)(2,1)S(1)}, u32[]{:S(2)}) copy-start(bf16[128,2,1,256]{0,3,1,2:T(8,128)(2,1)S(1)} %copy.187) | copy-start | bytes 393220
  729.8 253.6 %reduce-scatter.17.cloned.1.call-start = ((), (), s32[]{:S(2)}) async-start(), calls=%async_computation.25 | async-start | bytes 22560768 | tf_op jit(solution)/shard_map/reduce_scatter | solution.py:74
  742.6 469.4 %reduce-scatter.15.cloned.1.call-start = ((), (), s32[]{:S(2)}) async-start(), calls=%async_computation.24 | async-start | bytes 45121536 | tf_op jit(solution)/shard_map/reduce_scatter | solution.py:74
  762.5 449.6 %copy-start.6 = (f32[2,128,1,768]{3,1,0,2:T(8,128)S(1)}, f32[2,128,1,768]{3,1,0,2:T(8,128)}, u32[]{:S(2)}) copy-start(f32[2,128,1,768]{3,1,0,2:T(8,128)} %copy-done.5) | copy-start | bytes 2359300
  762.5 686.3 %all-reduce.4.cloned.1.call-start = ((), (), s32[]{:S(2)}) async-start(), calls=%async_computation.26 | async-start | bytes 9535488 | tf_op jit(solution)/shard_map/psum | solution.py:312
  1239.6 208.1 %copy-start.2 = (f32[128,1536]{1,0:T(8,128)S(1)}, f32[128,1536]{1,0:T(8,128)}, u32[]{:S(2)}) copy-start(f32[128,1536]{1,0:T(8,128)} %copy-done.1) | copy-start | bytes 2359300
  (37 other events, 233.1 us)
Sparse Core Ops, SparseCore 0:
  10.3 52.1 all-gather.6
  73.4 38.1 all-gather.10
  113.7 38.9 all-gather.8
  154.3 40.2 all-gather.12
  196.7 212.4 all-gather.14
  410.8 113.3 all-gather.16
  584.1 93.3 reduce-scatter.8
  679.8 37.9 reduce-scatter.6
  720.2 66.6 reduce-scatter.12
  789.2 72.4 reduce-scatter.10
  864.1 119.2 reduce-scatter.16
  985.8 226.1 reduce-scatter.14
  1214.8 209.0 all-reduce.3
where the time goes:
time: 1470 us
  waiting for transfers between devices  997 us (68%)
  blocking collectives  237 us (16%)
  matrix products  131 us (9%)
  local copies, waits for them, and re-layouts  52.7 us (4%)
  other arithmetic  31.7 us (2%)
  between operations  15.1 us (1%)
    reduce_scatter x4, waiting for transfers between devices, weight_terms(): lax.psum_scatter(lax.dot_general(inputs, grads, (((0,), (0,)), ((), ())),...  449 us
    all_gather x4, waiting for transfers between devices, fold_rows(): lax.all_gather(weight_shard, ('sq', 'hd'), axis=0, tiled=True)  379 us
    psum x1, blocking collectives, on_device(): lax.psum((norm_gain_part, query_gain_part, key_gain_part, ffn_gain_part),...  202 us
    reduce_scatter x1, waiting for transfers between devices, on_device(): lax.psum_scatter(value_term.astype(jnp.bfloat16), 'sq', scatter_dimension...  71.7 us
    dot_general x4, matrix products, map_rows(): lax.dot_general(grads, lax.all_gather(weight_shard, ('sq', 'hd'), axis=0,...  44.4 us
    dot_general x4, matrix products, weight_terms(): lax.dot_general(inputs, grads, (((0,), (0,)), ((), ())), preferred_elemen...  41.4 us
    all_gather x1, waiting for transfers between devices, on_device(): lax.all_gather(value_flat, 'sq', axis=0, tiled=True)  38.7 us
    dot_general x4, matrix products, fold_rows(): jnp.dot(inputs, lax.all_gather(weight_shard, ('sq', 'hd'), axis=0, tiled=...  38.3 us
  transfers between devices with their start and end apart: 13, of which 12 were waited for; matrix products, arithmetic and copies ran while one was open for 10% of the time, Pallas kernels for 0%

commit v1 on v0

v1 whole, which is shorter than its diff:
```python
import jax
import jax.numpy as jnp
from jax import lax
from jax.experimental import pallas as pl
from jax.experimental.pallas import tpu as pltpu
from jax.sharding import PartitionSpec as P

HQ = 24
HK = 8
HS = 64
GROUP = HQ // HK

EPSILON = 1e-05
ROPE_BASE = 1000000.0
SCORE_SCALE = 0.125

RING = 4
OFFSETS = ((2, 1), (2, 0), (1, 1), (3, 1), (1, 0), (3, 0), (0, 1))
BLOCK = 128
ROWS = GROUP * BLOCK


def rms_forward(values, gain):
    factor = lax.rsqrt(jnp.mean(values * values, axis=-1, keepdims=True) + EPSILON)
    return values * factor * gain


def rms_backward(values, gain, grad_out):
    factor = lax.rsqrt(jnp.mean(values * values, axis=-1, keepdims=True) + EPSILON)
    normal = values * factor
    scaled = grad_out * gain
    grad_in = factor * (scaled - normal * jnp.mean(scaled * normal, axis=-1, keepdims=True))
    grad_gain = jnp.sum(grad_out * normal, axis=0)
    return (grad_in, grad_gain)


def dot(left, right, contract):
    return lax.dot_general(
        left, right, (((contract[0],), (contract[1],)), ((), ())), preferred_element_type=jnp.float32
    )


def neighbour(index, dy, dz):
    return (index // RING + dz) % 2 * RING + (index % RING + dy) % RING


def shift(array, dy, dz):
    return lax.ppermute(array, "sq", [(i, neighbour(i, dy, dz)) for i in range(2 * RING)])


def place(buffer, array, index):
    return lax.dynamic_update_index_in_dim(buffer, array, index, 0)


def gather_blocks(array):
    me = lax.axis_index("sq")
    arrived = [shift(array, dy, dz) for dy, dz in OFFSETS]
    whole = place(jnp.zeros((2 * RING, *array.shape), array.dtype), array, me)
    for (dy, dz), block in zip(OFFSETS, arrived):
        whole = place(whole, block, neighbour(me, -dy, dz))
    return whole


def exchange_blocks(blocks):
    me = lax.axis_index("sq")
    whole = jnp.zeros_like(blocks)
    whole = place(whole, lax.dynamic_index_in_dim(blocks, me, 0, keepdims=False), me)
    arrived = [
        shift(lax.dynamic_index_in_dim(blocks, neighbour(me, dy, dz), 0, keepdims=False), dy, dz)
        for dy, dz in OFFSETS
    ]
    for (dy, dz), block in zip(OFFSETS, arrived):
        whole = place(whole, block, neighbour(me, -dy, dz))
    return whole


def scatter_sum(parts):
    me = lax.axis_index("sq")
    arrived = [
        shift(lax.dynamic_index_in_dim(parts, neighbour(me, dy, dz), 0, keepdims=False), dy, dz)
        for dy, dz in OFFSETS
    ]
    total = lax.dynamic_index_in_dim(parts, me, 0, keepdims=False).astype(jnp.float32)
    for block in arrived:
        total = total + block.astype(jnp.float32)
    return total


def shift_x(array, dx):
    return lax.ppermute(array, "dp", [(i, (i + 2 * dx) % (2 * RING)) for i in range(2 * RING)])


def other_z(array):
    return lax.ppermute(array, "dp", [(i, i ^ 1) for i in range(2 * RING)])


def sequence_scatter(pieces):
    me = lax.axis_index("dp")
    x, z = me // 2, me % 2
    pieces = pieces.reshape(RING, 2, *pieces.shape[1:])
    take = lambda i: lax.dynamic_index_in_dim(pieces, i % RING, 0, keepdims=False)
    arrived = [shift_x(take(x + dx), dx) for dx in (2, 1, 3)]
    total = take(x).astype(jnp.float32)
    for block in arrived:
        total = total + block.astype(jnp.float32)
    total = total.astype(jnp.bfloat16)
    mine = lax.dynamic_index_in_dim(total, z, 0, keepdims=False)
    came = other_z(lax.dynamic_index_in_dim(total, 1 - z, 0, keepdims=False))
    return (mine.astype(jnp.float32) + came.astype(jnp.float32)).astype(jnp.bfloat16)


def sequence_gather(piece):
    me = lax.axis_index("dp")
    x, z = me // 2, me % 2
    came = other_z(piece)
    pair = jnp.stack([jnp.where(z == 0, piece, came), jnp.where(z == 0, came, piece)])
    arrived = [shift_x(pair, dx) for dx in (2, 1, 3)]
    whole = place(jnp.zeros((RING, *pair.shape), pair.dtype), pair, x)
    for dx, block in zip((2, 1, 3), arrived):
        whole = place(whole, block, (x - dx) % RING)
    return whole.reshape(2 * RING, *piece.shape)


def sum_everywhere(terms):
    for axis, count in (("hd", 2), ("sq", 8), ("dp", 8)):
        step = 1
        while step < count:
            terms = terms + lax.ppermute(terms, axis, [(i, i ^ step) for i in range(count)])
            step *= 2
    return terms


def after(array, *earlier):
    return lax.optimization_barrier((array, *earlier))[0]


def partner(array):
    return lax.ppermute(array, "hd", [(0, 1), (1, 0)])


def both_cores(array, axis):
    other = partner(array)
    first = lax.axis_index("hd") == 0
    return jnp.stack([jnp.where(first, array, other), jnp.where(first, other, array)], axis=axis)


def sum_cores(terms, axis):
    hd = lax.axis_index("hd")
    mine = lax.dynamic_index_in_dim(terms, hd, axis, keepdims=False)
    other = lax.dynamic_index_in_dim(terms, 1 - hd, axis, keepdims=False)
    return (mine.astype(jnp.float32) + partner(other).astype(jnp.float32)).astype(jnp.bfloat16)


def turn(values, cosine, sine):
    first, second = values[: HS // 2], values[HS // 2 :]
    return jnp.concatenate([first * cosine - second * sine, second * cosine + first * sine], axis=0)


def unturn(grads, cosine, sine):
    first, second = grads[: HS // 2], grads[HS // 2 :]
    return jnp.concatenate([first * cosine + second * sine, second * cosine - first * sine], axis=0)


def head_norm(values, gain):
    return values * lax.rsqrt(jnp.mean(values * values, axis=0, keepdims=True) + EPSILON) * gain


def head_norm_back(values, gain, grad_out):
    factor = lax.rsqrt(jnp.mean(values * values, axis=0, keepdims=True) + EPSILON)
    normal = values * factor
    scaled = grad_out * gain
    grad_in = factor * (scaled - normal * jnp.mean(scaled * normal, axis=0, keepdims=True))
    return grad_in, grad_out * normal


def allowed_keys(hd):
    key = lax.broadcasted_iota(jnp.int32, (2 * BLOCK, ROWS), 0)
    query = lax.broadcasted_iota(jnp.int32, (2 * BLOCK, ROWS), 1) % BLOCK
    bound = jnp.where(key < BLOCK, key, jnp.where(hd == 1, -1, BLOCK))
    return bound <= query


def attend_kernel(
    hd_ref, own_ref, other_ref, cos_ref, sin_ref, cos2_ref, sin2_ref, qgain_ref, kgain_ref,
    blocks_ref, att_ref, out_ref, lse_ref, q_ref, kt_ref, k_ref, v_ref, vt_ref,
):
    count = own_ref.shape[1] // BLOCK
    qgain, kgain = qgain_ref[...], kgain_ref[...]
    vt_ref[HS:, :] = jnp.ones((HS, vt_ref.shape[1]), jnp.bfloat16)
    for c in range(count):
        cols = slice(c * BLOCK, (c + 1) * BLOCK)
        sides = (
            (own_ref[GROUP * HS :, cols], cos_ref[:, cols], sin_ref[:, cols]),
            (other_ref[:, cols], cos2_ref[:, cols], sin2_ref[:, cols]),
        )
        for side, (pair, cosine, sine) in enumerate(sides):
            pair = pair.astype(jnp.float32)
            place_at = slice((2 * c + side) * BLOCK, (2 * c + side + 1) * BLOCK)
            key = turn(head_norm(pair[:HS], kgain), cosine, sine)
            kt_ref[:, place_at] = key.astype(jnp.bfloat16)
            k_ref[place_at, :] = key.T.astype(jnp.bfloat16)
            vt_ref[:HS, place_at] = pair[HS:].astype(jnp.bfloat16)
            v_ref[place_at, :] = pair[HS:].T.astype(jnp.bfloat16)
        for head in range(GROUP):
            query = own_ref[head * HS : (head + 1) * HS, cols].astype(jnp.float32)
            query = turn(head_norm(query, qgain), cos_ref[:, cols], sin_ref[:, cols])
            q_ref[c, :, head * BLOCK : (head + 1) * BLOCK] = (query * SCORE_SCALE).astype(jnp.bfloat16)
    allowed = allowed_keys(hd_ref[0])
    for i in range(count):
        query = q_ref[i]
        total = jnp.zeros((2 * HS, ROWS), jnp.float32)
        for c in range(i + 1):
            keys = slice(2 * c * BLOCK, 2 * (c + 1) * BLOCK)
            weights = jnp.exp(dot(k_ref[keys, :], query, (1, 0)))
            if c == i:
                weights = jnp.where(allowed, weights, 0.0)
            total = total + dot(vt_ref[:, keys], weights.astype(jnp.bfloat16), (1, 0))
        norm = total[HS : HS + 1]
        result = total[:HS] / norm
        lse_ref[i : i + 1, :] = jnp.log(norm)
        out_ref[i] = result
        for head in range(GROUP):
            part = result[:, head * BLOCK : (head + 1) * BLOCK].astype(jnp.bfloat16)
            att_ref[head * HS : (head + 1) * HS, i * BLOCK : (i + 1) * BLOCK] = part
            blocks_ref[i, head * HS : (head + 1) * HS, :] = part


def attend_back_kernel(
    hd_ref, own_ref, grad_ref, cos_ref, sin_ref, qgain_ref, out_ref, lse_ref, q_ref, kt_ref, k_ref, v_ref,
    qgrad_ref, kv_own_ref, kv_other_ref, gain_ref, dk_ref, dv_ref,
):
    count = own_ref.shape[1] // BLOCK
    qgain = qgain_ref[...]
    allowed = allowed_keys(hd_ref[0])
    gain_total = jnp.zeros((HS, BLOCK), jnp.float32)
    for i in range(count):
        cols = slice(i * BLOCK, (i + 1) * BLOCK)
        query = q_ref[i]
        grad = jnp.concatenate([grad_ref[i, head * HS : (head + 1) * HS, :] for head in range(GROUP)], axis=1)
        delta = jnp.sum(grad.astype(jnp.float32) * out_ref[i], axis=0, keepdims=True)
        lse = lse_ref[i : i + 1, :]
        query_grad = jnp.zeros((HS, ROWS), jnp.float32)
        for c in range(i + 1):
            keys = slice(2 * c * BLOCK, 2 * (c + 1) * BLOCK)
            weights = jnp.exp(dot(k_ref[keys, :], query, (1, 0)) - lse)
            if c == i:
                weights = jnp.where(allowed, weights, 0.0)
            prob_grad = dot(v_ref[keys, :], grad, (1, 0))
            score_grad = (weights * (prob_grad - delta)).astype(jnp.bfloat16)
            value_part = dot(weights.astype(jnp.bfloat16), grad, (1, 1))
            key_part = dot(score_grad, query, (1, 1))
            if c == i:
                dv_ref[keys, :] = value_part
                dk_ref[keys, :] = key_part
            else:
                dv_ref[keys, :] += value_part
                dk_ref[keys, :] += key_part
            query_grad = query_grad + dot(kt_ref[:, keys], score_grad, (1, 0))
        for head in range(GROUP):
            turned = query_grad[:, head * BLOCK : (head + 1) * BLOCK] * SCORE_SCALE
            back = unturn(turned, cos_ref[:, cols], sin_ref[:, cols])
            rows = slice(head * HS, (head + 1) * HS)
            lin, gain_part = head_norm_back(own_ref[rows, cols].astype(jnp.float32), qgain, back)
            qgrad_ref[rows, cols] = lin.astype(jnp.bfloat16)
            gain_total = gain_total + gain_part
    gain_ref[...] = gain_total
    for c in range(count):
        cols = slice(c * BLOCK, (c + 1) * BLOCK)
        for source, rows in ((dk_ref, slice(0, HS)), (dv_ref, slice(HS, 2 * HS))):
            kv_own_ref[rows, cols] = source[2 * c * BLOCK : (2 * c + 1) * BLOCK, :].T
            kv_other_ref[rows, cols] = source[(2 * c + 1) * BLOCK : (2 * c + 2) * BLOCK, :].T.astype(jnp.bfloat16)


def key_back_kernel(
    own_ref, kv_own_ref, kv_came_ref, cos_ref, sin_ref, kgain_ref, qgrad_ref, grad_ref, blocks_ref, gain_ref
):
    total = kv_own_ref[...] + kv_came_ref[...].astype(jnp.float32)
    back = unturn(total[:HS], cos_ref[...], sin_ref[...])
    key = own_ref[GROUP * HS : (GROUP + 1) * HS, :].astype(jnp.float32)
    lin, gain_part = head_norm_back(key, kgain_ref[...], back)
    grad_ref[: GROUP * HS, :] = qgrad_ref[...]
    grad_ref[GROUP * HS : (GROUP + 1) * HS, :] = lin.astype(jnp.bfloat16)
    grad_ref[(GROUP + 1) * HS :, :] = total[HS:].astype(jnp.bfloat16)
    for i in range(own_ref.shape[1] // BLOCK):
        blocks_ref[i] = grad_ref[:, i * BLOCK : (i + 1) * BLOCK]
    gain_ref[...] = jnp.sum(gain_part, axis=1, keepdims=True)


def call(kernel, outs, scratch, args, flops):
    smem = pl.BlockSpec(memory_space=pltpu.SMEM)
    vmem = pl.BlockSpec(memory_space=pltpu.VMEM)
    return pl.pallas_call(
        kernel,
        out_shape=[jax.ShapeDtypeStruct(shape, dtype) for shape, dtype in outs],
        in_specs=[smem if a.dtype == jnp.int32 else vmem for a in args],
        out_specs=[vmem for _ in outs],
        scratch_shapes=scratch,
        compiler_params=pltpu.CompilerParams(vmem_limit_bytes=40 * 1024 * 1024),
        cost_estimate=pl.CostEstimate(flops=flops, bytes_accessed=8 * 1024 * 1024, transcendentals=0),
    )(*args)


def rope_tables(positions):
    half = HS // 2
    freqs = ROPE_BASE ** (-jnp.arange(half, dtype=jnp.float32) * 2.0 / HS)
    angles = freqs[:, None] * positions[None, :].astype(jnp.float32)
    return jnp.cos(angles), jnp.sin(angles)


def on_device(
    inputs,
    norm_gain,
    w_query,
    w_key,
    w_value,
    w_out,
    query_gain,
    key_gain,
    ffn_gain,
    w_gate,
    w_up,
    w_down,
    cotangent,
):
    f32, bf16 = jnp.float32, jnp.bfloat16
    tokens = inputs[0]
    out_grad = cotangent[0]
    rows, width = tokens.shape
    chips = 2 * RING
    held = w_gate.shape[0]
    ffn = w_gate.shape[1] // chips
    seen = chips * rows
    hd = lax.axis_index("hd")
    tokens32 = tokens.astype(f32)

    by_chip = lambda w: w.reshape(held, chips, -1).transpose(1, 0, 2)
    joint_blocks = jnp.concatenate([by_chip(w_query), by_chip(w_key), by_chip(w_value)], axis=2)

    normed = rms_forward(tokens32, norm_gain).astype(bf16)
    normed_all = gather_blocks(normed).reshape(seen, width)
    w_joint_own = both_cores(exchange_blocks(joint_blocks), 1).reshape(width, -1)

    joint = dot(w_joint_own, normed_all, (0, 1)).astype(bf16)
    other_kv = partner(joint[GROUP * HS :])
    base = jnp.arange(seen, dtype=jnp.int32)
    base = base // BLOCK * (2 * BLOCK) + base % BLOCK
    cosine, sine = rope_tables(base + hd * BLOCK)
    cosine2, sine2 = rope_tables(base + (1 - hd) * BLOCK)
    hd_flag = jnp.reshape(hd, (1,)).astype(jnp.int32)
    qgain, kgain = query_gain[:, None], key_gain[:, None]
    heads_width = GROUP * HS
    att_blocks, att, att32, lse, q_rot, kt_rot, k_rot, v_nat = call(
        attend_kernel,
        [
            ((chips, heads_width, BLOCK), bf16),
            ((heads_width, seen), bf16),
            ((chips, HS, ROWS), f32),
            ((chips, ROWS), f32),
            ((chips, HS, ROWS), bf16),
            ((HS, 2 * seen), bf16),
            ((2 * seen, HS), bf16),
            ((2 * seen, HS), bf16),
        ],
        [pltpu.VMEM((2 * HS, 2 * seen), bf16)],
        (hd_flag, joint, other_kv, cosine, sine, cosine2, sine2, qgain, kgain),
        20_000_000_000,
    )
    attended = lax.all_to_all(att_blocks, "sq", split_axis=0, concat_axis=0, tiled=True)
    attended = attended.reshape(chips * heads_width, rows)

    w_out_all = lax.all_gather(after(w_out, normed_all), ("sq", "hd"), axis=0, tiled=True)
    grad_all = lax.all_gather(after(out_grad, w_out_all), "sq", axis=0, tiled=True)
    w_joint_rows = jnp.concatenate([w_query, w_key, w_value], axis=1)
    w_joint_all = lax.all_gather(after(w_joint_rows, grad_all), ("sq", "hd"), axis=0, tiled=True)

    gate_up_blocks = jnp.stack([by_chip(w_gate), by_chip(w_up)], axis=1)
    w_gate_up = both_cores(exchange_blocks(after(gate_up_blocks, normed_all)), 2)
    w_gate_own = w_gate_up[:, 0].reshape(width, ffn)
    w_up_own = w_gate_up[:, 1].reshape(width, ffn)
    w_down_own = both_cores(w_down, 0).reshape(ffn, width)

    middle = tokens32 + dot(attended, w_out_all, (0, 0))
    ffn_in = rms_forward(middle, ffn_gain).astype(bf16)
    ffn_all = gather_blocks(ffn_in).reshape(seen, width)
    hidden_grad = lax.optimization_barrier(dot(grad_all, w_down_own, (1, 1)))

    gate = dot(ffn_all, w_gate_own, (1, 0))
    up_val = dot(ffn_all, w_up_own, (1, 0))
    sigmoid = jax.nn.sigmoid(gate)
    hidden = (gate * sigmoid * up_val).astype(bf16)
    gate_grad = (hidden_grad * up_val * sigmoid * (1.0 + gate * (1.0 - sigmoid))).astype(bf16)
    up_grad = (hidden_grad * gate * sigmoid).astype(bf16)
    ffn_part = (dot(gate_grad, w_gate_own, (1, 1)) + dot(up_grad, w_up_own, (1, 1))).astype(bf16)
    ffn_in_grad = scatter_sum(ffn_part.reshape(chips, rows, width))

    out_part = dot(hidden, w_down_own, (1, 0)).astype(bf16)
    out_sum = lax.psum_scatter(out_part, "sq", scatter_dimension=0, tiled=True)
    output = (middle + out_sum.astype(f32)).astype(bf16)

    down_terms = dot(hidden, grad_all, (0, 0)).astype(bf16)
    down_sum = sum_cores(down_terms.reshape(2, ffn // 2, width), 0)
    gate_terms = dot(ffn_all, gate_grad, (0, 0)).astype(bf16).reshape(chips, 2, held, ffn)
    up_terms = dot(ffn_all, up_grad, (0, 0)).astype(bf16).reshape(chips, 2, held, ffn)
    gate_up_sum = sum_cores(jnp.stack([gate_terms, up_terms]), 2)
    down_half, quarter, few = ffn // 4, width // 4, held // 4
    down_pieces = down_sum.reshape(2, down_half, 4, quarter).transpose(0, 2, 1, 3)
    w_down_grad = sequence_gather(sequence_scatter(down_pieces.reshape(8, down_half, quarter)))
    w_down_grad = w_down_grad.reshape(2, 4, down_half, quarter).transpose(0, 2, 1, 3)
    w_down_grad = w_down_grad.reshape(ffn // 2, width).astype(f32)
    gate_up_pieces = gate_up_sum.reshape(2, chips, 4, few, ffn).transpose(0, 2, 1, 3, 4)
    gate_up_mine = sequence_scatter(gate_up_pieces.reshape(8, chips, few, ffn))
    gate_up_grad = sequence_gather(exchange_blocks(gate_up_mine))
    gate_up_grad = gate_up_grad.reshape(2, 4, chips, few, ffn).transpose(0, 1, 3, 2, 4)
    gate_up_grad = gate_up_grad.reshape(2, held, chips * ffn).astype(f32)

    middle_part, ffn_gain_part = rms_backward(middle, ffn_gain, ffn_in_grad)
    middle_grad = out_grad.astype(f32) + middle_part
    branch_grad = middle_grad.astype(bf16)
    att_grad = dot(w_out_all, branch_grad, (1, 1)).astype(bf16).reshape(chips, heads_width, rows)
    att_grad = lax.all_to_all(att_grad, "sq", split_axis=0, concat_axis=0, tiled=True)

    q_grad, kv_own, kv_other, qgain_part = call(
        attend_back_kernel,
        [
            ((heads_width, seen), bf16),
            ((2 * HS, seen), f32),
            ((2 * HS, seen), bf16),
            ((HS, BLOCK), f32),
        ],
        [pltpu.VMEM((2 * seen, HS), f32), pltpu.VMEM((2 * seen, HS), f32)],
        (hd_flag, joint, att_grad, cosine, sine, qgain, att32, lse, q_rot, kt_rot, k_rot, v_nat),
        40_000_000_000,
    )
    joint_grad, joint_grad_blocks, kgain_part = call(
        key_back_kernel,
        [(joint.shape, bf16), ((chips, joint.shape[0], BLOCK), bf16), ((HS, 1), f32)],
        [],
        (joint, kv_own, partner(kv_other), cosine, sine, kgain, q_grad),
        1_000_000_000,
    )
    came = lax.all_to_all(joint_grad_blocks, "sq", split_axis=0, concat_axis=0, tiled=True)
    key_at, value_at = heads_width, heads_width + HS
    came = jnp.concatenate(
        [
            came[:, :key_at].reshape(-1, rows),
            came[:, key_at:value_at].reshape(-1, rows),
            came[:, value_at:].reshape(-1, rows),
        ]
    )
    normed_grad = dot(came, w_joint_all, (0, 1))
    input_part, norm_gain_part = rms_backward(tokens32, norm_gain, normed_grad)
    input_grad = middle_grad + input_part

    branch_all = lax.all_gather(branch_grad, "sq", axis=0, tiled=True)
    out_terms = dot(att, branch_all, (1, 0)).astype(bf16)
    out_w_sum = sum_cores(out_terms.reshape(2, held, width), 0)
    out_pieces = out_w_sum.reshape(2, held // 2, 4, quarter).transpose(0, 2, 1, 3)
    w_out_grad = sequence_gather(sequence_scatter(out_pieces.reshape(8, held // 2, quarter)))
    w_out_grad = w_out_grad.reshape(2, 4, held // 2, quarter).transpose(0, 2, 1, 3)
    w_out_grad = w_out_grad.reshape(held, width).astype(f32)
    joint_terms = dot(normed_all, joint_grad, (0, 1)).astype(bf16).reshape(chips, 2, held, -1)
    joint_sum = sum_cores(joint_terms, 1)
    joint_pieces = joint_sum.reshape(chips, 8, held // 8, -1).transpose(1, 0, 2, 3)
    joint_mine = exchange_blocks(sequence_scatter(joint_pieces))
    w_joint_grad = sequence_gather(joint_mine)
    w_joint_grad = w_joint_grad.transpose(0, 2, 1, 3).reshape(held, chips, -1).astype(f32)

    gains = jnp.concatenate([norm_gain_part, ffn_gain_part, jnp.sum(qgain_part, axis=1), kgain_part[:, 0]])
    gains = sum_everywhere(gains.reshape(-1, BLOCK)).reshape(-1)
    return (
        output[None],
        input_grad[None],
        gains[:width],
        w_joint_grad[:, :, :key_at].reshape(held, -1),
        w_joint_grad[:, :, key_at:value_at].reshape(held, -1),
        w_joint_grad[:, :, value_at:].reshape(held, -1),
        w_out_grad,
        gains[2 * width : 2 * width + HS],
        gains[2 * width + HS :],
        gains[width : 2 * width],
        gate_up_grad[0],
        gate_up_grad[1],
        w_down_grad,
    )


def solution(mesh):
    return jax.shard_map(
        on_device,
        mesh=mesh,
        in_specs=(
            P("dp", ("sq", "hd"), None),
            P(),
            P(("sq", "hd"), None),
            P(("sq", "hd"), None),
            P(("sq", "hd"), None),
            P(("sq", "hd"), None),
            P(),
            P(),
            P(),
            P(("sq", "hd"), None),
            P(("sq", "hd"), None),
            P(("sq", "hd"), None),
            P("dp", ("sq", "hd"), None),
        ),
        out_specs=(
            P("dp", ("sq", "hd"), None),
            P("dp", ("sq", "hd"), None),
            P(),
            P(("sq", "hd"), None),
            P(("sq", "hd"), None),
            P(("sq", "hd"), None),
            P(("sq", "hd"), None),
            P(),
            P(),
            P(),
            P(("sq", "hd"), None),
            P(("sq", "hd"), None),
            P(("sq", "hd"), None),
        ),
        check_vma=False,
    )
```

time: 1470 us -> 691 us (0.47)
  waiting for transfers between devices: 997 us -> 239 us
  blocking collectives: 237 us -> 0 us
  starting transfers between devices: 0.7 us -> 163 us
  local copies, waits for them, and re-layouts: 52.7 us -> 132 us
  matrix products: 131 us -> 70.5 us
  Pallas kernels: 0 us -> 19.8 us
    reduce_scatter x6 -> x1, waiting for transfers between devices: 556 us -> 0.01 us  [on_device(): out_sum = lax.psum_scatter(out_part, 'sq', scatter_dimension=0, tiled=True)]
    all_gather x6 -> x4, waiting for transfers between devices: 439 us -> 0.03 us  [the longest x1 0.02 us: on_device(): branch_all = lax.all_gather(branch_grad, 'sq', axis=0, tiled=True)]
    ppermute x0 -> x97, waiting for transfers between devices: none -> 230 us  [the longest x49 142 us: shift(): lax.ppermute(array, 'sq', [(i, neighbour(i, dy, dz)) for i in range(2 * R...]
    psum x1 -> x0, blocking collectives: 202 us -> none  [on_device(): lax.psum((norm_gain_part, query_gain_part, key_gain_part, ffn_gain_part),...]
    ppermute x0 -> x97, starting transfers between devices: none -> 148 us  [the longest x49 85.7 us: shift(): lax.ppermute(array, 'sq', [(i, neighbour(i, dy, dz)) for i in range(2 * R...]
    dot_general x21 -> x15, matrix products: 131 us -> 70.5 us  [dot(): lax.dot_general(left, right, (((contract[0],), (contract[1],)), ((), ()))...]
    all_to_all x8 -> x0, blocking collectives: 34.9 us -> none  [the longest x1 6.12 us: on_device(): lax.all_to_all(attn_heads, 'hd', split_axis=0, concat_axis=1, tiled=True)]
    dynamic_update_slice x3 -> x57, local copies, waits for them, and re-layouts: 2.38 us -> 30.1 us  [place(): return lax.dynamic_update_index_in_dim(buffer, array, index, 0)]
  transfers between devices with their start and end apart: 13 -> 105, of which waited for: 12 -> 49; matrix products, arithmetic and copies ran while one was open for 10% -> 30% of each run, Pallas kernels for 0% -> 3%
where the time goes in v1:
time: 691 us; the launch traced here: 682 us
  waiting for transfers between devices  239 us (35%)
  starting transfers between devices  163 us (24%)
  local copies, waits for them, and re-layouts  132 us (19%)
  matrix products  70.5 us (10%)
  other arithmetic  41.5 us (6%)
  Pallas kernels  19.8 us (3%)
  between operations  15.7 us (2%)
    ppermute x49, waiting for transfers between devices, shift(): lax.ppermute(array, 'sq', [(i, neighbour(i, dy, dz)) for i in range(2 * R...  142 us
    ppermute x49, starting transfers between devices, shift(): lax.ppermute(array, 'sq', [(i, neighbour(i, dy, dz)) for i in range(2 * R...  85.7 us
    dot_general x15, matrix products, dot(): lax.dot_general(left, right, (((contract[0],), (contract[1],)), ((), ()))...  70.5 us
    ppermute x24, waiting for transfers between devices, shift_x(): lax.ppermute(array, 'dp', [(i, (i + 2 * dx) % (2 * RING)) for i in range(...  45.4 us
    ppermute x24, starting transfers between devices, shift_x(): lax.ppermute(array, 'dp', [(i, (i + 2 * dx) % (2 * RING)) for i in range(...  41.8 us
    dynamic_update_slice x57, local copies, waits for them, and re-layouts, place(): return lax.dynamic_update_index_in_dim(buffer, array, index, 0)  30.1 us
    ppermute x8, waiting for transfers between devices, other_z(): return lax.ppermute(array, 'dp', [(i, i ^ 1) for i in range(2 * RING)])  23 us
    unnamed x151, local copies, waits for them, and re-layouts  21 us
  transfers between devices with their start and end apart: 105, of which 49 were waited for; matrix products, arithmetic and copies ran while one was open for 30% of the time, Pallas kernels for 3%

profile of v1, /device:TPU:0, one launch (start us, length us, event | category | flops | bytes accessed | tf_op | source)
XLA Modules:
  0.0 682.4 jit_solution(5831773213702216372)
XLA Ops:
  9.6 4.7 collective-permute-start.8
  28.1 5.0 collective-permute-done.9
  34.1 11.9 %collective-permute-done.10 = bf16[128,1536]{1,0:T(8,128)(2,1)S(1)} collective-permute-done((bf16[128,1536]{1,0:T(8,128)(2,1)S(1)}, bf16[128,1536]{1,0:T(8,128)(2,1)S(1)}, u32[]{:S(2)}, u32[]{:S(2)}) %collective-permute-start.10) | collective-permute-done | bytes 393248 | tf_op jit(solution)/shard_map/ppermute | solution.py:48
  94.7 15.4 %constant_dynamic-slice_fusion.8 = (bf16[1,2,96,864]{3,0,2,1:T(2,128)(2,1)S(1)}, bf16[1,2,96,864]{3,0,2,1:T(2,128)(2,1)S(1)}, bf16[1,2,96,864]{3,0,2,1:T(2,128)(...) fusion(bf16[8,2,96,864]{3,0,2,1:T(8,128)(2,1)} %pad_maximum_fus, ...), kind=kLoop, calls=%fused_computation.238 | loop fusion | bytes 5308448 | tf_op jit(solution)/shard_map/jit(dynamic_index_in_dim)/dynamic_slice | solution.py:69
  131.7 10.8 %collective-permute-done.25 = bf16[2,96,864]{2,1,0:T(8,128)(2,1)S(1)} collective-permute-done((bf16[2,96,864]{2,1,0:T(8,128)(2,1)S(1)}, bf16[2,96,864]{2,1,0:T(8,128)(2,1)S(1)}, u32[]{:S(2)}, u32[]{:S(2)}) %collective-permute-start.25) | collective-permute-done | bytes 331808 | tf_op jit(solution)/shard_map/ppermute | solution.py:48
  152.9 8.1 %shard_map.228 = (bf16[8,192,128]{2,1,0:T(8,128)(2,1)}, bf16[192,1024]{1,0:T(8,128)(2,1)S(1)}, f32[8,64,384]{2,1,0:T(8,128)S(1)}, f32[8,384]{1,0:T(8,128)S(1)}, ...) custom-call(s32[1]{0:T(128)} %bitcast.1.hd_ref, ...), custom_call_target="tpu_custom_call" | custom-call | flops 20000000000 | bytes 8388608 | tf_op jit(solution)/shard_map/pallas_call | solution.py:292
  171.0 5.7 all-to-all-done
  193.9 9.4 %collective-permute-done.16 = bf16[128,1536]{1,0:T(8,128)(2,1)S(1)} collective-permute-done((bf16[128,1536]{1,0:T(8,128)(2,1)S(1)}, bf16[128,1536]{1,0:T(8,128)(2,1)S(1)}, u32[]{:S(2)}, u32[]{:S(2)}) %collective-permute-start.16) | collective-permute-done | bytes 393248 | tf_op jit(solution)/shard_map/ppermute | solution.py:48
  204.4 8.4 %collective-permute-done.17 = bf16[128,1536]{1,0:T(8,128)(2,1)S(1)} collective-permute-done((bf16[128,1536]{1,0:T(8,128)(2,1)S(1)}, bf16[128,1536]{1,0:T(8,128)(2,1)S(1)}, u32[]{:S(2)}, u32[]{:S(2)}) %collective-permute-start.17) | collective-permute-done | bytes 393248 | tf_op jit(solution)/shard_map/ppermute | solution.py:48
  214.3 15.7 %collective-permute-done.18 = bf16[128,1536]{1,0:T(8,128)(2,1)S(1)} collective-permute-done((bf16[128,1536]{1,0:T(8,128)(2,1)S(1)}, bf16[128,1536]{1,0:T(8,128)(2,1)S(1)}, u32[]{:S(2)}, u32[]{:S(2)}) %collective-permute-start.18) | collective-permute-done | bytes 393248 | tf_op jit(solution)/shard_map/ppermute | solution.py:48
  231.1 14.8 %collective-permute-done.20 = bf16[128,1536]{1,0:T(8,128)(2,1)S(1)} collective-permute-done((bf16[128,1536]{1,0:T(8,128)(2,1)S(1)}, bf16[128,1536]{1,0:T(8,128)(2,1)S(1)}, u32[]{:S(2)}, u32[]{:S(2)}) %collective-permute-start.20) | collective-permute-done | bytes 393248 | tf_op jit(solution)/shard_map/ppermute | solution.py:48
  246.3 9.2 %collective-permute-done.22 = bf16[128,1536]{1,0:T(8,128)(2,1)S(1)} collective-permute-done((bf16[128,1536]{1,0:T(8,128)(2,1)S(1)}, bf16[128,1536]{1,0:T(8,128)(2,1)S(1)}, u32[]{:S(2)}, u32[]{:S(2)}) %collective-permute-start.22) | collective-permute-done | bytes 393248 | tf_op jit(solution)/shard_map/ppermute | solution.py:48
  257.3 4.8 fusion.71
  262.1 5.8 fusion.72
  267.9 6.2 multiply_convert_fusion
  290.5 5.7 collective-permute-done.32
  297.1 7.6 %collective-permute-done.33 = bf16[128,1536]{1,0:T(8,128)(2,1)S(1)} collective-permute-done((bf16[128,1536]{1,0:T(8,128)(2,1)S(1)}, bf16[128,1536]{1,0:T(8,128)(2,1)S(1)}, u32[]{:S(2)}, u32[]{:S(2)}) %collective-permute-start.33) | collective-permute-done | bytes 393248 | tf_op jit(solution)/shard_map/ppermute | solution.py:48
  305.1 12.1 %collective-permute-done.34 = bf16[128,1536]{1,0:T(8,128)(2,1)S(1)} collective-permute-done((bf16[128,1536]{1,0:T(8,128)(2,1)S(1)}, bf16[128,1536]{1,0:T(8,128)(2,1)S(1)}, u32[]{:S(2)}, u32[]{:S(2)}) %collective-permute-start.34) | collective-permute-done | bytes 393248 | tf_op jit(solution)/shard_map/ppermute | solution.py:48
  317.3 7.4 %collective-permute-done.36 = bf16[128,1536]{1,0:T(8,128)(2,1)S(1)} collective-permute-done((bf16[128,1536]{1,0:T(8,128)(2,1)S(1)}, bf16[128,1536]{1,0:T(8,128)(2,1)S(1)}, u32[]{:S(2)}, u32[]{:S(2)}) %collective-permute-start.36) | collective-permute-done | bytes 393248 | tf_op jit(solution)/shard_map/ppermute | solution.py:48
  330.0 7.0 %convolution_convert_fusion.1 = bf16[1536,864]{0,1:T(8,128)(2,1)} fusion(bf16[1024,864]{0,1:T(8,128)(2,1)} %get-tuple-element.110, bf16[1024,1536]{1,0:T(8,128)(2,1)} %bitcast.513), kind=kOutput, calls=%fused_computation.15 | convolution fusion | flops 2719236096 | bytes 7569408 | tf_op jit(solution)/shard_map/dot_general | solution.py:38
  343.4 5.0 all-to-all-start.1
  348.9 6.9 %convolution_convert_fusion.3 = bf16[864,1536]{1,0:T(8,128)(2,1)} fusion(bf16[1024,864]{0,1:T(8,128)(2,1)} %get-tuple-element.112, bf16[1024,1536]{1,0:T(8,128)(2,1)} %all-gather.7.cloned.1.call-done), kind=kOutput, calls=%fused_computation.17 | convolution fusion | flops 2719236096 | bytes 7569408 | tf_op jit(solution)/shard_map/dot_general | solution.py:38
  363.8 10.5 %shard_map.229 = (bf16[192,1024]{1,0:T(8,128)(2,1)S(1)}, f32[128,1024]{1,0:T(8,128)S(1)}, bf16[128,1024]{1,0:T(8,128)(2,1)S(1)}, f32[64,128]{1,0:T(8,128)S(1)}) custom-call(s32[1]{0:T(128)} %bitcast.1.hd_ref, bf16[320,1024]{1,0:T(8,128)(2,1)S(1)} %convolution_convert_fusion.7.own_ref, bf16[8,192,128]{2,1,0:T(8,128)(2,1)S(1)} %all-to-all-done.1.grad_ref, ...), custom_call_target="tpu_custom_call" | custom-call | flops 40000000000 | bytes 8388608 | tf_op jit(solution)/shard_map/pallas_call | solution.py:292
  394.5 7.6 %convolution_convert_fusion = bf16[1024,1536]{1,0:T(8,128)(2,1)} fusion(bf16[1024,864]{0,1:T(8,128)(2,1)} %get-tuple-element.112, bf16[864,1536]{1,0:T(8,128)(2,1)} %bitcast.523), kind=kOutput, calls=%fused_computation.10 | convolution fusion | flops 2719481856 | bytes 7569408 | tf_op jit(solution)/shard_map/dot_general | solution.py:38
  402.7 5.2 all-to-all-start.2
  478.6 9.3 %collective-permute-done.59 = bf16[8,12,320]{2,0,1:T(8,128)(2,1)S(1)} collective-permute-done((bf16[8,12,320]{2,0,1:T(8,128)(2,1)S(1)}, bf16[8,12,320]{2,0,1:T(8,128)(2,1)S(1)}, u32[]{:S(2)}, u32[]{:S(2)}) %collective-permute-start.59) | collective-permute-done | bytes 61472 | tf_op jit(solution)/shard_map/ppermute | solution.py:94
  525.4 12.3 %collective-permute-done.74 = bf16[2,8,24,864]{3,2,1,0:T(8,128)(2,1)} collective-permute-done((bf16[2,8,24,864]{3,2,1,0:T(8,128)(2,1)}, bf16[2,8,24,864]{3,2,1,0:T(8,128)(2,1)}, u32[]{:S(2)}, u32[]{:S(2)}) %collective-permute-start.74) | collective-permute-done | bytes 663584 | tf_op jit(solution)/shard_map/ppermute | solution.py:90
  544.8 6.2 collective-permute-done.76
  585.2 12.2 %collective-permute-done.85 = bf16[2,8,24,864]{3,2,1,0:T(8,128)(2,1)} collective-permute-done((bf16[2,8,24,864]{3,2,1,0:T(8,128)(2,1)}, bf16[2,8,24,864]{3,2,1,0:T(8,128)(2,1)}, u32[]{:S(2)}, u32[]{:S(2)}) %collective-permute-start.85) | collective-permute-done | bytes 663584 | tf_op jit(solution)/shard_map/ppermute | solution.py:90
  598.6 7.3 %collective-permute-done.86 = bf16[2,8,24,864]{3,2,1,0:T(8,128)(2,1)} collective-permute-done((bf16[2,8,24,864]{3,2,1,0:T(8,128)(2,1)}, bf16[2,8,24,864]{3,2,1,0:T(8,128)(2,1)}, u32[]{:S(2)}, u32[]{:S(2)}) %collective-permute-start.86) | collective-permute-done | bytes 663584 | tf_op jit(solution)/shard_map/ppermute | solution.py:90
  640.1 6.1 fusion.23
  651.3 5.2 collective-permute-done.42
  (538 shorter events, 397.4 us)
Async XLA Ops:
  7.2 163.7 %all-gather.5.cloned.1.call-start = ((), (), s32[]{:S(2)}) async-start(), calls=%async_computation.4 | async-start | bytes 5013504 | tf_op jit(solution)/shard_map/all_gather | solution.py:371
  14.7 31.4 %collective-permute-start.10 = (bf16[128,1536]{1,0:T(8,128)(2,1)S(1)}, bf16[128,1536]{1,0:T(8,128)(2,1)S(1)}, u32[]{:S(2)}, u32[]{:S(2)}) collective-permute-start(bf16[128,1536]{1,0:T(8,128)(2,1)S(1)} %fusion.17), channel_id=1, source_target_pairs={{0,10},{2,12},{4,14},{6,8},{8,2},{10,4},{12,6},{14,0},{1,11},{3,13... | collective-permute-start | bytes 1179656 | tf_op jit(solution)/shard_map/ppermute | solution.py:48
  15.8 33.1 %collective-permute-start.11 = (bf16[128,1536]{1,0:T(8,128)(2,1)S(1)}, bf16[128,1536]{1,0:T(8,128)(2,1)S(1)}, u32[]{:S(2)}, u32[]{:S(2)}) collective-permute-start(bf16[128,1536]{1,0:T(8,128)(2,1)S(1)} %fusion.17), channel_id=1, source_target_pairs={{0,14},{2,8},{4,10},{6,12},{8,6},{10,0},{12,2},{14,4},{1,15},{3,9}... | collective-permute-start | bytes 1179656 | tf_op jit(solution)/shard_map/ppermute | solution.py:48
  18.8 34.5 %collective-permute-start.12 = (bf16[128,1536]{1,0:T(8,128)(2,1)S(1)}, bf16[128,1536]{1,0:T(8,128)(2,1)S(1)}, u32[]{:S(2)}, u32[]{:S(2)}) collective-permute-start(bf16[128,1536]{1,0:T(8,128)(2,1)S(1)} %fusion.17), channel_id=1, source_target_pairs={{0,2},{2,4},{4,6},{6,0},{8,10},{10,12},{12,14},{14,8},{1,3},{3,5},... | collective-permute-start | bytes 1179656 | tf_op jit(solution)/shard_map/ppermute | solution.py:48
  24.4 31.9 %collective-permute-start.13 = (bf16[128,1536]{1,0:T(8,128)(2,1)S(1)}, bf16[128,1536]{1,0:T(8,128)(2,1)S(1)}, u32[]{:S(2)}, u32[]{:S(2)}) collective-permute-start(bf16[128,1536]{1,0:T(8,128)(2,1)S(1)} %fusion.17), channel_id=1, source_target_pairs={{0,6},{2,0},{4,2},{6,4},{8,14},{10,8},{12,10},{14,12},{1,7},{3,1},... | collective-permute-start | bytes 1179656 | tf_op jit(solution)/shard_map/ppermute | solution.py:48
  64.4 26.6 %collective-permute-start.2 = (bf16[96,320]{1,0:T(8,128)(2,1)S(1)}, bf16[96,320]{1,0:T(8,128)(2,1)S(1)}, u32[]{:S(2)}, u32[]{:S(2)}) collective-permute-start(bf16[96,320]{1,0:T(8,128)(2,1)S(1)} %bitcast.558), channel_id=1, source_target_pairs={{0,10},{2,12},{4,14},{6,8},{8,2},{10,4},{12,6},{14,0},{1,11},{3,13... | collective-permute-start | bytes 184328 | tf_op jit(solution)/shard_map/ppermute | solution.py:48
  91.0 76.3 %collective-permute-start.31 = (bf16[432,1536]{1,0:T(8,128)(2,1)}, bf16[432,1536]{1,0:T(8,128)(2,1)}, u32[]{:S(2)}, u32[]{:S(2)}) collective-permute-start(bf16[432,1536]{1,0:T(8,128)(2,1)} %param.24), channel_id=1, source_target_pairs={{0,1},{1,0},{2,3},{3,2},{4,5},{5,4},{6,7},{7,6},{8,9},{9,8},{10,11... | collective-permute-start | bytes 3981320 | tf_op jit(solution)/shard_map/ppermute | solution.py:138
  114.5 28.0 %collective-permute-start.25 = (bf16[2,96,864]{2,1,0:T(8,128)(2,1)S(1)}, bf16[2,96,864]{2,1,0:T(8,128)(2,1)S(1)}, u32[]{:S(2)}, u32[]{:S(2)}) collective-permute-start(bf16[2,96,864]{2,1,0:T(8,128)(2,1)S(1)} %bitcast.550), channel_id=1, source_target_pairs={{0,10},{2,12},{4,14},{6,8},{8,2},{10,4},{12,6},{14,0},{1,11},{3,13... | collective-permute-start | bytes 995336 | tf_op jit(solution)/shard_map/ppermute | solution.py:48
  117.3 27.3 %collective-permute-start.26 = (bf16[2,96,864]{2,1,0:T(8,128)(2,1)S(1)}, bf16[2,96,864]{2,1,0:T(8,128)(2,1)S(1)}, u32[]{:S(2)}, u32[]{:S(2)}) collective-permute-start(bf16[2,96,864]{2,1,0:T(8,128)(2,1)S(1)} %bitcast.549), channel_id=1, source_target_pairs={{0,14},{2,8},{4,10},{6,12},{8,6},{10,0},{12,2},{14,4},{1,15},{3,9}... | collective-permute-start | bytes 995336 | tf_op jit(solution)/shard_map/ppermute | solution.py:48
  152.9 29.1 %collective-permute-start.30 = (bf16[8,2,96,864]{3,2,0,1:T(8,128)(2,1)}, bf16[8,2,96,864]{3,2,0,1:T(8,128)(2,1)}, u32[]{:S(2)}, u32[]{:S(2)}) collective-permute-start(bf16[8,2,96,864]{3,2,0,1:T(8,128)(2,1)} %bitcast_dynamic-update-slice_fusion.19), channel_id=1, source_target_pairs={{0,1},{1,0},{2,3},{3,2},{4,5},{5,4},{6,7},{7,6},{8,9},{9,8},{10,11... | collective-permute-start | bytes 7962632 | tf_op jit(solution)/shard_map/ppermute | solution.py:138
  167.2 94.9 %all-gather.7.cloned.1.call-start = ((), (), s32[]{:S(2)}) async-start(), calls=%async_computation.6 | async-start | bytes 3538944 | tf_op jit(solution)/shard_map/all_gather | solution.py:372
  170.9 411.4 %all-gather.11.cloned.1.call-start = ((), (), s32[]{:S(2)}) async-start(), calls=%async_computation.8 | async-start | bytes 3538944 | tf_op jit(solution)/shard_map/all_gather | solution.py:454
  189.8 40.2 %collective-permute-start.18 = (bf16[128,1536]{1,0:T(8,128)(2,1)S(1)}, bf16[128,1536]{1,0:T(8,128)(2,1)S(1)}, u32[]{:S(2)}, u32[]{:S(2)}) collective-permute-start(bf16[128,1536]{1,0:T(8,128)(2,1)S(1)} %get-tuple-element.109), channel_id=1, source_target_pairs={{0,10},{2,12},{4,14},{6,8},{8,2},{10,4},{12,6},{14,0},{1,11},{3,13... | collective-permute-start | bytes 1179656 | tf_op jit(solution)/shard_map/ppermute | solution.py:48
  191.5 39.6 %collective-permute-start.19 = (bf16[128,1536]{1,0:T(8,128)(2,1)S(1)}, bf16[128,1536]{1,0:T(8,128)(2,1)S(1)}, u32[]{:S(2)}, u32[]{:S(2)}) collective-permute-start(bf16[128,1536]{1,0:T(8,128)(2,1)S(1)} %get-tuple-element.109), channel_id=1, source_target_pairs={{0,14},{2,8},{4,10},{6,12},{8,6},{10,0},{12,2},{14,4},{1,15},{3,9}... | collective-permute-start | bytes 1179656 | tf_op jit(solution)/shard_map/ppermute | solution.py:48
  193.9 52.1 %collective-permute-start.20 = (bf16[128,1536]{1,0:T(8,128)(2,1)S(1)}, bf16[128,1536]{1,0:T(8,128)(2,1)S(1)}, u32[]{:S(2)}, u32[]{:S(2)}) collective-permute-start(bf16[128,1536]{1,0:T(8,128)(2,1)S(1)} %get-tuple-element.109), channel_id=1, source_target_pairs={{0,2},{2,4},{4,6},{6,0},{8,10},{10,12},{12,14},{14,8},{1,3},{3,5},... | collective-permute-start | bytes 1179656 | tf_op jit(solution)/shard_map/ppermute | solution.py:48
  203.3 42.9 %collective-permute-start.21 = (bf16[128,1536]{1,0:T(8,128)(2,1)S(1)}, bf16[128,1536]{1,0:T(8,128)(2,1)S(1)}, u32[]{:S(2)}, u32[]{:S(2)}) collective-permute-start(bf16[128,1536]{1,0:T(8,128)(2,1)S(1)} %get-tuple-element.109), channel_id=1, source_target_pairs={{0,6},{2,0},{4,2},{6,4},{8,14},{10,8},{12,10},{14,12},{1,7},{3,1},... | collective-permute-start | bytes 1179656 | tf_op jit(solution)/shard_map/ppermute | solution.py:48
  212.8 42.7 %collective-permute-start.22 = (bf16[128,1536]{1,0:T(8,128)(2,1)S(1)}, bf16[128,1536]{1,0:T(8,128)(2,1)S(1)}, u32[]{:S(2)}, u32[]{:S(2)}) collective-permute-start(bf16[128,1536]{1,0:T(8,128)(2,1)S(1)} %get-tuple-element.109), channel_id=1, source_target_pairs={{0,8},{2,10},{4,12},{6,14},{8,0},{10,2},{12,4},{14,6},{1,9},{3,11}... | collective-permute-start | bytes 1179656 | tf_op jit(solution)/shard_map/ppermute | solution.py:48
  286.3 31.0 %collective-permute-start.34 = (bf16[128,1536]{1,0:T(8,128)(2,1)S(1)}, bf16[128,1536]{1,0:T(8,128)(2,1)S(1)}, u32[]{:S(2)}, u32[]{:S(2)}) collective-permute-start(bf16[128,1536]{1,0:T(8,128)(2,1)S(1)} %get-tuple-element.124), channel_id=1, source_target_pairs={{0,10},{2,12},{4,14},{6,8},{8,2},{10,4},{12,6},{14,0},{1,11},{3,13... | collective-permute-start | bytes 1179656 | tf_op jit(solution)/shard_map/ppermute | solution.py:48
  286.3 31.0 %collective-permute-start.35 = (bf16[128,1536]{1,0:T(8,128)(2,1)S(1)}, bf16[128,1536]{1,0:T(8,128)(2,1)S(1)}, u32[]{:S(2)}, u32[]{:S(2)}) collective-permute-start(bf16[128,1536]{1,0:T(8,128)(2,1)S(1)} %get-tuple-element.123), channel_id=1, source_target_pairs={{0,14},{2,8},{4,10},{6,12},{8,6},{10,0},{12,2},{14,4},{1,15},{3,9}... | collective-permute-start | bytes 1179656 | tf_op jit(solution)/shard_map/ppermute | solution.py:48
  290.5 34.2 %collective-permute-start.36 = (bf16[128,1536]{1,0:T(8,128)(2,1)S(1)}, bf16[128,1536]{1,0:T(8,128)(2,1)S(1)}, u32[]{:S(2)}, u32[]{:S(2)}) collective-permute-start(bf16[128,1536]{1,0:T(8,128)(2,1)S(1)} %get-tuple-element.122), channel_id=1, source_target_pairs={{0,2},{2,4},{4,6},{6,0},{8,10},{10,12},{12,14},{14,8},{1,3},{3,5},... | collective-permute-start | bytes 1179656 | tf_op jit(solution)/shard_map/ppermute | solution.py:48
  296.2 29.3 %collective-permute-start.37 = (bf16[128,1536]{1,0:T(8,128)(2,1)S(1)}, bf16[128,1536]{1,0:T(8,128)(2,1)S(1)}, u32[]{:S(2)}, u32[]{:S(2)}) collective-permute-start(bf16[128,1536]{1,0:T(8,128)(2,1)S(1)} %get-tuple-element.121), channel_id=1, source_target_pairs={{0,6},{2,0},{4,2},{6,4},{8,14},{10,8},{12,10},{14,12},{1,7},{3,1},... | collective-permute-start | bytes 1179656 | tf_op jit(solution)/shard_map/ppermute | solution.py:48
  328.9 311.1 %all-gather.9.cloned.1.call-start = ((), (), s32[]{:S(2)}) async-start(), calls=%async_computation.7 | async-start | bytes 8355840 | tf_op jit(solution)/shard_map/all_gather | solution.py:374
  348.4 322.0 %reduce-scatter.2.cloned.1.call-start = ((), (), s32[]{:S(2)}) async-start(), calls=%async_computation.5 | async-start | bytes 3538944 | tf_op jit(solution)/shard_map/reduce_scatter | solution.py:397
  375.6 40.7 %collective-permute-start.88 = (bf16[432,1536]{1,0:T(8,128)(2,1)}, bf16[432,1536]{1,0:T(8,128)(2,1)}, u32[]{:S(2)}, u32[]{:S(2)}) collective-permute-start(bf16[432,1536]{1,0:T(8,128)(2,1)} %dynamic-slice_bitcast_fusion), channel_id=1, source_target_pairs={{0,1},{1,0},{2,3},{3,2},{4,5},{5,4},{6,7},{7,6},{8,9},{9,8},{10,11... | collective-permute-start | bytes 3981320 | tf_op jit(solution)/shard_map/ppermute | solution.py:138
  388.9 109.6 %collective-permute-start.72 = (bf16[2,8,96,864]{3,2,1,0:T(8,128)(2,1)}, bf16[2,8,96,864]{3,2,1,0:T(8,128)(2,1)}, u32[]{:S(2)}, u32[]{:S(2)}) collective-permute-start(bf16[2,8,96,864]{3,2,1,0:T(8,128)(2,1)} %fusion.3), channel_id=1, source_target_pairs={{0,1},{1,0},{2,3},{3,2},{4,5},{5,4},{6,7},{7,6},{8,9},{9,8},{10,11... | collective-permute-start | bytes 7962632 | tf_op jit(solution)/shard_map/ppermute | solution.py:138
  402.7 42.1 %all-to-all-start.2 = ((bf16[8,320,128]{2,1,0:T(8,128)(2,1)}), bf16[8,320,128]{2,1,0:T(8,128)(2,1)}, u32[]{:S(2)}, u32[]{:S(2)}) async-start(bf16[8,320,128]{2,1,0:T(8,128)(2,1)} %get-tuple-element.45), calls=%async_computation.3 | async-start | bytes 1310720 | tf_op jit(solution)/shard_map/all_to_all | solution.py:441
  504.8 33.0 %collective-permute-start.74 = (bf16[2,8,24,864]{3,2,1,0:T(8,128)(2,1)}, bf16[2,8,24,864]{3,2,1,0:T(8,128)(2,1)}, u32[]{:S(2)}, u32[]{:S(2)}) collective-permute-start(bf16[2,8,24,864]{3,2,1,0:T(8,128)(2,1)} %get-tuple-element.128), channel_id=1, source_target_pairs={{0,32},{16,48},{32,64},{48,80},{64,96},{80,112},{96,0},{112,16},{1... | collective-permute-start | bytes 1990664 | tf_op jit(solution)/shard_map/ppermute | solution.py:90
  506.1 31.6 %collective-permute-start.75 = (bf16[2,8,24,864]{3,2,1,0:T(8,128)(2,1)}, bf16[2,8,24,864]{3,2,1,0:T(8,128)(2,1)}, u32[]{:S(2)}, u32[]{:S(2)}) collective-permute-start(bf16[2,8,24,864]{3,2,1,0:T(8,128)(2,1)} %get-tuple-element.127), channel_id=1, source_target_pairs={{0,96},{16,112},{32,0},{48,16},{64,32},{80,48},{96,64},{112,80},{1... | collective-permute-start | bytes 1990664 | tf_op jit(solution)/shard_map/ppermute | solution.py:90
  522.0 29.2 %collective-permute-start.95 = (bf16[2,216,384]{2,1,0:T(8,128)(2,1)S(1)}, bf16[2,216,384]{2,1,0:T(8,128)(2,1)S(1)}, u32[]{:S(2)}, u32[]{:S(2)}) collective-permute-start(bf16[2,216,384]{2,1,0:T(8,128)(2,1)S(1)} %pad_maximum_fusion.7), channel_id=1, source_target_pairs={{0,32},{16,48},{32,64},{48,80},{64,96},{80,112},{96,0},{112,16},{1... | collective-permute-start | bytes 995336 | tf_op jit(solution)/shard_map/ppermute | solution.py:90
  523.5 45.6 %collective-permute-start.96 = (bf16[2,216,384]{2,1,0:T(8,128)(2,1)S(1)}, bf16[2,216,384]{2,1,0:T(8,128)(2,1)S(1)}, u32[]{:S(2)}, u32[]{:S(2)}) collective-permute-start(bf16[2,216,384]{2,1,0:T(8,128)(2,1)S(1)} %pad_maximum_fusion.7), channel_id=1, source_target_pairs={{0,96},{16,112},{32,0},{48,16},{64,32},{80,48},{96,64},{112,80},{1... | collective-permute-start | bytes 995336 | tf_op jit(solution)/shard_map/ppermute | solution.py:90
  578.8 27.1 %collective-permute-start.86 = (bf16[2,8,24,864]{3,2,1,0:T(8,128)(2,1)}, bf16[2,8,24,864]{3,2,1,0:T(8,128)(2,1)}, u32[]{:S(2)}, u32[]{:S(2)}) collective-permute-start(bf16[2,8,24,864]{3,2,1,0:T(8,128)(2,1)} %pad_maximum_fusion.4), channel_id=1, source_target_pairs={{0,32},{16,48},{32,64},{48,80},{64,96},{80,112},{96,0},{112,16},{1... | collective-permute-start | bytes 1990664 | tf_op jit(solution)/shard_map/ppermute | solution.py:90
  580.6 32.0 %collective-permute-start.87 = (bf16[2,8,24,864]{3,2,1,0:T(8,128)(2,1)}, bf16[2,8,24,864]{3,2,1,0:T(8,128)(2,1)}, u32[]{:S(2)}, u32[]{:S(2)}) collective-permute-start(bf16[2,8,24,864]{3,2,1,0:T(8,128)(2,1)} %pad_maximum_fusion.4), channel_id=1, source_target_pairs={{0,96},{16,112},{32,0},{48,16},{64,32},{80,48},{96,64},{112,80},{1... | collective-permute-start | bytes 1990664 | tf_op jit(solution)/shard_map/ppermute | solution.py:90
  (135 other events, 1827.1 us)
Sparse Core Ops, SparseCore 0:
  58.0 42.1 all-gather.4
  171.1 83.6 all-gather.6
  329.0 49.5 all-gather.10
  380.2 58.6 all-gather.8
  441.1 47.0 reduce-scatter.1

commit v2 on v1

v2 whole, which is shorter than its diff:
```python
import jax
import jax.numpy as jnp
from jax import lax
from jax.experimental import pallas as pl
from jax.experimental.pallas import tpu as pltpu
from jax.sharding import Mesh, PartitionSpec as P

HQ = 24
HK = 8
HS = 64
GROUP = HQ // HK

EPSILON = 1e-05
ROPE_BASE = 1000000.0
SCORE_SCALE = 0.125

TEAM = ("hd", "y")
RING = 4
STEPS = (2, 1, 3)
BLOCK = 128
WIDE = 2 * BLOCK
ROWS = GROUP * WIDE


def rms_forward(values, gain):
    factor = lax.rsqrt(jnp.mean(values * values, axis=-1, keepdims=True) + EPSILON)
    return values * factor * gain


def rms_backward(values, gain, grad_out):
    factor = lax.rsqrt(jnp.mean(values * values, axis=-1, keepdims=True) + EPSILON)
    normal = values * factor
    scaled = grad_out * gain
    grad_in = factor * (scaled - normal * jnp.mean(scaled * normal, axis=-1, keepdims=True))
    grad_gain = jnp.sum(grad_out * normal, axis=0)
    return (grad_in, grad_gain)


def dot(left, right, contract):
    return lax.dot_general(
        left, right, (((contract[0],), (contract[1],)), ((), ())), preferred_element_type=jnp.float32
    )


def at(array, index, axis=0):
    return lax.dynamic_index_in_dim(array, index, axis, keepdims=False)


def put(whole, array, *index):
    lead = (1,) * len(index)
    return lax.dynamic_update_slice(whole, array.reshape(lead + array.shape), index + (0,) * array.ndim)


def fence(*values):
    return lax.optimization_barrier(values)


def ring(array, axis, step):
    return lax.ppermute(array, axis, [(i, (i + step) % RING) for i in range(RING)])


def ring_z(array, step):
    return ring(array, ("zh", "zl"), step)


def swap(array, axis):
    return lax.ppermute(array, axis, [(0, 1), (1, 0)])


def in_order(mine, other, axis_name, axis):
    first = lax.axis_index(axis_name) == 0
    return jnp.stack([jnp.where(first, mine, other), jnp.where(first, other, mine)], axis=axis)


def gather_tokens(block):
    y, hd = lax.axis_index("y"), lax.axis_index("hd")
    whole = jnp.zeros((RING, 2, *block.shape), block.dtype)
    blocks = [(y, block)] + [((y - step) % RING, ring(block, "y", step)) for step in STEPS]
    for source, came in blocks:
        whole = put(whole, came, source, hd)
        whole = put(whole, swap(came, "hd"), source, 1 - hd)
    return whole.reshape(-1, block.shape[-1])


def scatter_tokens(parts):
    y, hd = lax.axis_index("y"), lax.axis_index("hd")
    parts = parts.reshape(RING, 2, BLOCK, -1)
    chip = at(parts, hd, 1).astype(jnp.float32) + swap(at(parts, 1 - hd, 1), "hd").astype(jnp.float32)
    chip = chip.astype(jnp.bfloat16)
    arrived = [ring(at(chip, (y + step) % RING), "y", step) for step in STEPS]
    return sum((came.astype(jnp.float32) for came in arrived), at(chip, y).astype(jnp.float32))


def exchange_large(blocks):
    y, hd = lax.axis_index("y"), lax.axis_index("hd")
    came = jnp.zeros((RING, 2, *blocks.shape[2:]), blocks.dtype)
    came = put(came, at(blocks, y, 1), y)
    for step in STEPS:
        came = put(came, ring(at(blocks, (y + step) % RING, 1), "y", step), (y - step) % RING)
    return in_order(at(came, hd, 1), swap(at(came, 1 - hd, 1), "hd"), "hd", 0)


def exchange(blocks):
    return lax.all_to_all(blocks, TEAM, split_axis=0, concat_axis=0, tiled=True)


def whole_rows(blocks):
    other = jnp.stack([ring_z(blocks[0], 1), ring_z(blocks[1], 3)], axis=1)
    return in_order(blocks.swapaxes(0, 1), other, "zl", 0)


def sum_ring(pieces, index, move):
    arrived = [move(at(pieces, (index + step) % RING), step) for step in STEPS]
    total = sum((came.astype(jnp.float32) for came in arrived), at(pieces, index).astype(jnp.float32))
    return total.astype(jnp.bfloat16)


def sum_x(pieces):
    return sum_ring(pieces, lax.axis_index("x"), lambda a, step: ring(a, "x", step))


def sum_z(pieces):
    z = lax.axis_index("zh") * 2 + lax.axis_index("zl")
    return sum_ring(pieces, z, ring_z)


def spread(piece):
    x = lax.axis_index("x")
    pair = in_order(piece, swap(piece, "zh"), "zh", 0)
    whole = put(jnp.zeros((RING, *pair.shape), pair.dtype), pair, x)
    for step in STEPS:
        whole = put(whole, ring(pair, "x", step), (x - step) % RING)
    return whole


def sum_everywhere(terms):
    for axis, count in (("hd", 2), ("y", 4), ("zl", 2), ("zh", 2), ("x", 4)):
        step = 1
        while step < count:
            terms = terms + lax.ppermute(terms, axis, [(i, i ^ step) for i in range(count)])
            step *= 2
    return terms


def turn(values, cosine, sine):
    first, second = values[: HS // 2], values[HS // 2 :]
    return jnp.concatenate([first * cosine - second * sine, second * cosine + first * sine], axis=0)


def unturn(grads, cosine, sine):
    first, second = grads[: HS // 2], grads[HS // 2 :]
    return jnp.concatenate([first * cosine + second * sine, second * cosine - first * sine], axis=0)


def head_norm(values, gain):
    return values * lax.rsqrt(jnp.mean(values * values, axis=0, keepdims=True) + EPSILON) * gain


def head_norm_back(values, gain, grad_out):
    factor = lax.rsqrt(jnp.mean(values * values, axis=0, keepdims=True) + EPSILON)
    normal = values * factor
    scaled = grad_out * gain
    grad_in = factor * (scaled - normal * jnp.mean(scaled * normal, axis=0, keepdims=True))
    return grad_in, grad_out * normal


def allowed_keys():
    key = lax.broadcasted_iota(jnp.int32, (WIDE, ROWS), 0)
    query = lax.broadcasted_iota(jnp.int32, (WIDE, ROWS), 1) % WIDE
    return key <= query


def member(block):
    return block % 2 * RING + block // 2


def attend_kernel(
    half_ref, own_ref, other_ref, cos_ref, sin_ref, cos2_ref, sin2_ref, qgain_ref, kgain_ref,
    blocks_ref, att_ref, out_ref, lse_ref, q_ref, kt_ref, k_ref, v_ref, vt_ref, total_ref,
):
    seen = own_ref.shape[1]
    count = seen // WIDE
    qgain, kgain = qgain_ref[...], kgain_ref[...]
    vt_ref[HS:, :] = jnp.ones((HS, vt_ref.shape[1]), jnp.bfloat16)
    for c in range(count):
        cols = slice(c * WIDE, (c + 1) * WIDE)
        sides = (
            (own_ref[GROUP * HS :, cols], cos_ref[:, cols], sin_ref[:, cols]),
            (other_ref[:, cols], cos2_ref[:, cols], sin2_ref[:, cols]),
        )
        for side, (pair, cosine, sine) in enumerate(sides):
            pair = pair.astype(jnp.float32)
            place = slice(side * seen + c * WIDE, side * seen + (c + 1) * WIDE)
            key = turn(head_norm(pair[:HS], kgain), cosine, sine)
            kt_ref[:, place] = key.astype(jnp.bfloat16)
            k_ref[place, :] = key.T.astype(jnp.bfloat16)
            vt_ref[:HS, place] = pair[HS:].astype(jnp.bfloat16)
            v_ref[place, :] = pair[HS:].T.astype(jnp.bfloat16)
        for head in range(GROUP):
            query = own_ref[head * HS : (head + 1) * HS, cols].astype(jnp.float32)
            query = turn(head_norm(query, qgain), cos_ref[:, cols], sin_ref[:, cols])
            q_ref[c, :, head * WIDE : (head + 1) * WIDE] = (query * SCORE_SCALE).astype(jnp.bfloat16)
    allowed = allowed_keys()

    def terms(i, start, masked):
        keys = slice(start, start + WIDE)
        weights = jnp.exp(dot(k_ref[keys, :], q_ref[i], (1, 0)))
        if masked:
            weights = jnp.where(allowed, weights, 0.0)
        return dot(vt_ref[:, keys], weights.astype(jnp.bfloat16), (1, 0))

    for i in range(count):
        total_ref[i] = sum(terms(i, c * WIDE, c == i) for c in range(i + 1))

    @pl.when(half_ref[0] == 1)
    def _():
        for i in range(count):
            total_ref[i] += sum(terms(i, seen + c * WIDE, False) for c in range(count))

    for i in range(count):
        total = total_ref[i]
        norm = total[HS : HS + 1]
        result = total[:HS] / norm
        lse_ref[i : i + 1, :] = jnp.log(norm)
        out_ref[i] = result
        for head in range(GROUP):
            part = result[:, head * WIDE : (head + 1) * WIDE].astype(jnp.bfloat16)
            att_ref[head * HS : (head + 1) * HS, i * WIDE : (i + 1) * WIDE] = part
            for side in range(2):
                blocks_ref[member(2 * i + side), head * HS : (head + 1) * HS, :] = part[
                    :, side * BLOCK : (side + 1) * BLOCK
                ]


def attend_back_kernel(
    half_ref, own_ref, grad_ref, cos_ref, sin_ref, qgain_ref, out_ref, lse_ref, q_ref, kt_ref, k_ref, v_ref,
    qgrad_ref, kv_own_ref, kv_other_ref, gain_ref, dk_ref, dv_ref, dq_ref, g_ref, delta_ref,
):
    seen = own_ref.shape[1]
    count = seen // WIDE
    qgain = qgain_ref[...]
    allowed = allowed_keys()

    def terms(i, start, masked):
        keys = slice(start, start + WIDE)
        query, grad = q_ref[i], g_ref[i]
        weights = jnp.exp(dot(k_ref[keys, :], query, (1, 0)) - lse_ref[i : i + 1, :])
        if masked:
            weights = jnp.where(allowed, weights, 0.0)
        prob_grad = dot(v_ref[keys, :], grad, (1, 0))
        score_grad = (weights * (prob_grad - delta_ref[i : i + 1, :])).astype(jnp.bfloat16)
        dv_ref[keys, :] += dot(weights.astype(jnp.bfloat16), grad, (1, 1))
        dk_ref[keys, :] += dot(score_grad, query, (1, 1))
        return dot(kt_ref[:, keys], score_grad, (1, 0))

    dk_ref[...] = jnp.zeros_like(dk_ref)
    dv_ref[...] = jnp.zeros_like(dv_ref)
    for i in range(count):
        for head in range(GROUP):
            for side in range(2):
                place = slice(head * WIDE + side * BLOCK, head * WIDE + (side + 1) * BLOCK)
                g_ref[i, :, place] = grad_ref[member(2 * i + side), head * HS : (head + 1) * HS, :]
        delta_ref[i : i + 1, :] = jnp.sum(g_ref[i].astype(jnp.float32) * out_ref[i], axis=0, keepdims=True)
        dq_ref[i] = sum(terms(i, c * WIDE, c == i) for c in range(i + 1))

    @pl.when(half_ref[0] == 1)
    def _():
        for i in range(count):
            dq_ref[i] += sum(terms(i, seen + c * WIDE, False) for c in range(count))

    gain_total = jnp.zeros((HS, WIDE), jnp.float32)
    for i in range(count):
        cols = slice(i * WIDE, (i + 1) * WIDE)
        for head in range(GROUP):
            turned = dq_ref[i, :, head * WIDE : (head + 1) * WIDE] * SCORE_SCALE
            back = unturn(turned, cos_ref[:, cols], sin_ref[:, cols])
            rows = slice(head * HS, (head + 1) * HS)
            lin, gain_part = head_norm_back(own_ref[rows, cols].astype(jnp.float32), qgain, back)
            qgrad_ref[rows, cols] = lin.astype(jnp.bfloat16)
            gain_total = gain_total + gain_part
        for source, rows in ((dk_ref, slice(0, HS)), (dv_ref, slice(HS, 2 * HS))):
            kv_own_ref[rows, cols] = source[i * WIDE : (i + 1) * WIDE, :].T
            kv_other_ref[rows, cols] = source[seen + i * WIDE : seen + (i + 1) * WIDE, :].T.astype(jnp.bfloat16)
    gain_ref[...] = gain_total


def key_back_kernel(
    own_ref, kv_own_ref, kv_came_ref, cos_ref, sin_ref, kgain_ref, qgrad_ref, grad_ref, blocks_ref, gain_ref
):
    total = kv_own_ref[...] + kv_came_ref[...].astype(jnp.float32)
    back = unturn(total[:HS], cos_ref[...], sin_ref[...])
    key = own_ref[GROUP * HS : (GROUP + 1) * HS, :].astype(jnp.float32)
    lin, gain_part = head_norm_back(key, kgain_ref[...], back)
    grad_ref[: GROUP * HS, :] = qgrad_ref[...]
    grad_ref[GROUP * HS : (GROUP + 1) * HS, :] = lin.astype(jnp.bfloat16)
    grad_ref[(GROUP + 1) * HS :, :] = total[HS:].astype(jnp.bfloat16)
    for i in range(own_ref.shape[1] // BLOCK):
        blocks_ref[member(i)] = grad_ref[:, i * BLOCK : (i + 1) * BLOCK]
    gain_ref[...] = jnp.sum(gain_part, axis=1, keepdims=True)


def call(kernel, outs, scratch, args, flops):
    smem = pl.BlockSpec(memory_space=pltpu.SMEM)
    vmem = pl.BlockSpec(memory_space=pltpu.VMEM)
    return pl.pallas_call(
        kernel,
        out_shape=[jax.ShapeDtypeStruct(shape, dtype) for shape, dtype in outs],
        in_specs=[smem if a.dtype == jnp.int32 else vmem for a in args],
        out_specs=[vmem for _ in outs],
        scratch_shapes=scratch,
        compiler_params=pltpu.CompilerParams(vmem_limit_bytes=40 * 1024 * 1024),
        cost_estimate=pl.CostEstimate(flops=flops, bytes_accessed=8 * 1024 * 1024, transcendentals=0),
    )(*args)


def rope_tables(positions):
    half = HS // 2
    freqs = ROPE_BASE ** (-jnp.arange(half, dtype=jnp.float32) * 2.0 / HS)
    angles = freqs[:, None] * positions[None, :].astype(jnp.float32)
    return jnp.cos(angles), jnp.sin(angles)


def on_device(
    inputs,
    norm_gain,
    w_query,
    w_key,
    w_value,
    w_out,
    query_gain,
    key_gain,
    ffn_gain,
    w_gate,
    w_up,
    w_down,
    cotangent,
):
    f32, bf16 = jnp.float32, jnp.bfloat16
    tokens = inputs[0]
    out_grad = cotangent[0]
    rows, width = tokens.shape
    held = w_gate.shape[0]
    half_ffn = w_down.shape[0]
    ffn = 2 * half_ffn
    team = 2 * RING
    seen = team * rows
    quarter, few = width // 4, held // 4
    heads_width = GROUP * HS
    key_at, value_at = heads_width, heads_width + HS
    zl, hd = lax.axis_index("zl"), lax.axis_index("hd")
    tokens32 = tokens.astype(f32)

    normed = rms_forward(tokens32, norm_gain).astype(bf16)
    normed_all = gather_tokens(normed)

    by_head = lambda w: w.reshape(held, team, -1).transpose(1, 0, 2)
    joint_blocks = jnp.concatenate([by_head(w_query), by_head(w_key), by_head(w_value)], axis=2)
    w_joint = exchange(joint_blocks).reshape(2, RING, held, -1)
    w_joint = whole_rows(w_joint).reshape(width, -1)
    by_team = lambda w: w.reshape(held, 2, RING, 2, half_ffn).transpose(3, 2, 0, 1, 4).reshape(2, RING, held, ffn)
    gate_up_blocks = jnp.concatenate([by_team(w_gate), by_team(w_up)], axis=2)
    w_gate_up = whole_rows(exchange_large(gate_up_blocks))
    w_gate_own = w_gate_up[:, :, :, :held].reshape(width, ffn)
    w_up_own = w_gate_up[:, :, :, held:].reshape(width, ffn)
    down_other = jnp.concatenate([ring_z(w_down[: half_ffn // 2], 1), ring_z(w_down[half_ffn // 2 :], 3)])
    w_down_own = in_order(w_down, down_other, "zl", 0).reshape(ffn, width)

    w_out_all = lax.all_gather(w_out, ("zl", "y", "hd"), axis=0, tiled=True)
    grad_in, _ = fence(out_grad, w_out_all)
    grad_all = lax.all_gather(grad_in, ("y", "hd"), axis=0, tiled=True)

    joint = dot(w_joint, normed_all, (0, 1)).astype(bf16)
    other_kv = swap(joint[heads_width:], "zl")
    base = jnp.arange(seen, dtype=jnp.int32)
    cosine, sine = rope_tables(base + zl * seen)
    cosine2, sine2 = rope_tables(base + (1 - zl) * seen)
    half_flag = jnp.reshape(zl, (1,)).astype(jnp.int32)
    qgain, kgain = query_gain[:, None], key_gain[:, None]
    wide = seen // WIDE
    att_blocks, att, att32, lse, q_rot, kt_rot, k_rot, v_nat = call(
        attend_kernel,
        [
            ((team, heads_width, BLOCK), bf16),
            ((heads_width, seen), bf16),
            ((wide, HS, ROWS), f32),
            ((wide, ROWS), f32),
            ((wide, HS, ROWS), bf16),
            ((HS, 2 * seen), bf16),
            ((2 * seen, HS), bf16),
            ((2 * seen, HS), bf16),
        ],
        [pltpu.VMEM((2 * HS, 2 * seen), bf16), pltpu.VMEM((wide, 2 * HS, ROWS), f32)],
        (half_flag, joint, other_kv, cosine, sine, cosine2, sine2, qgain, kgain),
        10_000_000_000,
    )
    attended = exchange(att_blocks).reshape(team * heads_width, rows)

    middle = tokens32 + dot(attended, w_out_all, (0, 0))
    ffn_in = rms_forward(middle, ffn_gain).astype(bf16)
    ffn_all = gather_tokens(ffn_in)
    hidden_grad = lax.optimization_barrier(dot(grad_all, w_down_own, (1, 1)))
    w_joint_rows, _ = fence(jnp.concatenate([w_query, w_key, w_value], axis=1), ffn_all)
    w_joint_all = lax.all_gather(w_joint_rows, ("zl", "y", "hd"), axis=0, tiled=True)

    gate = dot(ffn_all, w_gate_own, (1, 0))
    up_val = dot(ffn_all, w_up_own, (1, 0))
    sigmoid = jax.nn.sigmoid(gate)
    hidden = (gate * sigmoid * up_val).astype(bf16)
    gate_grad = (hidden_grad * up_val * sigmoid * (1.0 + gate * (1.0 - sigmoid))).astype(bf16)
    up_grad = (hidden_grad * gate * sigmoid).astype(bf16)
    ffn_part = (dot(gate_grad, w_gate_own, (1, 1)) + dot(up_grad, w_up_own, (1, 1))).astype(bf16)
    ffn_in_grad = scatter_tokens(ffn_part)

    down_terms = dot(hidden, grad_all, (0, 0)).astype(bf16)
    down_pieces = down_terms.reshape(2, 2, half_ffn // 2, 4, quarter).transpose(1, 0, 3, 2, 4)
    down_pieces = sum_z(down_pieces.reshape(4, 4, half_ffn // 2, quarter))
    by_piece = lambda g: g.astype(bf16).reshape(2, RING, 2, 4, few, ffn).transpose(3, 0, 2, 1, 4, 5)
    gate_up_pieces = jnp.stack(
        [by_piece(dot(ffn_all, gate_grad, (0, 0))), by_piece(dot(ffn_all, up_grad, (0, 0)))], axis=1
    )
    gate_up_pieces = sum_x(gate_up_pieces)

    out_part = dot(hidden, w_down_own, (1, 0)).astype(bf16)
    out_sum = lax.psum_scatter(out_part, ("y", "hd"), scatter_dimension=0, tiled=True)
    output = (middle + out_sum.astype(f32)).astype(bf16)

    middle_part, ffn_gain_part = rms_backward(middle, ffn_gain, ffn_in_grad)
    middle_grad = out_grad.astype(f32) + middle_part
    branch_grad = middle_grad.astype(bf16)
    att_grad = dot(w_out_all, branch_grad, (1, 1)).astype(bf16).reshape(team, heads_width, rows)
    att_grad, down_pieces = fence(exchange(att_grad), down_pieces)

    q_grad, kv_own, kv_other, qgain_part = call(
        attend_back_kernel,
        [
            ((heads_width, seen), bf16),
            ((2 * HS, seen), f32),
            ((2 * HS, seen), bf16),
            ((HS, WIDE), f32),
        ],
        [
            pltpu.VMEM((2 * seen, HS), f32),
            pltpu.VMEM((2 * seen, HS), f32),
            pltpu.VMEM((wide, HS, ROWS), f32),
            pltpu.VMEM((wide, HS, ROWS), bf16),
            pltpu.VMEM((2 * wide, ROWS), f32),
        ],
        (half_flag, joint, att_grad, cosine, sine, qgain, att32, lse, q_rot, kt_rot, k_rot, v_nat),
        20_000_000_000,
    )
    down_pieces = sum_x(down_pieces)
    kv_came, gate_up_pieces, down_pieces = fence(swap(kv_other, "zl"), gate_up_pieces, down_pieces)
    joint_grad, joint_grad_blocks, kgain_part = call(
        key_back_kernel,
        [(joint.shape, bf16), ((team, joint.shape[0], BLOCK), bf16), ((HS, 1), f32)],
        [],
        (joint, kv_own, kv_came, cosine, sine, kgain, q_grad),
        1_000_000_000,
    )
    gate_up_mine = sum_z(gate_up_pieces.reshape(4, 2, RING, few, ffn))
    came = exchange(joint_grad_blocks)
    came = jnp.concatenate(
        [
            came[:, :key_at].reshape(-1, rows),
            came[:, key_at:value_at].reshape(-1, rows),
            came[:, value_at:].reshape(-1, rows),
        ]
    )
    came, gate_up_mine = fence(came, gate_up_mine)
    gate_up_mine = exchange(gate_up_mine.reshape(team, few, ffn))
    normed_grad = dot(came, w_joint_all, (0, 1))
    input_part, norm_gain_part = rms_backward(tokens32, norm_gain, normed_grad)
    input_grad = middle_grad + input_part

    branch_all = lax.all_gather(branch_grad, ("y", "hd"), axis=0, tiled=True)
    out_terms = dot(att, branch_all, (1, 0)).astype(bf16).reshape(2, held, width)
    out_terms = in_order(at(out_terms, hd), swap(at(out_terms, 1 - hd), "hd"), "hd", 0)
    out_pieces = out_terms.reshape(2, 2, held // 2, 4, quarter).transpose(3, 1, 0, 2, 4)
    out_mine = sum_z(sum_x(out_pieces).reshape(4, held // 2, quarter))
    joint_terms = dot(normed_all, joint_grad, (0, 1)).astype(bf16)
    joint_pieces = joint_terms.reshape(2, RING, 2, 4, 2, held // 8, -1).transpose(3, 4, 0, 2, 1, 5, 6)
    joint_mine = sum_z(sum_x(joint_pieces).reshape(4, team, held // 8, -1))
    joint_mine = exchange(joint_mine)

    w_down_grad = spread(down_pieces).transpose(1, 2, 0, 3).reshape(half_ffn, width).astype(f32)
    w_out_grad = spread(out_mine).transpose(1, 2, 0, 3).reshape(held, width).astype(f32)
    gate_up_grad = spread(gate_up_mine).reshape(4, 2, 2, RING, few, 2, half_ffn)
    gate_up_grad = gate_up_grad.transpose(1, 0, 4, 5, 3, 2, 6).reshape(2, held, -1).astype(f32)
    w_joint_grad = spread(joint_mine).reshape(team, team, held // 8, -1)
    w_joint_grad = w_joint_grad.transpose(0, 2, 1, 3).reshape(held, team, -1).astype(f32)

    gains = jnp.concatenate([norm_gain_part, ffn_gain_part, jnp.sum(qgain_part, axis=1), kgain_part[:, 0]])
    gains = sum_everywhere(gains.reshape(-1, BLOCK)).reshape(-1)
    return (
        output[None],
        input_grad[None],
        gains[:width],
        w_joint_grad[:, :, :key_at].reshape(held, -1),
        w_joint_grad[:, :, key_at:value_at].reshape(held, -1),
        w_joint_grad[:, :, value_at:].reshape(held, -1),
        w_out_grad,
        gains[2 * width : 2 * width + HS],
        gains[2 * width + HS :],
        gains[width : 2 * width],
        gate_up_grad[0],
        gate_up_grad[1],
        w_down_grad,
    )


def solution(mesh):
    fine = Mesh(mesh.devices.reshape(4, 2, 2, 4, 2), ("x", "zh", "zl", "y", "hd"))
    by_tokens = P(("x", "zh"), ("zl", "y", "hd"), None)
    by_rows = P(("zl", "y", "hd"), None)
    return jax.shard_map(
        on_device,
        mesh=fine,
        in_specs=(
            by_tokens, P(), by_rows, by_rows, by_rows, by_rows, P(), P(), P(), by_rows, by_rows, by_rows, by_tokens
        ),
        out_specs=(
            by_tokens, by_tokens, P(), by_rows, by_rows, by_rows, by_rows, P(), P(), P(), by_rows, by_rows, by_rows
        ),
        check_vma=False,
    )
```

time: 691 us -> 651 us (0.942)
  waiting for transfers between devices: 239 us -> 195 us
  starting transfers between devices: 163 us -> 133 us
  local copies, waits for them, and re-layouts: 132 us -> 161 us
  other arithmetic: 41.5 us -> 54.4 us
  Pallas kernels: 19.8 us -> 11.4 us
    ppermute x90 -> x71, starting transfers between devices: 144 us -> 99 us  [the longest x54 92.9 us: ring(): lax.ppermute(array, axis, [(i, (i + step) % RING) for i in range(RING)])]
    ppermute x90 -> x71, waiting for transfers between devices: 210 us -> 180 us  [the longest x54 155 us: ring(): lax.ppermute(array, axis, [(i, (i + step) % RING) for i in range(RING)])]
    dynamic_update_slice x57 -> x32, local copies, waits for them, and re-layouts: 30.1 us -> 49.3 us  [put(): lax.dynamic_update_slice(whole, array.reshape(lead + array.shape), index...]
    reshape x7 -> x17, local copies, waits for them, and re-layouts: 8.74 us -> 27.7 us  [the longest x6 13.8 us: on_device(): w.reshape(held, 2, RING, 2, half_ffn).transpose(3, 2, 0, 1, 4)]
    dynamic_slice x3 -> x0, local copies, waits for them, and re-layouts: 17.6 us -> none  [exchange_blocks(): lax.dynamic_index_in_dim(blocks, neighbour(me, dy, dz), 0, keepdims=False)]
    ppermute x7, waiting for transfers between devices: 19.6 us -> 6.56 us  [sum_everywhere(): lax.ppermute(terms, axis, [(i, i ^ step) for i in range(count)])]
    broadcast_in_dim x15 -> x5, local copies, waits for them, and re-layouts: 12.4 us -> 0.76 us  [the longest x4 0.42 us: spread(): whole = put(jnp.zeros((RING, *pair.shape), pair.dtype), pair, x)]
    convert_element_type x6 -> x8, local copies, waits for them, and re-layouts: 10.9 us -> 21.2 us  [the longest x2 8.99 us: on_device(): g.astype(bf16).reshape(2, RING, 2, 4, few, ffn).transpose(3, 0, 2, 1, 4, 5)]
  transfers between devices with their start and end apart: 105 -> 89, of which waited for: 49 -> 32; matrix products, arithmetic and copies ran while one was open for 30% -> 38% of each run, Pallas kernels for 3% -> 2%
where the time goes in v2:
time: 651 us; the launch traced here: 640 us
  waiting for transfers between devices  195 us (30%)
  local copies, waits for them, and re-layouts  161 us (25%)
  starting transfers between devices  133 us (20%)
  matrix products  69.1 us (11%)
  other arithmetic  54.4 us (8%)
  between operations  15.5 us (2%)
  Pallas kernels  11.4 us (2%)
    ppermute x54, waiting for transfers between devices, ring(): lax.ppermute(array, axis, [(i, (i + step) % RING) for i in range(RING)])  155 us
    ppermute x54, starting transfers between devices, ring(): lax.ppermute(array, axis, [(i, (i + step) % RING) for i in range(RING)])  92.9 us
    dot_general x15, matrix products, dot(): lax.dot_general(left, right, (((contract[0],), (contract[1],)), ((), ()))...  69.1 us
    dynamic_update_slice x32, local copies, waits for them, and re-layouts, put(): lax.dynamic_update_slice(whole, array.reshape(lead + array.shape), index...  49.3 us
    ppermute x17, waiting for transfers between devices, swap(): return lax.ppermute(array, axis, [(0, 1), (1, 0)])  25 us
    all_to_all x6, starting transfers between devices, exchange(): return lax.all_to_all(blocks, TEAM, split_axis=0, concat_axis=0, tiled=True)  24.6 us
    unnamed x139, local copies, waits for them, and re-layouts  17.5 us
    reshape x6, local copies, waits for them, and re-layouts, on_device(): w.reshape(held, 2, RING, 2, half_ffn).transpose(3, 2, 0, 1, 4)  13.8 us
  transfers between devices with their start and end apart: 89, of which 32 were waited for; matrix products, arithmetic and copies ran while one was open for 38% of the time, Pallas kernels for 2%

profile of v2, /device:TPU:0, one launch (start us, length us, event | category | flops | bytes accessed | tf_op | source)
XLA Modules:
  0.0 640.3 jit_solution(5075503798506779265)
XLA Ops:
  16.8 5.6 reshape.424
  38.7 4.8 all-to-all-start
  65.7 23.2 %collective-permute-done.18 = bf16[2,192,864]{2,1,0:T(8,128)(2,1)} collective-permute-done((bf16[2,192,864]{2,1,0:T(8,128)(2,1)}, bf16[2,192,864]{2,1,0:T(8,128)(2,1)}, u32[]{:S(2)}, u32[]{:S(2)}) %collective-permute-start.18) | collective-permute-done | bytes 663584 | tf_op jit(solution)/shard_map/ppermute | solution.py:59
  88.9 4.9 collective-permute-start.24
  101.0 10.4 %collective-permute-done.24 = bf16[216,1536]{1,0:T(8,128)(2,1)S(1)} collective-permute-done((bf16[216,1536]{1,0:T(8,128)(2,1)}, bf16[216,1536]{1,0:T(8,128)(2,1)S(1)}, u32[]{:S(2)}, u32[]{:S(2)}) %collective-permute-start.24) | collective-permute-done | bytes 663584 | tf_op jit(solution)/shard_map/ppermute | solution.py:59
  131.4 4.6 collective-permute-done.9.other_ref
  165.1 20.8 %collective-permute-done.21 = bf16[4,192,864]{2,1,0:T(8,128)(2,1)} collective-permute-done((bf16[4,192,864]{2,1,0:T(8,128)(2,1)}, bf16[4,192,864]{2,1,0:T(8,128)(2,1)}, u32[]{:S(2)}, u32[]{:S(2)}) %collective-permute-start.21) | collective-permute-done | bytes 1327136 | tf_op jit(solution)/shard_map/ppermute | solution.py:59
  194.7 4.8 collective-permute-done.15
  202.9 4.8 fusion.66
  207.8 5.8 fusion.67
  213.6 6.5 %multiply_convert_fusion = (bf16[1024,864]{0,1:T(8,128)(2,1)}, bf16[1024,864]{0,1:T(8,128)(2,1)S(1)}, bf16[1024,864]{0,1:T(8,128)(2,1)}) fusion(f32[1024,864]{0,1:T(8,128)S(1)} %fusion.67, f32[1024,864]{0,1:T(8,128)S(1)} %copy-done.61, bf16[1024,1536]{1,0:T(8,128)(2,1)S(1)} %bitcast.433, bf16[1536,864]{1,0:T(8,128)(2,1)S(1)} %bitcast.438), kind=kOutput, calls=%fused_computation.12 | convolution fusion | flops 2732064768 | bytes 18186240 | tf_op jit(solution)/shard_map/dot_general | solution.py:40
  237.1 8.1 %collective-permute-done.26 = bf16[128,1536]{1,0:T(8,128)(2,1)S(1)} collective-permute-done((bf16[128,1536]{1,0:T(8,128)(2,1)S(1)}, bf16[128,1536]{1,0:T(8,128)(2,1)S(1)}, u32[]{:S(2)}, u32[]{:S(2)}) %collective-permute-start.26) | collective-permute-done | bytes 393248 | tf_op jit(solution)/shard_map/ppermute | solution.py:59
  245.2 7.6 %collective-permute-done.27 = bf16[128,1536]{1,0:T(8,128)(2,1)S(1)} collective-permute-done((bf16[128,1536]{1,0:T(8,128)(2,1)S(1)}, bf16[128,1536]{1,0:T(8,128)(2,1)S(1)}, u32[]{:S(2)}, u32[]{:S(2)}) %collective-permute-start.27) | collective-permute-done | bytes 393248 | tf_op jit(solution)/shard_map/ppermute | solution.py:59
  257.8 6.8 %convolution_convert_fusion.3 = bf16[864,1536]{1,0:T(8,128)(2,1)} fusion(bf16[1024,864]{0,1:T(8,128)(2,1)} %get-tuple-element.135, bf16[1024,1536]{1,0:T(8,128)(2,1)} %all-gather.7.cloned.1.call-done), kind=kOutput, calls=%fused_computation.18 | convolution fusion | flops 2719236096 | bytes 7569408 | tf_op jit(solution)/shard_map/dot_general | solution.py:40
  264.6 5.9 reshape.437
  286.9 5.1 convolution_convert_fusion
  296.4 4.5 copy.248
  328.7 6.4 shard_map.229
  335.1 14.0 %collective-permute-done.33 = bf16[2,2,2,4,24,864]{5,4,2,3,1,0:T(8,128)(2,1)} collective-permute-done((bf16[2,2,2,4,24,864]{5,4,2,3,1,0:T(8,128)(2,1)}, bf16[2,2,2,4,24,864]{5,4,2,3,1,0:T(8,128)(2,1)}, u32[]{:S(2)}, u32[]{:S(2)}) %collective-permute-start.33) | collective-permute-done | bytes 1327136 | tf_op jit(solution)/shard_map/ppermute | solution.py:59
  351.7 26.8 %collective-permute-done.34 = bf16[2,2,2,4,24,864]{5,4,2,3,1,0:T(8,128)(2,1)} collective-permute-done((bf16[2,2,2,4,24,864]{5,4,2,3,1,0:T(8,128)(2,1)}, bf16[2,2,2,4,24,864]{5,4,2,3,1,0:T(8,128)(2,1)}, u32[]{:S(2)}, u32[]{:S(2)}) %collective-permute-start.34) | collective-permute-done | bytes 1327136 | tf_op jit(solution)/shard_map/ppermute | solution.py:59
  411.3 7.0 %collective-permute-done.50 = bf16[2,2,2,4,12,320]{5,4,0,2,3,1:T(8,128)(2,1)} collective-permute-done((bf16[2,2,2,4,12,320]{5,4,0,2,3,1:T(8,128)(2,1)S(1)}, bf16[2,2,2,4,12,320]{5,4,0,2,3,1:T(8,128)(2,1)}, u32[]{:S(2)}, u32[]{:S(2)}) %collective-permute-start.50) | collective-permute-done | bytes 245792 | tf_op jit(solution)/shard_map/ppermute | solution.py:59
  437.3 5.2 all-to-all-done.4
  468.7 8.8 %dynamic_update_slice.142 = bf16[4,2,216,384]{3,0,2,1:T(4,128)(2,1)S(1)} dynamic-update-slice(bf16[4,2,216,384]{3,0,2,1:T(4,128)(2,1)S(1)} %copy.281, bf16[1,2,216,384]{3,0,2,1:T(2,128)(2,1)S(1)} %copy.282, s32[]{:T(128)S(6)} %select_n.441, s32[]{:T(128)} %constant.304.clone.1, s32[]{:T(128)} %constant.304.clone.1, s32[]{:T(128)} %constant.304.clone.1) | dynamic-update-slice | bytes 663556 | tf_op jit(solution)/shard_map/dynamic_update_slice | solution.py:51
  477.5 8.8 %dynamic_update_slice.143 = bf16[4,2,216,384]{3,0,2,1:T(4,128)(2,1)S(1)} dynamic-update-slice(bf16[4,2,216,384]{3,0,2,1:T(4,128)(2,1)S(1)} %dynamic_update_slice.142, bf16[1,2,216,384]{3,0,2,1:T(2,128)(2,1)S(1)} %copy.283, s32[]{:T(128)S(6)} %select_n.443, s32[]{:T(128)} %constant.304.clone.1, s32[]{:T(128)} %constant.304.clone.1, s32[]{:T(128)} %constant.304.clone.1) | dynamic-update-slice | bytes 663556 | tf_op jit(solution)/shard_map/dynamic_update_slice | solution.py:51
  490.2 10.0 %collective-permute-done.70 = bf16[8,24,864]{2,1,0:T(8,128)(2,1)S(1)} collective-permute-done((bf16[8,24,864]{2,1,0:T(8,128)(2,1)S(1)}, bf16[8,24,864]{2,1,0:T(8,128)(2,1)S(1)}, u32[]{:S(2)}, u32[]{:S(2)}) %collective-permute-start.70) | collective-permute-done | bytes 331808 | tf_op jit(solution)/shard_map/ppermute | solution.py:67
  513.7 9.0 %collective-permute-done.71 = bf16[2,8,24,864]{3,2,1,0:T(8,128)(2,1)} collective-permute-done((bf16[2,8,24,864]{3,2,1,0:T(8,128)(2,1)}, bf16[2,8,24,864]{3,2,1,0:T(8,128)(2,1)}, u32[]{:S(2)}, u32[]{:S(2)}) %collective-permute-start.71) | collective-permute-done | bytes 663584 | tf_op jit(solution)/shard_map/ppermute | solution.py:59
  526.8 9.0 %collective-permute-done.72 = bf16[2,8,24,864]{3,2,1,0:T(8,128)(2,1)} collective-permute-done((bf16[2,8,24,864]{3,2,1,0:T(8,128)(2,1)}, bf16[2,8,24,864]{3,2,1,0:T(8,128)(2,1)}, u32[]{:S(2)}, u32[]{:S(2)}) %collective-permute-start.72) | collective-permute-done | bytes 663584 | tf_op jit(solution)/shard_map/ppermute | solution.py:59
  538.2 8.8 %reshape.486 = f32[4,2,2,4,24,2,432]{6,5,4,3,2,1,0:T(2,128)} reshape(bf16[4,2,8,24,864]{4,3,2,1,0:T(8,128)(2,1)S(1)} %bitcast_dynamic-update-slice_fusion) | data formatting | bytes 7962624 | tf_op jit(solution)/shard_map/convert_element_type | solution.py:488
  558.3 7.4 %fusion.60 = (f32[1,4,24,2,4,2,432]{6,3,2,4,5,0,1:T(2,128)}, f32[1,4,24,2,4,2,432]{6,3,2,4,5,0,1:T(2,128)S(1)}) fusion(f32[2,4,24,2,4,2,432]{6,3,2,4,5,0,1:T(2,128)} %bitcast.414), kind=kLoop, calls=%fused_computation.220 | loop fusion | bytes 10616832 | tf_op jit(solution)/shard_map/slice | solution.py:506
  568.1 4.7 squeeze.181
  577.1 4.7 squeeze.182
  587.1 6.8 %fusion.31 = (f32[1536]{0:T(1024)S(1)}, f32[128]{0:T(128)}, f32[128,1536]{1,0:T(8,128)S(1)}) fusion(bf16[1,128,1536]{2,1,0:T(8,128)(2,1)S(1)} %copy-done.13, f32[128]{0:T(128)S(1)} %copy-done.53, f32[1536]{0:T(1024)S(1)} %copy-done.48, bf16[2560,128]{1,0:T(8,128)(2,1)} %pad_maximum_fusion.6, bf16[1536,2560]{1,0:T(8,128)(2,1)} %all-gather.9.cloned.1.call-done), kind=kOutput, calls=%fused_computation.75 | convolution fusion | flops 1008007552 | bytes 9712640 | tf_op jit(solution)/shard_map/dot_general | solution.py:40
  (475 shorter events, 353.1 us)
Async XLA Ops:
  10.3 42.5 %collective-permute-start.2 = (bf16[128,1536]{1,0:T(8,128)(2,1)}, bf16[128,1536]{1,0:T(8,128)(2,1)}, u32[]{:S(2)}, u32[]{:S(2)}) collective-permute-start(bf16[128,1536]{1,0:T(8,128)(2,1)} %fusion.25), channel_id=1, source_target_pairs={{0,1},{1,0},{2,3},{3,2},{4,5},{5,4},{6,7},{7,6},{8,9},{9,8},{10,11... | collective-permute-start | bytes 1179656 | tf_op jit(solution)/shard_map/ppermute | solution.py:67
  10.3 46.3 %collective-permute-start.3 = (bf16[128,1536]{1,0:T(8,128)(2,1)}, bf16[128,1536]{1,0:T(8,128)(2,1)}, u32[]{:S(2)}, u32[]{:S(2)}) collective-permute-start(bf16[128,1536]{1,0:T(8,128)(2,1)} %fusion.25), channel_id=1, source_target_pairs={{0,4},{2,6},{4,0},{6,2},{1,5},{3,7},{5,1},{7,3},{8,12},{10,14},{12... | collective-permute-start | bytes 1179656 | tf_op jit(solution)/shard_map/ppermute | solution.py:59
  13.5 82.2 %collective-permute-start.5 = (bf16[128,1536]{1,0:T(8,128)(2,1)}, bf16[128,1536]{1,0:T(8,128)(2,1)}, u32[]{:S(2)}, u32[]{:S(2)}) collective-permute-start(bf16[128,1536]{1,0:T(8,128)(2,1)} %fusion.25), channel_id=1, source_target_pairs={{0,2},{2,4},{4,6},{6,0},{1,3},{3,5},{5,7},{7,1},{8,10},{10,12},{12... | collective-permute-start | bytes 1179656 | tf_op jit(solution)/shard_map/ppermute | solution.py:59
  14.2 81.5 %collective-permute-start.7 = (bf16[128,1536]{1,0:T(8,128)(2,1)}, bf16[128,1536]{1,0:T(8,128)(2,1)}, u32[]{:S(2)}, u32[]{:S(2)}) collective-permute-start(bf16[128,1536]{1,0:T(8,128)(2,1)} %fusion.25), channel_id=1, source_target_pairs={{0,6},{2,0},{4,2},{6,4},{1,7},{3,1},{5,3},{7,5},{8,14},{10,8},{12,... | collective-permute-start | bytes 1179656 | tf_op jit(solution)/shard_map/ppermute | solution.py:59
  43.5 113.1 %all-gather.5.cloned.1.call-start = ((), (), s32[]{:S(2)}) async-start(), calls=%async_computation.7 | async-start | bytes 5013504 | tf_op jit(solution)/shard_map/all_gather | solution.py:368
  52.8 36.1 %collective-permute-start.18 = (bf16[2,192,864]{2,1,0:T(8,128)(2,1)}, bf16[2,192,864]{2,1,0:T(8,128)(2,1)}, u32[]{:S(2)}, u32[]{:S(2)}) collective-permute-start(bf16[2,192,864]{2,1,0:T(8,128)(2,1)} %get-tuple-element.148), channel_id=1, source_target_pairs={{0,2},{2,4},{4,6},{6,0},{1,3},{3,5},{5,7},{7,1},{8,10},{10,12},{12... | collective-permute-start | bytes 1990664 | tf_op jit(solution)/shard_map/ppermute | solution.py:59
  56.5 39.7 %collective-permute-start.19 = (bf16[2,192,864]{2,1,0:T(8,128)(2,1)S(1)}, bf16[2,192,864]{2,1,0:T(8,128)(2,1)}, u32[]{:S(2)}, u32[]{:S(2)}) collective-permute-start(bf16[2,192,864]{2,1,0:T(8,128)(2,1)S(1)} %copy-done.43), channel_id=1, source_target_pairs={{0,6},{2,0},{4,2},{6,4},{1,7},{3,1},{5,3},{7,5},{8,14},{10,8},{12,... | collective-permute-start | bytes 1990664 | tf_op jit(solution)/shard_map/ppermute | solution.py:59
  61.7 39.2 %collective-permute-start.23 = (bf16[216,1536]{1,0:T(8,128)(2,1)}, bf16[216,1536]{1,0:T(8,128)(2,1)S(1)}, u32[]{:S(2)}, u32[]{:S(2)}) collective-permute-start(bf16[216,1536]{1,0:T(8,128)(2,1)} %get-tuple-element.165), channel_id=1, source_target_pairs={{0,8},{8,16},{16,24},{24,0},{1,9},{9,17},{17,25},{25,1},{2,10},{10... | collective-permute-start | bytes 1990664 | tf_op jit(solution)/shard_map/ppermute | solution.py:59
  145.6 62.2 %all-gather.7.cloned.1.call-start = ((), (), s32[]{:S(2)}) async-start(), calls=%async_computation.9 | async-start | bytes 3538944 | tf_op jit(solution)/shard_map/all_gather | solution.py:370
  149.4 36.6 %collective-permute-start.21 = (bf16[4,192,864]{2,1,0:T(8,128)(2,1)}, bf16[4,192,864]{2,1,0:T(8,128)(2,1)}, u32[]{:S(2)}, u32[]{:S(2)}) collective-permute-start(bf16[4,192,864]{2,1,0:T(8,128)(2,1)} %get-tuple-element.145), channel_id=1, source_target_pairs={{0,8},{8,16},{16,24},{24,0},{1,9},{9,17},{17,25},{25,1},{2,10},{10... | collective-permute-start | bytes 3981320 | tf_op jit(solution)/shard_map/ppermute | solution.py:59
  153.4 35.4 %collective-permute-start.22 = (bf16[4,192,864]{2,1,0:T(8,128)(2,1)}, bf16[4,192,864]{2,1,0:T(8,128)(2,1)}, u32[]{:S(2)}, u32[]{:S(2)}) collective-permute-start(bf16[4,192,864]{2,1,0:T(8,128)(2,1)} %get-tuple-element.146), channel_id=1, source_target_pairs={{0,24},{8,0},{16,8},{24,16},{1,25},{9,1},{17,9},{25,17},{2,26},{10... | collective-permute-start | bytes 3981320 | tf_op jit(solution)/shard_map/ppermute | solution.py:59
  156.7 367.3 %all-gather.11.cloned.1.call-start = ((), (), s32[]{:S(2)}) async-start(), calls=%async_computation.11 | async-start | bytes 3538944 | tf_op jit(solution)/shard_map/all_gather | solution.py:475
  160.9 38.6 %collective-permute-start.10 = (bf16[128,1536]{1,0:T(8,128)(2,1)S(1)}, bf16[128,1536]{1,0:T(8,128)(2,1)S(1)}, u32[]{:S(2)}, u32[]{:S(2)}) collective-permute-start(bf16[128,1536]{1,0:T(8,128)(2,1)S(1)} %get-tuple-element.132), channel_id=1, source_target_pairs={{0,1},{1,0},{2,3},{3,2},{4,5},{5,4},{6,7},{7,6},{8,9},{9,8},{10,11... | collective-permute-start | bytes 1179656 | tf_op jit(solution)/shard_map/ppermute | solution.py:67
  161.2 32.7 %collective-permute-start.11 = (bf16[128,1536]{1,0:T(8,128)(2,1)S(1)}, bf16[128,1536]{1,0:T(8,128)(2,1)S(1)}, u32[]{:S(2)}, u32[]{:S(2)}) collective-permute-start(bf16[128,1536]{1,0:T(8,128)(2,1)S(1)} %get-tuple-element.132), channel_id=1, source_target_pairs={{0,4},{2,6},{4,0},{6,2},{1,5},{3,7},{5,1},{7,3},{8,12},{10,14},{12... | collective-permute-start | bytes 1179656 | tf_op jit(solution)/shard_map/ppermute | solution.py:59
  256.7 330.4 %all-gather.9.cloned.1.call-start = ((), (), s32[]{:S(2)}) async-start(), calls=%async_computation.10 | async-start | bytes 8355840 | tf_op jit(solution)/shard_map/all_gather | solution.py:403
  274.1 43.7 %collective-permute-start.29 = (bf16[4,216,384]{2,1,0:T(8,128)(2,1)}, bf16[4,216,384]{2,1,0:T(8,128)(2,1)}, u32[]{:S(2)}, u32[]{:S(2)}) collective-permute-start(bf16[4,216,384]{2,1,0:T(8,128)(2,1)} %get-tuple-element.150), channel_id=1, source_target_pairs={{0,16},{8,24},{16,0},{24,8},{1,17},{9,25},{17,1},{25,9},{2,18},{10... | collective-permute-start | bytes 1990664 | tf_op jit(solution)/shard_map/ppermute | solution.py:59
  275.3 45.2 %collective-permute-start.30 = (bf16[4,216,384]{2,1,0:T(8,128)(2,1)}, bf16[4,216,384]{2,1,0:T(8,128)(2,1)}, u32[]{:S(2)}, u32[]{:S(2)}) collective-permute-start(bf16[4,216,384]{2,1,0:T(8,128)(2,1)} %get-tuple-element.152), channel_id=1, source_target_pairs={{0,8},{8,16},{16,24},{24,0},{1,9},{9,17},{17,25},{25,1},{2,10},{10... | collective-permute-start | bytes 1990664 | tf_op jit(solution)/shard_map/ppermute | solution.py:59
  276.9 43.6 %collective-permute-start.31 = (bf16[4,216,384]{2,1,0:T(8,128)(2,1)S(1)}, bf16[4,216,384]{2,1,0:T(8,128)(2,1)}, u32[]{:S(2)}, u32[]{:S(2)}) collective-permute-start(bf16[4,216,384]{2,1,0:T(8,128)(2,1)S(1)} %get-tuple-element.151), channel_id=1, source_target_pairs={{0,24},{8,0},{16,8},{24,16},{1,25},{9,1},{17,9},{25,17},{2,26},{10... | collective-permute-start | bytes 1990664 | tf_op jit(solution)/shard_map/ppermute | solution.py:59
  309.8 319.6 %reduce-scatter.2.cloned.1.call-start = ((), (), s32[]{:S(2)}) async-start(), calls=%async_computation.8 | async-start | bytes 3538944 | tf_op jit(solution)/shard_map/reduce_scatter | solution.py:424
  314.2 34.8 %collective-permute-start.33 = (bf16[2,2,2,4,24,864]{5,4,2,3,1,0:T(8,128)(2,1)}, bf16[2,2,2,4,24,864]{5,4,2,3,1,0:T(8,128)(2,1)}, u32[]{:S(2)}, u32[]{:S(2)}) collective-permute-start(bf16[2,2,2,4,24,864]{5,4,2,3,1,0:T(8,128)(2,1)} %get-tuple-element.138), channel_id=1, source_target_pairs={{0,64},{32,96},{64,0},{96,32},{1,65},{33,97},{65,1},{97,33},{2,66}... | collective-permute-start | bytes 3981320 | tf_op jit(solution)/shard_map/ppermute | solution.py:59
  317.2 61.4 %collective-permute-start.34 = (bf16[2,2,2,4,24,864]{5,4,2,3,1,0:T(8,128)(2,1)}, bf16[2,2,2,4,24,864]{5,4,2,3,1,0:T(8,128)(2,1)}, u32[]{:S(2)}, u32[]{:S(2)}) collective-permute-start(bf16[2,2,2,4,24,864]{5,4,2,3,1,0:T(8,128)(2,1)} %get-tuple-element.139), channel_id=1, source_target_pairs={{0,32},{32,64},{64,96},{96,0},{1,33},{33,65},{65,97},{97,1},{2,34}... | collective-permute-start | bytes 3981320 | tf_op jit(solution)/shard_map/ppermute | solution.py:59
  317.8 61.3 %collective-permute-start.35 = (bf16[2,2,2,4,24,864]{5,4,2,3,1,0:T(8,128)(2,1)}, bf16[2,2,2,4,24,864]{5,4,2,3,1,0:T(8,128)(2,1)}, u32[]{:S(2)}, u32[]{:S(2)}) collective-permute-start(bf16[2,2,2,4,24,864]{5,4,2,3,1,0:T(8,128)(2,1)} %get-tuple-element.140), channel_id=1, source_target_pairs={{0,96},{32,0},{64,32},{96,64},{1,97},{33,1},{65,33},{97,65},{2,98}... | collective-permute-start | bytes 3981320 | tf_op jit(solution)/shard_map/ppermute | solution.py:59
  323.5 60.1 %collective-permute-start.36 = (bf16[216,384]{1,0:T(8,128)(2,1)}, bf16[216,384]{1,0:T(8,128)(2,1)}, u32[]{:S(2)}, u32[]{:S(2)}) collective-permute-start(bf16[216,384]{1,0:T(8,128)(2,1)} %get-tuple-element.176), channel_id=1, source_target_pairs={{0,64},{32,96},{64,0},{96,32},{1,65},{33,97},{65,1},{97,33},{2,66}... | collective-permute-start | bytes 497672 | tf_op jit(solution)/shard_map/ppermute | solution.py:59
  323.5 61.6 %collective-permute-start.37 = (bf16[216,384]{1,0:T(8,128)(2,1)}, bf16[216,384]{1,0:T(8,128)(2,1)}, u32[]{:S(2)}, u32[]{:S(2)}) collective-permute-start(bf16[216,384]{1,0:T(8,128)(2,1)} %get-tuple-element.178), channel_id=1, source_target_pairs={{0,32},{32,64},{64,96},{96,0},{1,33},{33,65},{65,97},{97,1},{2,34}... | collective-permute-start | bytes 497672 | tf_op jit(solution)/shard_map/ppermute | solution.py:59
  349.0 36.2 %collective-permute-start.38 = (bf16[216,384]{1,0:T(8,128)(2,1)}, bf16[216,384]{1,0:T(8,128)(2,1)S(1)}, u32[]{:S(2)}, u32[]{:S(2)}) collective-permute-start(bf16[216,384]{1,0:T(8,128)(2,1)} %get-tuple-element.177), channel_id=1, source_target_pairs={{0,96},{32,0},{64,32},{96,64},{1,97},{33,1},{65,33},{97,65},{2,98}... | collective-permute-start | bytes 497672 | tf_op jit(solution)/shard_map/ppermute | solution.py:59
  403.7 42.4 %collective-permute-start.39 = (bf16[2,4,24,864]{3,2,1,0:T(8,128)(2,1)}, bf16[2,4,24,864]{3,2,1,0:T(8,128)(2,1)}, u32[]{:S(2)}, u32[]{:S(2)}) collective-permute-start(bf16[2,4,24,864]{3,2,1,0:T(8,128)(2,1)} %get-tuple-element.161), channel_id=1, source_target_pairs={{0,16},{8,24},{16,0},{24,8},{1,17},{9,25},{17,1},{25,9},{2,18},{10... | collective-permute-start | bytes 995336 | tf_op jit(solution)/shard_map/ppermute | solution.py:59
  406.6 41.8 %collective-permute-start.40 = (bf16[2,4,24,864]{3,2,1,0:T(8,128)(2,1)}, bf16[2,4,24,864]{3,2,1,0:T(8,128)(2,1)}, u32[]{:S(2)}, u32[]{:S(2)}) collective-permute-start(bf16[2,4,24,864]{3,2,1,0:T(8,128)(2,1)} %get-tuple-element.163), channel_id=1, source_target_pairs={{0,8},{8,16},{16,24},{24,0},{1,9},{9,17},{17,25},{25,1},{2,10},{10... | collective-permute-start | bytes 995336 | tf_op jit(solution)/shard_map/ppermute | solution.py:59
  428.6 33.4 %collective-permute-start.75 = (bf16[2,216,384]{2,1,0:T(8,128)(2,1)}, bf16[2,216,384]{2,1,0:T(8,128)(2,1)}, u32[]{:S(2)}, u32[]{:S(2)}) collective-permute-start(bf16[2,216,384]{2,1,0:T(8,128)(2,1)} %pad_maximum_fusion.10), channel_id=1, source_target_pairs={{0,64},{32,96},{64,0},{96,32},{1,65},{33,97},{65,1},{97,33},{2,66}... | collective-permute-start | bytes 995336 | tf_op jit(solution)/shard_map/ppermute | solution.py:59
  430.8 34.9 %collective-permute-start.76 = (bf16[2,216,384]{2,1,0:T(8,128)(2,1)}, bf16[2,216,384]{2,1,0:T(8,128)(2,1)}, u32[]{:S(2)}, u32[]{:S(2)}) collective-permute-start(bf16[2,216,384]{2,1,0:T(8,128)(2,1)} %pad_maximum_fusion.10), channel_id=1, source_target_pairs={{0,32},{32,64},{64,96},{96,0},{1,33},{33,65},{65,97},{97,1},{2,34}... | collective-permute-start | bytes 995336 | tf_op jit(solution)/shard_map/ppermute | solution.py:59
  455.0 34.2 %collective-permute-start.56 = (bf16[2,8,12,320]{3,1,2,0:T(8,128)(2,1)}, bf16[2,8,12,320]{3,1,2,0:T(8,128)(2,1)}, u32[]{:S(2)}, u32[]{:S(2)}) collective-permute-start(bf16[2,8,12,320]{3,1,2,0:T(8,128)(2,1)} %pad_maximum_fusion.11), channel_id=1, source_target_pairs={{0,64},{32,96},{64,0},{96,32},{1,65},{33,97},{65,1},{97,33},{2,66}... | collective-permute-start | bytes 368648 | tf_op jit(solution)/shard_map/ppermute | solution.py:59
  455.2 35.0 %collective-permute-start.57 = (bf16[2,8,12,320]{3,1,2,0:T(8,128)(2,1)}, bf16[2,8,12,320]{3,1,2,0:T(8,128)(2,1)S(1)}, u32[]{:S(2)}, u32[]{:S(2)}) collective-permute-start(bf16[2,8,12,320]{3,1,2,0:T(8,128)(2,1)} %pad_maximum_fusion.11), channel_id=1, source_target_pairs={{0,32},{32,64},{64,96},{96,0},{1,33},{33,65},{65,97},{97,1},{2,34}... | collective-permute-start | bytes 368648 | tf_op jit(solution)/shard_map/ppermute | solution.py:59
  462.0 42.8 %collective-permute-start.58 = (bf16[2,8,12,320]{3,1,2,0:T(8,128)(2,1)}, bf16[2,8,12,320]{3,1,2,0:T(8,128)(2,1)}, u32[]{:S(2)}, u32[]{:S(2)}) collective-permute-start(bf16[2,8,12,320]{3,1,2,0:T(8,128)(2,1)} %pad_maximum_fusion.11), channel_id=1, source_target_pairs={{0,96},{32,0},{64,32},{96,64},{1,97},{33,1},{65,33},{97,65},{2,98}... | collective-permute-start | bytes 368648 | tf_op jit(solution)/shard_map/ppermute | solution.py:59
  (122 other events, 1559.1 us)
Sparse Core Ops, SparseCore 0:
  46.1 57.7 all-gather.4
  156.8 40.1 all-gather.6
  256.8 27.6 all-gather.10
  286.1 57.9 all-gather.8
  346.3 37.6 reduce-scatter.1

commit v3 on v2

--- a/solution.py
+++ b/solution.py
@@ -14,7 +14,6 @@
 ROPE_BASE = 1000000.0
 SCORE_SCALE = 0.125
 
-TEAM = ("hd", "y")
 RING = 4
 STEPS = (2, 1, 3)
 BLOCK = 128
@@ -42,6 +41,10 @@
     )
 
 
+SUMMED = ("x", "zh", "zl")
+TEAM = ("y", "hd")
+
+
 def at(array, index, axis=0):
     return lax.dynamic_index_in_dim(array, index, axis, keepdims=False)
 
@@ -72,56 +75,43 @@
     return jnp.stack([jnp.where(first, mine, other), jnp.where(first, other, mine)], axis=axis)
 
 
-def gather_tokens(block):
-    y, hd = lax.axis_index("y"), lax.axis_index("hd")
-    whole = jnp.zeros((RING, 2, *block.shape), block.dtype)
-    blocks = [(y, block)] + [((y - step) % RING, ring(block, "y", step)) for step in STEPS]
-    for source, came in blocks:
-        whole = put(whole, came, source, hd)
-        whole = put(whole, swap(came, "hd"), source, 1 - hd)
-    return whole.reshape(-1, block.shape[-1])
-
-
-def scatter_tokens(parts):
-    y, hd = lax.axis_index("y"), lax.axis_index("hd")
+def gather_column(block):
+    y = lax.axis_index("y")
+    column = put(jnp.zeros((RING, *block.shape), block.dtype), block, y)
+    for step in STEPS:
+        column = put(column, ring(block, "y", step), (y - step) % RING)
+    return column
+
+
+def both_columns(column):
+    return in_order(column, swap(column, "hd"), "hd", 1).reshape(-1, column.shape[-1])
+
+
+def chip_sum(parts):
+    hd = lax.axis_index("hd")
     parts = parts.reshape(RING, 2, BLOCK, -1)
-    chip = at(parts, hd, 1).astype(jnp.float32) + swap(at(parts, 1 - hd, 1), "hd").astype(jnp.float32)
-    chip = chip.astype(jnp.bfloat16)
+    total = at(parts, hd, 1).astype(jnp.float32) + swap(at(parts, 1 - hd, 1), "hd").astype(jnp.float32)
+    return total.astype(jnp.bfloat16)
+
+
+def column_sum(chip):
+    y = lax.axis_index("y")
     arrived = [ring(at(chip, (y + step) % RING), "y", step) for step in STEPS]
     return sum((came.astype(jnp.float32) for came in arrived), at(chip, y).astype(jnp.float32))
 
 
-def exchange_large(blocks):
-    y, hd = lax.axis_index("y"), lax.axis_index("hd")
-    came = jnp.zeros((RING, 2, *blocks.shape[2:]), blocks.dtype)
-    came = put(came, at(blocks, y, 1), y)
-    for step in STEPS:
-        came = put(came, ring(at(blocks, (y + step) % RING, 1), "y", step), (y - step) % RING)
-    return in_order(at(came, hd, 1), swap(at(came, 1 - hd, 1), "hd"), "hd", 0)
-
-
-def exchange(blocks):
-    return lax.all_to_all(blocks, TEAM, split_axis=0, concat_axis=0, tiled=True)
-
-
-def whole_rows(blocks):
-    other = jnp.stack([ring_z(blocks[0], 1), ring_z(blocks[1], 3)], axis=1)
-    return in_order(blocks.swapaxes(0, 1), other, "zl", 0)
-
-
-def sum_ring(pieces, index, move):
-    arrived = [move(at(pieces, (index + step) % RING), step) for step in STEPS]
-    total = sum((came.astype(jnp.float32) for came in arrived), at(pieces, index).astype(jnp.float32))
-    return total.astype(jnp.bfloat16)
+def exchange(blocks, axes):
+    return lax.all_to_all(blocks, axes, split_axis=0, concat_axis=0, tiled=True)
 
 
 def sum_x(pieces):
-    return sum_ring(pieces, lax.axis_index("x"), lambda a, step: ring(a, "x", step))
-
-
-def sum_z(pieces):
-    z = lax.axis_index("zh") * 2 + lax.axis_index("zl")
-    return sum_ring(pieces, z, ring_z)
+    x = lax.axis_index("x")
+    arrived = [ring(at(pieces, (x + step) % RING), "x", step) for step in STEPS]
+    return sum_first([at(pieces, x), *arrived])
+
+
+def sum_first(arrived):
+    return sum(arrived[i].astype(jnp.float32) for i in range(len(arrived))).astype(jnp.bfloat16)
 
 
 def spread(piece):
@@ -134,11 +124,10 @@
 
 
 def sum_everywhere(terms):
-    for axis, count in (("hd", 2), ("y", 4), ("zl", 2), ("zh", 2), ("x", 4)):
-        step = 1
-        while step < count:
-            terms = terms + lax.ppermute(terms, axis, [(i, i ^ step) for i in range(count)])
-            step *= 2
+    terms = terms + swap(terms, "hd")
+    for axis in ("y", ("zh", "zl"), "x"):
+        far, after, before = [ring(terms, axis, step) for step in STEPS]
+        terms = (terms + far) + (after + before)
     return terms
 
 
@@ -170,13 +159,13 @@
     return key <= query
 
 
-def member(block):
-    return block % 2 * RING + block // 2
+def place_of(head):
+    return head % RING * 2 + head // RING
 
 
 def attend_kernel(
     half_ref, own_ref, other_ref, cos_ref, sin_ref, cos2_ref, sin2_ref, qgain_ref, kgain_ref,
-    blocks_ref, att_ref, out_ref, lse_ref, q_ref, kt_ref, k_ref, v_ref, vt_ref, total_ref,
+    att_ref, out_ref, lse_ref, q_ref, kt_ref, k_ref, v_ref, vt_ref, total_ref,
 ):
     seen = own_ref.shape[1]
     count = seen // WIDE
@@ -226,10 +215,6 @@
         for head in range(GROUP):
             part = result[:, head * WIDE : (head + 1) * WIDE].astype(jnp.bfloat16)
             att_ref[head * HS : (head + 1) * HS, i * WIDE : (i + 1) * WIDE] = part
-            for side in range(2):
-                blocks_ref[member(2 * i + side), head * HS : (head + 1) * HS, :] = part[
-                    :, side * BLOCK : (side + 1) * BLOCK
-                ]
 
 
 def attend_back_kernel(
@@ -257,9 +242,9 @@
     dv_ref[...] = jnp.zeros_like(dv_ref)
     for i in range(count):
         for head in range(GROUP):
-            for side in range(2):
-                place = slice(head * WIDE + side * BLOCK, head * WIDE + (side + 1) * BLOCK)
-                g_ref[i, :, place] = grad_ref[member(2 * i + side), head * HS : (head + 1) * HS, :]
+            g_ref[i, :, head * WIDE : (head + 1) * WIDE] = grad_ref[
+                head * HS : (head + 1) * HS, i * WIDE : (i + 1) * WIDE
+            ]
         delta_ref[i : i + 1, :] = jnp.sum(g_ref[i].astype(jnp.float32) * out_ref[i], axis=0, keepdims=True)
         dq_ref[i] = sum(terms(i, c * WIDE, c == i) for c in range(i + 1))
 
@@ -285,7 +270,7 @@
 
 
 def key_back_kernel(
-    own_ref, kv_own_ref, kv_came_ref, cos_ref, sin_ref, kgain_ref, qgrad_ref, grad_ref, blocks_ref, gain_ref
+    own_ref, kv_own_ref, kv_came_ref, cos_ref, sin_ref, kgain_ref, qgrad_ref, grad_ref, gain_ref
 ):
     total = kv_own_ref[...] + kv_came_ref[...].astype(jnp.float32)
     back = unturn(total[:HS], cos_ref[...], sin_ref[...])
@@ -294,12 +279,97 @@
     grad_ref[: GROUP * HS, :] = qgrad_ref[...]
     grad_ref[GROUP * HS : (GROUP + 1) * HS, :] = lin.astype(jnp.bfloat16)
     grad_ref[(GROUP + 1) * HS :, :] = total[HS:].astype(jnp.bfloat16)
-    for i in range(own_ref.shape[1] // BLOCK):
-        blocks_ref[member(i)] = grad_ref[:, i * BLOCK : (i + 1) * BLOCK]
     gain_ref[...] = jnp.sum(gain_part, axis=1, keepdims=True)
 
 
-def call(kernel, outs, scratch, args, flops):
+def pack_kernel(gate_ref, up_ref, out_ref):
+    count, rows, ffn = out_ref.shape
+    team, half, few = count // 2, ffn // 2, rows // 2
+    for ref, top in ((gate_ref, 0), (up_ref, few)):
+        for place in range(team):
+            parts = [
+                ref[:, (zl * team + place) * half : (zl * team + place + 1) * half].astype(jnp.float32)
+                for zl in range(2)
+            ]
+            block = jnp.concatenate(parts, axis=1).astype(jnp.bfloat16)
+            out_ref[place, top : top + few, :] = block
+            out_ref[team + place, top : top + few, :] = block
+
+
+def gate_up_terms_kernel(ffn_ref, gate_ref, up_ref, out_ref):
+    few, ffn = out_ref.shape[2:]
+    chunk = RING * RING * few
+    for c in range(ffn_ref.shape[1] // chunk):
+        left = ffn_ref[:, c * chunk : (c + 1) * chunk]
+        for side, ref in enumerate((gate_ref, up_ref)):
+            terms = dot(left, ref[...], (0, 0)).reshape(RING, RING, few, ffn).astype(jnp.bfloat16)
+            for row in range(RING):
+                for quarter in range(RING):
+                    out_ref[quarter, (side * 2 + c // 2) * 8 + c % 2 * RING + row] = terms[row, quarter]
+
+
+def out_terms_kernel(hd_ref, att_ref, grad_ref, mine_ref, other_ref):
+    pieces, few, _ = mine_ref.shape
+    terms = dot(att_ref[...], grad_ref[...], (1, 0))
+    for hd in range(2):
+        for piece in range(pieces):
+            start = (hd * pieces + piece) * few
+            block = terms[start : start + few].astype(jnp.bfloat16)
+
+            @pl.when(hd_ref[0] == hd)
+            def _():
+                mine_ref[piece] = block
+
+            @pl.when(hd_ref[0] != hd)
+            def _():
+                other_ref[piece] = block
+
+
+def joint_terms_kernel(normed_ref, grad_ref, out_ref):
+    few = out_ref.shape[1]
+    team, half = 2 * RING, normed_ref.shape[1] // 2
+    for zl in range(2):
+        terms = dot(normed_ref[:, zl * half : (zl + 1) * half], grad_ref[...], (0, 1))
+        for place in range(team):
+            for piece in range(8):
+                start = (place * 8 + piece) * few
+                out_ref[(piece * 2 + zl) * team + place] = terms[start : start + few].astype(jnp.bfloat16)
+
+
+def unpack_ffn_kernel(pieces_ref, gate_ref, up_ref):
+    team, few, ffn = pieces_ref.shape[2:]
+    half = ffn // 2
+    for side, ref in enumerate((gate_ref, up_ref)):
+        blocks = [pieces_ref[0, side, place].astype(jnp.float32) for place in range(team)]
+        ref[...] = jnp.concatenate(
+            [block[:, zl * half : (zl + 1) * half] for zl in range(2) for block in blocks], axis=1
+        )
+
+
+def unpack_kernel(pieces_ref, w_down_ref, w_out_ref, w_query_ref, w_key_ref, w_value_ref):
+    team, cols = 2 * RING, pieces_ref.shape[3]
+    down, out, few = w_down_ref.shape[0] // 8, w_out_ref.shape[0] // 8, w_query_ref.shape[0] // 8
+    rows = down + out
+    down_rows, out_rows, joint_rows = [], [], []
+    for x in range(RING):
+        for zh in range(2):
+            piece = pieces_ref[x, zh].astype(jnp.float32)
+            ready = jnp.concatenate([piece[i * rows : (i + 1) * rows] for i in range(RING)], axis=1)
+            down_rows.append(ready[:down])
+            out_rows.append(ready[down:])
+            heads = [RING * rows + place_of(head) * few for head in range(team)]
+            joint_rows.append([piece[start : start + few] for start in heads])
+    w_down_ref[...] = jnp.concatenate([down_rows[x * 2 + zh] for zh in range(2) for x in range(RING)], axis=0)
+    w_out_ref[...] = jnp.concatenate(out_rows, axis=0)
+    targets = (w_query_ref, 0, GROUP * HS), (w_key_ref, GROUP * HS, HS), (w_value_ref, (GROUP + 1) * HS, HS)
+    for target, start, size in targets:
+        parts = [
+            jnp.concatenate([block[:, start : start + size] for block in blocks], axis=1) for blocks in joint_rows
+        ]
+        target[...] = jnp.concatenate(parts, axis=0)
+
+
+def call(kernel, outs, scratch, args):
     smem = pl.BlockSpec(memory_space=pltpu.SMEM)
     vmem = pl.BlockSpec(memory_space=pltpu.VMEM)
     return pl.pallas_call(
@@ -309,7 +379,7 @@
         out_specs=[vmem for _ in outs],
         scratch_shapes=scratch,
         compiler_params=pltpu.CompilerParams(vmem_limit_bytes=40 * 1024 * 1024),
-        cost_estimate=pl.CostEstimate(flops=flops, bytes_accessed=8 * 1024 * 1024, transcendentals=0),
+        cost_estimate=pl.CostEstimate(flops=1024, bytes_accessed=1024, transcendentals=0),
     )(*args)
 
 
@@ -346,28 +416,26 @@
     seen = team * rows
     quarter, few = width // 4, held // 4
     heads_width = GROUP * HS
-    key_at, value_at = heads_width, heads_width + HS
     zl, hd = lax.axis_index("zl"), lax.axis_index("hd")
     tokens32 = tokens.astype(f32)
 
-    normed = rms_forward(tokens32, norm_gain).astype(bf16)
-    normed_all = gather_tokens(normed)
-
     by_head = lambda w: w.reshape(held, team, -1).transpose(1, 0, 2)
     joint_blocks = jnp.concatenate([by_head(w_query), by_head(w_key), by_head(w_value)], axis=2)
-    w_joint = exchange(joint_blocks).reshape(2, RING, held, -1)
-    w_joint = whole_rows(w_joint).reshape(width, -1)
-    by_team = lambda w: w.reshape(held, 2, RING, 2, half_ffn).transpose(3, 2, 0, 1, 4).reshape(2, RING, held, ffn)
-    gate_up_blocks = jnp.concatenate([by_team(w_gate), by_team(w_up)], axis=2)
-    w_gate_up = whole_rows(exchange_large(gate_up_blocks))
-    w_gate_own = w_gate_up[:, :, :, :held].reshape(width, ffn)
-    w_up_own = w_gate_up[:, :, :, held:].reshape(width, ffn)
+    joint_blocks = joint_blocks.reshape(2, RING, held, -1).swapaxes(0, 1).reshape(team, held, -1)
+    joint_blocks = jnp.concatenate([joint_blocks, joint_blocks])
+    normed = rms_forward(tokens32, norm_gain).astype(bf16)
+    w_joint = exchange(joint_blocks, ("zl", "y", "hd"))
+    normed_all = lax.all_gather(normed, TEAM, axis=0, tiled=True)
+    my_rows = lambda w: lax.dynamic_slice_in_dim(w, lax.axis_index("x") * few, few, 0)
+    gate_up_rows = call(pack_kernel, [((2 * team, 2 * few, ffn), bf16)], [], (my_rows(w_gate), my_rows(w_up)))[0]
+    w_joint, gate_up_rows, grad_in = fence(w_joint, gate_up_rows, out_grad)
+    w_joint = w_joint.reshape(width, -1)
+    grad_all = lax.all_gather(grad_in, TEAM, axis=0, tiled=True)
+    gate_up_rows = exchange(gate_up_rows, ("zl", "y", "hd"))
     down_other = jnp.concatenate([ring_z(w_down[: half_ffn // 2], 1), ring_z(w_down[half_ffn // 2 :], 3)])
     w_down_own = in_order(w_down, down_other, "zl", 0).reshape(ffn, width)
-
-    w_out_all = lax.all_gather(w_out, ("zl", "y", "hd"), axis=0, tiled=True)
-    grad_in, _ = fence(out_grad, w_out_all)
-    grad_all = lax.all_gather(grad_in, ("y", "hd"), axis=0, tiled=True)
+    out_rows = in_order(w_out, swap(w_out, "zl"), "zl", 0)
+    w_out_own = in_order(at(out_rows, hd), swap(at(out_rows, 1 - hd), "hd"), "hd", 0).reshape(heads_width, width)
 
     joint = dot(w_joint, normed_all, (0, 1)).astype(bf16)
     other_kv = swap(joint[heads_width:], "zl")
@@ -377,10 +445,9 @@
     half_flag = jnp.reshape(zl, (1,)).astype(jnp.int32)
     qgain, kgain = query_gain[:, None], key_gain[:, None]
     wide = seen // WIDE
-    att_blocks, att, att32, lse, q_rot, kt_rot, k_rot, v_nat = call(
+    att, att32, lse, q_rot, kt_rot, k_rot, v_nat = call(
         attend_kernel,
         [
-            ((team, heads_width, BLOCK), bf16),
             ((heads_width, seen), bf16),
             ((wide, HS, ROWS), f32),
             ((wide, ROWS), f32),
@@ -391,17 +458,16 @@
         ],
         [pltpu.VMEM((2 * HS, 2 * seen), bf16), pltpu.VMEM((wide, 2 * HS, ROWS), f32)],
         (half_flag, joint, other_kv, cosine, sine, cosine2, sine2, qgain, kgain),
-        10_000_000_000,
-    )
-    attended = exchange(att_blocks).reshape(team * heads_width, rows)
-
-    middle = tokens32 + dot(attended, w_out_all, (0, 0))
+    )
+    att, gate_up_rows = fence(att, gate_up_rows)
+    gate_up_all = lax.all_gather(gate_up_rows, "x", axis=0, tiled=False)
+    chip = chip_sum(dot(att, w_out_own, (0, 0)).astype(bf16))
+    middle = tokens32 + column_sum(chip)
+    gate_up_all = gate_up_all.reshape(RING, 2 * team, 2, few, ffn).transpose(2, 1, 0, 3, 4).reshape(2, width, ffn)
+    w_gate_own, w_up_own = gate_up_all[0], gate_up_all[1]
     ffn_in = rms_forward(middle, ffn_gain).astype(bf16)
-    ffn_all = gather_tokens(ffn_in)
-    hidden_grad = lax.optimization_barrier(dot(grad_all, w_down_own, (1, 1)))
-    w_joint_rows, _ = fence(jnp.concatenate([w_query, w_key, w_value], axis=1), ffn_all)
-    w_joint_all = lax.all_gather(w_joint_rows, ("zl", "y", "hd"), axis=0, tiled=True)
-
+    ffn_all = both_columns(gather_column(ffn_in))
+    hidden_grad = dot(grad_all, w_down_own, (1, 1))
     gate = dot(ffn_all, w_gate_own, (1, 0))
     up_val = dot(ffn_all, w_up_own, (1, 0))
     sigmoid = jax.nn.sigmoid(gate)
@@ -409,26 +475,27 @@
     gate_grad = (hidden_grad * up_val * sigmoid * (1.0 + gate * (1.0 - sigmoid))).astype(bf16)
     up_grad = (hidden_grad * gate * sigmoid).astype(bf16)
     ffn_part = (dot(gate_grad, w_gate_own, (1, 1)) + dot(up_grad, w_up_own, (1, 1))).astype(bf16)
-    ffn_in_grad = scatter_tokens(ffn_part)
-
-    down_terms = dot(hidden, grad_all, (0, 0)).astype(bf16)
-    down_pieces = down_terms.reshape(2, 2, half_ffn // 2, 4, quarter).transpose(1, 0, 3, 2, 4)
-    down_pieces = sum_z(down_pieces.reshape(4, 4, half_ffn // 2, quarter))
-    by_piece = lambda g: g.astype(bf16).reshape(2, RING, 2, 4, few, ffn).transpose(3, 0, 2, 1, 4, 5)
-    gate_up_pieces = jnp.stack(
-        [by_piece(dot(ffn_all, gate_grad, (0, 0))), by_piece(dot(ffn_all, up_grad, (0, 0)))], axis=1
-    )
-    gate_up_pieces = sum_x(gate_up_pieces)
-
-    out_part = dot(hidden, w_down_own, (1, 0)).astype(bf16)
-    out_sum = lax.psum_scatter(out_part, ("y", "hd"), scatter_dimension=0, tiled=True)
-    output = (middle + out_sum.astype(f32)).astype(bf16)
+    chip, gate_right, up_right, hidden_left = fence(chip_sum(ffn_part), gate_grad, up_grad, hidden)
+    ffn_in_grad = column_sum(chip)
+
+    gate_up_terms = call(
+        gate_up_terms_kernel,
+        [((RING, 4 * team, few, ffn), bf16)],
+        [],
+        (ffn_all, gate_right, up_right),
+    )[0]
+    gate_up_sum = lax.psum_scatter(gate_up_terms, "x", scatter_dimension=0, tiled=False)
+    down_terms = dot(hidden_left, grad_all, (0, 0)).astype(bf16).reshape(4, half_ffn // 2, width)
+    down_came = exchange(down_terms, ("zl", "zh"))
+    ffn_in_grad, _, _, hidden_last = fence(ffn_in_grad, gate_up_terms, down_terms, hidden)
 
     middle_part, ffn_gain_part = rms_backward(middle, ffn_gain, ffn_in_grad)
     middle_grad = out_grad.astype(f32) + middle_part
     branch_grad = middle_grad.astype(bf16)
-    att_grad = dot(w_out_all, branch_grad, (1, 1)).astype(bf16).reshape(team, heads_width, rows)
-    att_grad, down_pieces = fence(exchange(att_grad), down_pieces)
+    out_part = dot(hidden_last, w_down_own, (1, 0)).astype(bf16)
+    column, out_part, down_came = fence(gather_column(branch_grad), out_part, down_came)
+    branch_all = both_columns(column)
+    att_grad = dot(w_out_own, branch_all, (1, 1)).astype(bf16)
 
     q_grad, kv_own, kv_other, qgain_part = call(
         attend_back_kernel,
@@ -446,48 +513,63 @@
             pltpu.VMEM((2 * wide, ROWS), f32),
         ],
         (half_flag, joint, att_grad, cosine, sine, qgain, att32, lse, q_rot, kt_rot, k_rot, v_nat),
-        20_000_000_000,
-    )
-    down_pieces = sum_x(down_pieces)
-    kv_came, gate_up_pieces, down_pieces = fence(swap(kv_other, "zl"), gate_up_pieces, down_pieces)
-    joint_grad, joint_grad_blocks, kgain_part = call(
+    )
+    out_mine, out_other = call(
+        out_terms_kernel,
+        [((8, held // 8, width), bf16)] * 2,
+        [],
+        (jnp.reshape(hd, (1,)).astype(jnp.int32), att, branch_all),
+    )
+    out_pieces = in_order(out_mine, swap(out_other, "hd"), "hd", 1)
+    out_came = exchange(out_pieces.reshape(16, held // 8, width), SUMMED)
+    kv_other, out_came, gate_up_sum = fence(kv_other, out_came, gate_up_sum)
+    down_mine = sum_x(sum_first(down_came).reshape(4, half_ffn // 8, width))
+    gate_up_came = exchange(gate_up_sum, ("zh", "zl") + TEAM)
+    kv_came = swap(kv_other, "zl")
+    joint_grad, kgain_part = call(
         key_back_kernel,
-        [(joint.shape, bf16), ((team, joint.shape[0], BLOCK), bf16), ((HS, 1), f32)],
+        [(joint.shape, bf16), ((HS, 1), f32)],
         [],
         (joint, kv_own, kv_came, cosine, sine, kgain, q_grad),
-        1_000_000_000,
-    )
-    gate_up_mine = sum_z(gate_up_pieces.reshape(4, 2, RING, few, ffn))
-    came = exchange(joint_grad_blocks)
-    came = jnp.concatenate(
-        [
-            came[:, :key_at].reshape(-1, rows),
-            came[:, key_at:value_at].reshape(-1, rows),
-            came[:, value_at:].reshape(-1, rows),
-        ]
-    )
-    came, gate_up_mine = fence(came, gate_up_mine)
-    gate_up_mine = exchange(gate_up_mine.reshape(team, few, ffn))
-    normed_grad = dot(came, w_joint_all, (0, 1))
-    input_part, norm_gain_part = rms_backward(tokens32, norm_gain, normed_grad)
+    )
+    joint_pieces = call(
+        joint_terms_kernel,
+        [((16 * team, held // 8, joint.shape[0]), bf16)],
+        [],
+        (normed_all, joint_grad),
+    )[0]
+    normed_part = dot(joint_grad, w_joint, (0, 1))
+    norm_gain_part = jnp.sum(normed_part * normed_all.astype(f32), axis=0) / norm_gain
+    chip = chip_sum(normed_part.astype(bf16))
+    chip, joint_pieces, gate_up_came, out_part = fence(chip, joint_pieces, gate_up_came, out_part)
+    joint_came = exchange(joint_pieces, SUMMED + TEAM).reshape(16, team, held // 8, -1)
+    gate_up_mine = sum_first(gate_up_came.reshape(4, team * few, ffn))
+    gate_up_whole = lax.all_gather(gate_up_mine, ("x", "zh"), axis=0, tiled=False)
+    gate_up_whole = gate_up_whole.reshape(RING, 2, team, few, ffn)
+    out_sum = lax.psum_scatter(out_part, TEAM, scatter_dimension=0, tiled=True)
+    output = (middle + out_sum.astype(f32)).astype(bf16)
+    normed_grad = column_sum(chip)
+    input_part, _ = rms_backward(tokens32, norm_gain, normed_grad)
     input_grad = middle_grad + input_part
-
-    branch_all = lax.all_gather(branch_grad, ("y", "hd"), axis=0, tiled=True)
-    out_terms = dot(att, branch_all, (1, 0)).astype(bf16).reshape(2, held, width)
-    out_terms = in_order(at(out_terms, hd), swap(at(out_terms, 1 - hd), "hd"), "hd", 0)
-    out_pieces = out_terms.reshape(2, 2, held // 2, 4, quarter).transpose(3, 1, 0, 2, 4)
-    out_mine = sum_z(sum_x(out_pieces).reshape(4, held // 2, quarter))
-    joint_terms = dot(normed_all, joint_grad, (0, 1)).astype(bf16)
-    joint_pieces = joint_terms.reshape(2, RING, 2, 4, 2, held // 8, -1).transpose(3, 4, 0, 2, 1, 5, 6)
-    joint_mine = sum_z(sum_x(joint_pieces).reshape(4, team, held // 8, -1))
-    joint_mine = exchange(joint_mine)
-
-    w_down_grad = spread(down_pieces).transpose(1, 2, 0, 3).reshape(half_ffn, width).astype(f32)
-    w_out_grad = spread(out_mine).transpose(1, 2, 0, 3).reshape(held, width).astype(f32)
-    gate_up_grad = spread(gate_up_mine).reshape(4, 2, 2, RING, few, 2, half_ffn)
-    gate_up_grad = gate_up_grad.transpose(1, 0, 4, 5, 3, 2, 6).reshape(2, held, -1).astype(f32)
-    w_joint_grad = spread(joint_mine).reshape(team, team, held // 8, -1)
-    w_joint_grad = w_joint_grad.transpose(0, 2, 1, 3).reshape(held, team, -1).astype(f32)
+    joint_came, norm_gain_part = fence(joint_came, norm_gain_part)
+    joint_mine = sum_first(joint_came).reshape(held, -1)
+    joint_mine = jnp.pad(joint_mine, ((0, 0), (0, quarter - joint_mine.shape[1])))
+    ready = jnp.concatenate([down_mine, sum_first(out_came)])
+    ready = [ready[:, i * quarter : (i + 1) * quarter] for i in range(4)]
+    pieces = spread(jnp.concatenate([*ready, joint_mine]))
+    block = lambda shape, index: pl.BlockSpec(shape, index)
+    w_gate_grad, w_up_grad = pl.pallas_call(
+        unpack_ffn_kernel,
+        grid=(RING,),
+        in_specs=[block((1, 2, team, few, ffn), lambda i: (i, 0, 0, 0, 0))],
+        out_specs=[block((few, team * ffn), lambda i: (i, 0))] * 2,
+        out_shape=[jax.ShapeDtypeStruct((held, team * ffn), f32)] * 2,
+        compiler_params=pltpu.CompilerParams(vmem_limit_bytes=40 * 1024 * 1024),
+    )(gate_up_whole)
+    shapes = [(half_ffn, width), (held, width)] + [(held, w.shape[1]) for w in (w_query, w_key, w_value)]
+    w_down_grad, w_out_grad, w_query_grad, w_key_grad, w_value_grad = call(
+        unpack_kernel, [(shape, f32) for shape in shapes], [], (pieces,)
+    )
 
     gains = jnp.concatenate([norm_gain_part, ffn_gain_part, jnp.sum(qgain_part, axis=1), kgain_part[:, 0]])
     gains = sum_everywhere(gains.reshape(-1, BLOCK)).reshape(-1)
@@ -495,15 +577,15 @@
         output[None],
         input_grad[None],
         gains[:width],
-        w_joint_grad[:, :, :key_at].reshape(held, -1),
-        w_joint_grad[:, :, key_at:value_at].reshape(held, -1),
-        w_joint_grad[:, :, value_at:].reshape(held, -1),
+        w_query_grad,
+        w_key_grad,
+        w_value_grad,
         w_out_grad,
         gains[2 * width : 2 * width + HS],
         gains[2 * width + HS :],
         gains[width : 2 * width],
-        gate_up_grad[0],
-        gate_up_grad[1],
+        w_gate_grad,
+        w_up_grad,
         w_down_grad,
     )
 

time: 651 us -> 464 us (0.71)
  local copies, waits for them, and re-layouts: 161 us -> 40.8 us
  waiting for transfers between devices: 195 us -> 165 us
  matrix products: 69.1 us -> 48 us
  other arithmetic: 54.4 us -> 35.1 us
  Pallas kernels: 11.4 us -> 27.2 us
  starting transfers between devices: 133 us -> 123 us
    ppermute x54 -> x32, waiting for transfers between devices: 155 us -> 80.8 us  [ring(): lax.ppermute(array, axis, [(i, (i + step) % RING) for i in range(RING)])]
    dynamic_update_slice x32 -> x9, local copies, waits for them, and re-layouts: 49.3 us -> 4.67 us  [put(): lax.dynamic_update_slice(whole, array.reshape(lead + array.shape), index...]
    all_to_all x6, waiting for transfers between devices: 8.15 us -> 47.4 us  [exchange(): return lax.all_to_all(blocks, axes, split_axis=0, concat_axis=0, tiled=True)]
    reshape x15 -> x1, local copies, waits for them, and re-layouts: 28.1 us -> 3.05 us  [on_device(): gate_up_all.reshape(RING, 2 * team, 2, few, ffn).transpose(2, 1, 0, 3, 4)]
    ppermute x54 -> x32, starting transfers between devices: 92.9 us -> 69 us  [ring(): lax.ppermute(array, axis, [(i, (i + step) % RING) for i in range(RING)])]
    convert_element_type x8 -> x1, local copies, waits for them, and re-layouts: 21.2 us -> 0.02 us  [sum_first(): arrived[i].astype(jnp.float32)]
    dot_general x15 -> x11, matrix products: 69.1 us -> 48 us  [dot(): lax.dot_general(left, right, (((contract[0],), (contract[1],)), ((), ()))...]
    all_to_all x6, starting transfers between devices: 24.6 us -> 40.5 us  [exchange(): return lax.all_to_all(blocks, axes, split_axis=0, concat_axis=0, tiled=True)]
  transfers between devices with their start and end apart: 89 -> 56, of which waited for: 32 -> 31; matrix products, arithmetic and copies ran while one was open for 38% -> 16% of each run, Pallas kernels for 2% -> 4%
where the time goes in v3:
time: 464 us; the launch traced here: 456 us
  waiting for transfers between devices  165 us (36%)
  starting transfers between devices  123 us (27%)
  matrix products  48 us (10%)
  local copies, waits for them, and re-layouts  40.8 us (9%)
  other arithmetic  35.1 us (8%)
  Pallas kernels  27.2 us (6%)
  between operations  16 us (3%)
    ppermute x32, waiting for transfers between devices, ring(): lax.ppermute(array, axis, [(i, (i + step) % RING) for i in range(RING)])  80.8 us
    ppermute x32, starting transfers between devices, ring(): lax.ppermute(array, axis, [(i, (i + step) % RING) for i in range(RING)])  69 us
    dot_general x11, matrix products, dot(): lax.dot_general(left, right, (((contract[0],), (contract[1],)), ((), ()))...  48 us
    all_to_all x6, waiting for transfers between devices, exchange(): return lax.all_to_all(blocks, axes, split_axis=0, concat_axis=0, tiled=True)  47.4 us
    all_to_all x6, starting transfers between devices, exchange(): return lax.all_to_all(blocks, axes, split_axis=0, concat_axis=0, tiled=True)  40.5 us
    ppermute x12, waiting for transfers between devices, swap(): return lax.ppermute(array, axis, [(0, 1), (1, 0)])  35.5 us
    pallas_call x8, Pallas kernels, call(): pl.pallas_call(kernel, out_shape=[jax.ShapeDtypeStruct(shape, dtype) for...  24.3 us
    unnamed x141, local copies, waits for them, and re-layouts  17.5 us
  transfers between devices with their start and end apart: 56, of which 31 were waited for; matrix products, arithmetic and copies ran while one was open for 16% of the time, Pallas kernels for 4%

profile of v3, /device:TPU:0, one launch (start us, length us, event | category | flops | bytes accessed | tf_op | source)
XLA Modules:
  0.0 455.8 jit_solution(12014525799924397945)
XLA Ops:
  13.9 6.0 %all-to-all-start = ((bf16[16,96,320]{2,1,0:T(8,128)(2,1)}), bf16[16,96,320]{2,1,0:T(8,128)(2,1)S(1)}, u32[]{:S(2)}, u32[]{:S(2)}) async-start(bf16[16,96,320]{2,1,0:T(8,128)(2,1)} %pad_maximum_fusion.3), calls=%async_computation | async-start | bytes 2359296 | tf_op jit(solution)/shard_map/all_to_all | solution.py:104
  22.5 22.3 %all-to-all-done = bf16[16,96,320]{2,1,0:T(8,128)(2,1)S(1)} async-done(((bf16[16,96,320]{2,1,0:T(8,128)(2,1)}), bf16[16,96,320]{2,1,0:T(8,128)(2,1)S(1)}, u32[]{:S(2)}, u32[]{:S(2)}) %all-to-all-start) | async-done | bytes 983072 | tf_op jit(solution)/shard_map/all_to_all | solution.py:104
  47.7 6.5 %collective-permute-done.1 = bf16[96,1536]{1,0:T(8,128)(2,1)S(1)} collective-permute-done((bf16[96,1536]{1,0:T(8,128)(2,1)S(1)}, bf16[96,1536]{1,0:T(8,128)(2,1)S(1)}, u32[]{:S(2)}, u32[]{:S(2)}) %collective-permute-start.1) | collective-permute-done | bytes 294944 | tf_op jit(solution)/shard_map/ppermute | solution.py:70
  54.3 5.3 %all-to-all-start.1 = ((bf16[16,48,864]{2,1,0:T(8,128)(2,1)}), bf16[16,48,864]{2,1,0:T(8,128)(2,1)S(1)}, u32[]{:S(2)}, u32[]{:S(2)}) async-start(bf16[16,48,864]{2,1,0:T(8,128)(2,1)} %shard_map.228), calls=%async_computation.1 | async-start | bytes 2752512 | tf_op jit(solution)/shard_map/all_to_all | solution.py:104
  60.2 3.9 convolution_convert_fusion.3.own_ref
  67.0 11.0 %collective-permute-done.other_ref = bf16[128,1024]{1,0:T(8,128)(2,1)S(1)} collective-permute-done((bf16[128,1024]{1,0:T(8,128)(2,1)S(1)}, bf16[128,1024]{1,0:T(8,128)(2,1)S(1)}, u32[]{:S(2)}, u32[]{:S(2)}) %collective-permute-start) | collective-permute-done | bytes 262176 | tf_op jit(solution)/shard_map/ppermute | solution.py:70
  114.1 7.5 %collective-permute-done.5 = bf16[128,1536]{1,0:T(8,128)(2,1)S(1)} collective-permute-done((bf16[128,1536]{1,0:T(8,128)(2,1)}, bf16[128,1536]{1,0:T(8,128)(2,1)S(1)}, u32[]{:S(2)}, u32[]{:S(2)}) %collective-permute-start.5) | collective-permute-done | bytes 393248 | tf_op jit(solution)/shard_map/ppermute | solution.py:62
  137.1 7.6 %collective-permute-done.10 = bf16[128,1536]{1,0:T(8,128)(2,1)S(1)} collective-permute-done((bf16[128,1536]{1,0:T(8,128)(2,1)S(1)}, bf16[128,1536]{1,0:T(8,128)(2,1)S(1)}, u32[]{:S(2)}, u32[]{:S(2)}) %collective-permute-start.10) | collective-permute-done | bytes 393248 | tf_op jit(solution)/shard_map/ppermute | solution.py:62
  147.0 8.0 %fusion.37 = f32[1024,864]{1,0:T(8,128)} fusion(bf16[1024,1536]{1,0:T(8,128)(2,1)} %all-gather.8.cloned.1.call-done, bf16[864,1536]{1,0:T(8,128)(2,1)} %bitcast.234), kind=kOutput, calls=%fused_computation.151 | convolution fusion | flops 2717908992 | bytes 9338880 | tf_op jit(solution)/shard_map/dot_general | solution.py:39
  165.4 5.7 %multiply_convert_fusion = (bf16[1024,864]{1,0:T(8,128)(2,1)}, bf16[1024,864]{1,0:T(8,128)(2,1)S(1)}, bf16[1024,864]{1,0:T(8,128)(2,1)S(1)}) fusion(f32[1024,864]{1,0:T(8,128)S(1)} %fusion.38, f32[1024,864]{1,0:T(8,128)S(1)} %copy-done.68, bf16[1024,1536]{1,0:T(8,128)(2,1)S(1)} %bitcast.215, bf16[1536,864]{1,0:T(8,128)(2,1)S(1)} %bitcast.230), kind=kOutput, calls=%fused_computation.5 | convolution fusion | flops 2732064768 | bytes 18186240 | tf_op jit(solution)/shard_map/dot_general | solution.py:39
  174.6 3.7 add_convert_fusion
  183.9 6.7 %shard_map.230 = bf16[4,32,24,864]{3,2,1,0:T(8,128)(2,1)S(1)} custom-call(bf16[1024,1536]{1,0:T(8,128)(2,1)S(1)} %bitcast.216, bf16[1024,864]{1,0:T(8,128)(2,1)S(1)} %get-tuple-element.65.gate_ref, bf16[1024,864]{1,0:T(8,128)(2,1)S(1)} %get-tuple-element.66.up_ref), custom_call_target="tpu_custom_call" | custom-call | flops 1024 | bytes 1024 | tf_op jit(solution)/shard_map/pallas_call | solution.py:375
  201.7 6.4 %convolution_convert_fusion.2 = bf16[864,1536]{1,0:T(8,128)(2,1)} fusion(bf16[1024,864]{1,0:T(8,128)(2,1)S(1)} %copy-done.66, bf16[1024,1536]{1,0:T(8,128)(2,1)} %all-gather.8.cloned.1.call-done), kind=kOutput, calls=%fused_computation.9 | convolution fusion | flops 2719236096 | bytes 7569408 | tf_op jit(solution)/shard_map/dot_general | solution.py:39
  208.1 8.3 %all-to-all-start.2 = ((bf16[4,216,1536]{2,1,0:T(8,128)(2,1)}), bf16[4,216,1536]{2,1,0:T(8,128)(2,1)S(1)}, u32[]{:S(2)}, u32[]{:S(2)}) async-start(bf16[4,216,1536]{2,1,0:T(8,128)(2,1)} %bitcast.236), calls=%async_computation.2 | async-start | bytes 5308416 | tf_op jit(solution)/shard_map/all_to_all | solution.py:104
  227.2 4.9 %convolution_convert_fusion.1 = bf16[1024,1536]{1,0:T(8,128)(2,1)} fusion(bf16[1024,864]{1,0:T(8,128)(2,1)S(1)} %copy-done.67, bf16[864,1536]{1,0:T(8,128)(2,1)S(1)} %bitcast.235), kind=kOutput, calls=%fused_computation.4 | convolution fusion | flops 2719481856 | bytes 7569408 | tf_op jit(solution)/shard_map/dot_general | solution.py:39
  232.0 3.7 collective-permute-done.17
  237.5 5.5 %collective-permute-done.18 = bf16[128,1536]{1,0:T(8,128)(2,1)} collective-permute-done((bf16[128,1536]{1,0:T(8,128)(2,1)}, bf16[128,1536]{1,0:T(8,128)(2,1)}, u32[]{:S(2)}, u32[]{:S(2)}) %collective-permute-start.18) | collective-permute-done | bytes 393248 | tf_op jit(solution)/shard_map/ppermute | solution.py:62
  247.8 3.6 collective-permute-done.20
  257.5 8.6 %all-to-all-start.3 = ((bf16[16,12,1536]{2,1,0:T(8,128)(2,1)}), bf16[16,12,1536]{2,1,0:T(8,128)(2,1)}, u32[]{:S(2)}, u32[]{:S(2)}) async-start(bf16[16,12,1536]{2,1,0:T(8,128)(2,1)} %bitcast.229), calls=%async_computation.3 | async-start | bytes 1572864 | tf_op jit(solution)/shard_map/all_to_all | solution.py:104
  268.7 6.1 %shard_map.231 = (bf16[192,1024]{1,0:T(8,128)(2,1)S(1)}, f32[128,1024]{1,0:T(8,128)S(1)}, bf16[128,1024]{1,0:T(8,128)(2,1)S(1)}, f32[64,256]{1,0:T(8,128)S(1)}) custom-call(s32[1]{0:T(128)} %bitcast.1.half_ref, bf16[320,1024]{1,0:T(8,128)(2,1)S(1)} %copy-done.2, bf16[192,1024]{1,0:T(8,128)(2,1)S(1)} %convolution_convert_fusion.4.grad_ref, ...), custom_call_target="tpu_custom_call" | custom-call | flops 1024 | bytes 1024 | tf_op jit(solution)/shard_map/pallas_call | solution.py:375
  274.9 6.2 %all-to-all-done.3 = bf16[16,12,1536]{2,1,0:T(8,128)(2,1)} async-done(((bf16[16,12,1536]{2,1,0:T(8,128)(2,1)}), bf16[16,12,1536]{2,1,0:T(8,128)(2,1)}, u32[]{:S(2)}, u32[]{:S(2)}) %all-to-all-start.3) | async-done | bytes 589856 | tf_op jit(solution)/shard_map/all_to_all | solution.py:104
  284.4 6.0 %collective-permute-done.22.kv_came_ref = bf16[128,1024]{1,0:T(8,128)(2,1)S(1)} collective-permute-done((bf16[128,1024]{1,0:T(8,128)(2,1)S(1)}, bf16[128,1024]{1,0:T(8,128)(2,1)S(1)}, u32[]{:S(2)}, u32[]{:S(2)}) %collective-permute-start.22) | collective-permute-done | bytes 262176 | tf_op jit(solution)/shard_map/ppermute | solution.py:70
  290.7 4.0 multiply_reduce_fusion
  297.6 6.0 %all-to-all-start.4 = ((bf16[32,24,864]{2,1,0:T(8,128)(2,1)}), bf16[32,24,864]{2,1,0:T(8,128)(2,1)}, u32[]{:S(2)}, u32[]{:S(2)}) async-start(bf16[32,24,864]{2,1,0:T(8,128)(2,1)} %bitcast.240), calls=%async_computation.5 | async-start | bytes 2752512 | tf_op jit(solution)/shard_map/all_to_all | solution.py:104
  310.9 14.2 %all-to-all-done.4 = bf16[32,24,864]{2,1,0:T(8,128)(2,1)} async-done(((bf16[32,24,864]{2,1,0:T(8,128)(2,1)}), bf16[32,24,864]{2,1,0:T(8,128)(2,1)}, u32[]{:S(2)}, u32[]{:S(2)}) %all-to-all-start.4) | async-done | bytes 1327136 | tf_op jit(solution)/shard_map/all_to_all | solution.py:104
  338.9 3.8 collective-permute-done.38
  342.9 6.4 %all-to-all-start.5 = ((bf16[128,12,320]{2,1,0:T(8,128)(2,1)}), bf16[128,12,320]{2,1,0:T(8,128)(2,1)}, u32[]{:S(2)}, u32[]{:S(2)}) async-start(bf16[128,12,320]{2,1,0:T(8,128)(2,1)} %shard_map.234), calls=%async_computation.7 | async-start | bytes 3145728 | tf_op jit(solution)/shard_map/all_to_all | solution.py:104
  358.2 19.6 %collective-permute-done.24 = bf16[128,1536]{1,0:T(8,128)(2,1)S(1)} collective-permute-done((bf16[128,1536]{1,0:T(8,128)(2,1)}, bf16[128,1536]{1,0:T(8,128)(2,1)S(1)}, u32[]{:S(2)}, u32[]{:S(2)}) %collective-permute-start.24) | collective-permute-done | bytes 393248 | tf_op jit(solution)/shard_map/ppermute | solution.py:62
  377.8 7.3 %collective-permute-done.25 = bf16[128,1536]{1,0:T(8,128)(2,1)S(1)} collective-permute-done((bf16[128,1536]{1,0:T(8,128)(2,1)}, bf16[128,1536]{1,0:T(8,128)(2,1)S(1)}, u32[]{:S(2)}, u32[]{:S(2)}) %collective-permute-start.25) | collective-permute-done | bytes 393248 | tf_op jit(solution)/shard_map/ppermute | solution.py:62
  414.0 10.8 %collective-permute-start.43 = (bf16[2,360,384]{2,1,0:T(8,128)(2,1)S(1)}, bf16[2,360,384]{2,1,0:T(8,128)(2,1)S(1)}, u32[]{:S(2)}, u32[]{:S(2)}) collective-permute-start(bf16[2,360,384]{2,1,0:T(8,128)(2,1)S(1)} %pad_maximum_fusion.7), channel_id=1, source_target_pairs={{0,96},{32,0},{64,32},{96,64},{1,97},{33,1},{65,33},{97,65},{2,98}... | collective-permute-start | bytes 1658888 | tf_op jit(solution)/shard_map/ppermute | solution.py:62
  425.2 3.6 collective-permute-done.41
  428.9 8.6 %collective-permute-done.42 = bf16[2,360,384]{2,1,0:T(8,128)(2,1)S(1)} collective-permute-done((bf16[2,360,384]{2,1,0:T(8,128)(2,1)S(1)}, bf16[2,360,384]{2,1,0:T(8,128)(2,1)S(1)}, u32[]{:S(2)}, u32[]{:S(2)}) %collective-permute-start.42) | collective-permute-done | bytes 552992 | tf_op jit(solution)/shard_map/ppermute | solution.py:62
  (340 shorter events, 201.7 us)
Async XLA Ops:
  7.2 53.0 %all-gather.6.cloned.1.call-start = ((), (), s32[]{:S(2)}) async-start(), calls=%async_computation.8 | async-start | bytes 3538944 | tf_op jit(solution)/shard_map/all_gather | solution.py:428
  13.9 30.9 %all-to-all-start = ((bf16[16,96,320]{2,1,0:T(8,128)(2,1)}), bf16[16,96,320]{2,1,0:T(8,128)(2,1)S(1)}, u32[]{:S(2)}, u32[]{:S(2)}) async-start(bf16[16,96,320]{2,1,0:T(8,128)(2,1)} %pad_maximum_fusion.3), calls=%async_computation | async-start | bytes 2359296 | tf_op jit(solution)/shard_map/all_to_all | solution.py:104
  19.9 127.1 %all-gather.8.cloned.1.call-start = ((), (), s32[]{:S(2)}) async-start(), calls=%async_computation.9 | async-start | bytes 3538944 | tf_op jit(solution)/shard_map/all_gather | solution.py:433
  54.3 33.6 %all-to-all-start.1 = ((bf16[16,48,864]{2,1,0:T(8,128)(2,1)}), bf16[16,48,864]{2,1,0:T(8,128)(2,1)S(1)}, u32[]{:S(2)}, u32[]{:S(2)}) async-start(bf16[16,48,864]{2,1,0:T(8,128)(2,1)} %shard_map.228), calls=%async_computation.1 | async-start | bytes 2752512 | tf_op jit(solution)/shard_map/all_to_all | solution.py:104
  59.5 98.9 %all-gather.12.cloned.1.call-start = ((), (), s32[]{:S(2)}) async-start(), calls=%async_computation.13 | async-start | bytes 6881280 | tf_op jit(solution)/shard_map/all_gather | solution.py:463
  64.2 13.8 %collective-permute-start = (bf16[128,1024]{1,0:T(8,128)(2,1)S(1)}, bf16[128,1024]{1,0:T(8,128)(2,1)S(1)}, u32[]{:S(2)}, u32[]{:S(2)}) collective-permute-start(bf16[128,1024]{1,0:T(8,128)(2,1)S(1)} %slice.226), channel_id=1, source_target_pairs={{0,8},{8,0},{1,9},{9,1},{2,10},{10,2},{3,11},{11,3},{4,12},{12,4},... | collective-permute-start | bytes 786440 | tf_op jit(solution)/shard_map/ppermute | solution.py:70
  94.0 187.1 %reduce-scatter.3.cloned.1.call-start = ((), (), s32[]{:S(2)}) async-start(), calls=%async_computation.10 | async-start | bytes 6881280 | tf_op jit(solution)/shard_map/reduce_scatter | solution.py:487
  100.1 14.0 %collective-permute-start.4 = (bf16[128,1536]{1,0:T(8,128)(2,1)}, bf16[128,1536]{1,0:T(8,128)(2,1)S(1)}, u32[]{:S(2)}, u32[]{:S(2)}) collective-permute-start(bf16[128,1536]{1,0:T(8,128)(2,1)} %get-tuple-element.130), channel_id=1, source_target_pairs={{0,4},{2,6},{4,0},{6,2},{1,5},{3,7},{5,1},{7,3},{8,12},{10,14},{12... | collective-permute-start | bytes 1179656 | tf_op jit(solution)/shard_map/ppermute | solution.py:62
  103.3 18.3 %collective-permute-start.5 = (bf16[128,1536]{1,0:T(8,128)(2,1)}, bf16[128,1536]{1,0:T(8,128)(2,1)S(1)}, u32[]{:S(2)}, u32[]{:S(2)}) collective-permute-start(bf16[128,1536]{1,0:T(8,128)(2,1)} %get-tuple-element.132), channel_id=1, source_target_pairs={{0,2},{2,4},{4,6},{6,0},{1,3},{3,5},{5,7},{7,1},{8,10},{10,12},{12... | collective-permute-start | bytes 1179656 | tf_op jit(solution)/shard_map/ppermute | solution.py:62
  103.6 18.0 %collective-permute-start.6 = (bf16[128,1536]{1,0:T(8,128)(2,1)S(1)}, bf16[128,1536]{1,0:T(8,128)(2,1)}, u32[]{:S(2)}, u32[]{:S(2)}) collective-permute-start(bf16[128,1536]{1,0:T(8,128)(2,1)S(1)} %get-tuple-element.131), channel_id=1, source_target_pairs={{0,6},{2,0},{4,2},{6,4},{1,7},{3,1},{5,3},{7,5},{8,14},{10,8},{12,... | collective-permute-start | bytes 1179656 | tf_op jit(solution)/shard_map/ppermute | solution.py:62
  107.7 21.4 %collective-permute-start.7 = (bf16[216,1536]{1,0:T(8,128)(2,1)}, bf16[216,1536]{1,0:T(8,128)(2,1)}, u32[]{:S(2)}, u32[]{:S(2)}) collective-permute-start(bf16[216,1536]{1,0:T(8,128)(2,1)} %get-tuple-element.134), channel_id=1, source_target_pairs={{0,8},{8,16},{16,24},{24,0},{1,9},{9,17},{17,25},{25,1},{2,10},{10... | collective-permute-start | bytes 1990664 | tf_op jit(solution)/shard_map/ppermute | solution.py:62
  111.1 19.2 %collective-permute-start.8 = (bf16[216,1536]{1,0:T(8,128)(2,1)}, bf16[216,1536]{1,0:T(8,128)(2,1)}, u32[]{:S(2)}, u32[]{:S(2)}) collective-permute-start(bf16[216,1536]{1,0:T(8,128)(2,1)} %get-tuple-element.133), channel_id=1, source_target_pairs={{0,24},{8,0},{16,8},{24,16},{1,25},{9,1},{17,9},{25,17},{2,26},{10... | collective-permute-start | bytes 1990664 | tf_op jit(solution)/shard_map/ppermute | solution.py:62
  123.5 13.5 %collective-permute-start.9 = (bf16[128,1536]{1,0:T(8,128)(2,1)S(1)}, bf16[128,1536]{1,0:T(8,128)(2,1)S(1)}, u32[]{:S(2)}, u32[]{:S(2)}) collective-permute-start(bf16[128,1536]{1,0:T(8,128)(2,1)S(1)} %get-tuple-element.108), channel_id=1, source_target_pairs={{0,4},{2,6},{4,0},{6,2},{1,5},{3,7},{5,1},{7,3},{8,12},{10,14},{12... | collective-permute-start | bytes 1179656 | tf_op jit(solution)/shard_map/ppermute | solution.py:62
  195.4 20.9 %collective-permute-start.14 = (bf16[128,1536]{1,0:T(8,128)(2,1)}, bf16[128,1536]{1,0:T(8,128)(2,1)S(1)}, u32[]{:S(2)}, u32[]{:S(2)}) collective-permute-start(bf16[128,1536]{1,0:T(8,128)(2,1)} %get-tuple-element.127), channel_id=1, source_target_pairs={{0,4},{2,6},{4,0},{6,2},{1,5},{3,7},{5,1},{7,3},{8,12},{10,14},{12... | collective-permute-start | bytes 1179656 | tf_op jit(solution)/shard_map/ppermute | solution.py:62
  198.5 18.4 %collective-permute-start.15 = (bf16[128,1536]{1,0:T(8,128)(2,1)}, bf16[128,1536]{1,0:T(8,128)(2,1)}, u32[]{:S(2)}, u32[]{:S(2)}) collective-permute-start(bf16[128,1536]{1,0:T(8,128)(2,1)} %get-tuple-element.129), channel_id=1, source_target_pairs={{0,2},{2,4},{4,6},{6,0},{1,3},{3,5},{5,7},{7,1},{8,10},{10,12},{12... | collective-permute-start | bytes 1179656 | tf_op jit(solution)/shard_map/ppermute | solution.py:62
  199.0 17.9 %collective-permute-start.16 = (bf16[128,1536]{1,0:T(8,128)(2,1)}, bf16[128,1536]{1,0:T(8,128)(2,1)}, u32[]{:S(2)}, u32[]{:S(2)}) collective-permute-start(bf16[128,1536]{1,0:T(8,128)(2,1)} %get-tuple-element.128), channel_id=1, source_target_pairs={{0,6},{2,0},{4,2},{6,4},{1,7},{3,1},{5,3},{7,5},{8,14},{10,8},{12,... | collective-permute-start | bytes 1179656 | tf_op jit(solution)/shard_map/ppermute | solution.py:62
  208.1 39.5 %all-to-all-start.2 = ((bf16[4,216,1536]{2,1,0:T(8,128)(2,1)}), bf16[4,216,1536]{2,1,0:T(8,128)(2,1)S(1)}, u32[]{:S(2)}, u32[]{:S(2)}) async-start(bf16[4,216,1536]{2,1,0:T(8,128)(2,1)} %bitcast.236), calls=%async_computation.2 | async-start | bytes 5308416 | tf_op jit(solution)/shard_map/all_to_all | solution.py:104
  221.9 13.9 %collective-permute-start.17 = (bf16[128,1536]{1,0:T(8,128)(2,1)}, bf16[128,1536]{1,0:T(8,128)(2,1)}, u32[]{:S(2)}, u32[]{:S(2)}) collective-permute-start(bf16[128,1536]{1,0:T(8,128)(2,1)} %get-tuple-element.106), channel_id=1, source_target_pairs={{0,4},{2,6},{4,0},{6,2},{1,5},{3,7},{5,1},{7,3},{8,12},{10,14},{12... | collective-permute-start | bytes 1179656 | tf_op jit(solution)/shard_map/ppermute | solution.py:62
  223.9 19.1 %collective-permute-start.18 = (bf16[128,1536]{1,0:T(8,128)(2,1)}, bf16[128,1536]{1,0:T(8,128)(2,1)}, u32[]{:S(2)}, u32[]{:S(2)}) collective-permute-start(bf16[128,1536]{1,0:T(8,128)(2,1)} %get-tuple-element.106), channel_id=1, source_target_pairs={{0,2},{2,4},{4,6},{6,0},{1,3},{3,5},{5,7},{7,1},{8,10},{10,12},{12... | collective-permute-start | bytes 1179656 | tf_op jit(solution)/shard_map/ppermute | solution.py:62
  225.4 19.4 %collective-permute-start.19 = (bf16[128,1536]{1,0:T(8,128)(2,1)}, bf16[128,1536]{1,0:T(8,128)(2,1)S(1)}, u32[]{:S(2)}, u32[]{:S(2)}) collective-permute-start(bf16[128,1536]{1,0:T(8,128)(2,1)} %get-tuple-element.106), channel_id=1, source_target_pairs={{0,6},{2,0},{4,2},{6,4},{1,7},{3,1},{5,3},{7,5},{8,14},{10,8},{12,... | collective-permute-start | bytes 1179656 | tf_op jit(solution)/shard_map/ppermute | solution.py:62
  257.5 23.5 %all-to-all-start.3 = ((bf16[16,12,1536]{2,1,0:T(8,128)(2,1)}), bf16[16,12,1536]{2,1,0:T(8,128)(2,1)}, u32[]{:S(2)}, u32[]{:S(2)}) async-start(bf16[16,12,1536]{2,1,0:T(8,128)(2,1)} %bitcast.229), calls=%async_computation.3 | async-start | bytes 1572864 | tf_op jit(solution)/shard_map/all_to_all | solution.py:104
  297.6 27.6 %all-to-all-start.4 = ((bf16[32,24,864]{2,1,0:T(8,128)(2,1)}), bf16[32,24,864]{2,1,0:T(8,128)(2,1)}, u32[]{:S(2)}, u32[]{:S(2)}) async-start(bf16[32,24,864]{2,1,0:T(8,128)(2,1)} %bitcast.240), calls=%async_computation.5 | async-start | bytes 2752512 | tf_op jit(solution)/shard_map/all_to_all | solution.py:104
  303.6 137.4 %all-gather.10.cloned.1.call-start = ((), (), s32[]{:S(2)}) async-start(), calls=%async_computation.12 | async-start | bytes 3096576 | tf_op jit(solution)/shard_map/all_gather | solution.py:547
  327.4 118.3 %reduce-scatter.5.cloned.1.call-start = ((), (), s32[]{:S(2)}) async-start(), calls=%async_computation.11 | async-start | bytes 3538944 | tf_op jit(solution)/shard_map/reduce_scatter | solution.py:549
  342.9 42.6 %all-to-all-start.5 = ((bf16[128,12,320]{2,1,0:T(8,128)(2,1)}), bf16[128,12,320]{2,1,0:T(8,128)(2,1)}, u32[]{:S(2)}, u32[]{:S(2)}) async-start(bf16[128,12,320]{2,1,0:T(8,128)(2,1)} %shard_map.234), calls=%async_computation.7 | async-start | bytes 3145728 | tf_op jit(solution)/shard_map/all_to_all | solution.py:104
  350.4 27.4 %collective-permute-start.24 = (bf16[128,1536]{1,0:T(8,128)(2,1)}, bf16[128,1536]{1,0:T(8,128)(2,1)S(1)}, u32[]{:S(2)}, u32[]{:S(2)}) collective-permute-start(bf16[128,1536]{1,0:T(8,128)(2,1)} %get-tuple-element.124), channel_id=1, source_target_pairs={{0,4},{2,6},{4,0},{6,2},{1,5},{3,7},{5,1},{7,3},{8,12},{10,14},{12... | collective-permute-start | bytes 1179656 | tf_op jit(solution)/shard_map/ppermute | solution.py:62
  352.8 32.3 %collective-permute-start.25 = (bf16[128,1536]{1,0:T(8,128)(2,1)}, bf16[128,1536]{1,0:T(8,128)(2,1)S(1)}, u32[]{:S(2)}, u32[]{:S(2)}) collective-permute-start(bf16[128,1536]{1,0:T(8,128)(2,1)} %get-tuple-element.126), channel_id=1, source_target_pairs={{0,2},{2,4},{4,6},{6,0},{1,3},{3,5},{5,7},{7,1},{8,10},{10,12},{12... | collective-permute-start | bytes 1179656 | tf_op jit(solution)/shard_map/ppermute | solution.py:62
  353.4 31.7 %collective-permute-start.26 = (bf16[128,1536]{1,0:T(8,128)(2,1)}, bf16[128,1536]{1,0:T(8,128)(2,1)S(1)}, u32[]{:S(2)}, u32[]{:S(2)}) collective-permute-start(bf16[128,1536]{1,0:T(8,128)(2,1)} %get-tuple-element.125), channel_id=1, source_target_pairs={{0,6},{2,0},{4,2},{6,4},{1,7},{3,1},{5,3},{7,5},{8,14},{10,8},{12,... | collective-permute-start | bytes 1179656 | tf_op jit(solution)/shard_map/ppermute | solution.py:62
  394.0 17.6 %collective-permute-start.40 = (bf16[360,384]{1,0:T(8,128)(2,1)S(1)}, bf16[360,384]{1,0:T(8,128)(2,1)S(1)}, u32[]{:S(2)}, u32[]{:S(2)}) collective-permute-start(bf16[360,384]{1,0:T(8,128)(2,1)S(1)} %concatenate.23), channel_id=1, source_target_pairs={{0,16},{16,0},{1,17},{17,1},{2,18},{18,2},{3,19},{19,3},{4,20},{20... | collective-permute-start | bytes 829448 | tf_op jit(solution)/shard_map/ppermute | solution.py:70
  411.7 17.1 %collective-permute-start.41 = (bf16[2,360,384]{2,1,0:T(8,128)(2,1)S(1)}, bf16[2,360,384]{2,1,0:T(8,128)(2,1)S(1)}, u32[]{:S(2)}, u32[]{:S(2)}) collective-permute-start(bf16[2,360,384]{2,1,0:T(8,128)(2,1)S(1)} %pad_maximum_fusion.7), channel_id=1, source_target_pairs={{0,64},{32,96},{64,0},{96,32},{1,65},{33,97},{65,1},{97,33},{2,66}... | collective-permute-start | bytes 1658888 | tf_op jit(solution)/shard_map/ppermute | solution.py:62
  413.3 24.2 %collective-permute-start.42 = (bf16[2,360,384]{2,1,0:T(8,128)(2,1)S(1)}, bf16[2,360,384]{2,1,0:T(8,128)(2,1)S(1)}, u32[]{:S(2)}, u32[]{:S(2)}) collective-permute-start(bf16[2,360,384]{2,1,0:T(8,128)(2,1)S(1)} %pad_maximum_fusion.7), channel_id=1, source_target_pairs={{0,32},{32,64},{64,96},{96,0},{1,33},{33,65},{65,97},{97,1},{2,34}... | collective-permute-start | bytes 1658888 | tf_op jit(solution)/shard_map/ppermute | solution.py:62
  414.0 23.6 %collective-permute-start.43 = (bf16[2,360,384]{2,1,0:T(8,128)(2,1)S(1)}, bf16[2,360,384]{2,1,0:T(8,128)(2,1)S(1)}, u32[]{:S(2)}, u32[]{:S(2)}) collective-permute-start(bf16[2,360,384]{2,1,0:T(8,128)(2,1)S(1)} %pad_maximum_fusion.7), channel_id=1, source_target_pairs={{0,96},{32,0},{64,32},{96,64},{1,97},{33,1},{65,33},{97,65},{2,98}... | collective-permute-start | bytes 1658888 | tf_op jit(solution)/shard_map/ppermute | solution.py:62
  (93 other events, 889.5 us)
Sparse Core Ops, SparseCore 0:
  10.5 40.6 all-gather.5
  52.9 39.9 all-gather.7
  95.1 63.2 all-gather.11
  193.1 62.2 reduce-scatter.2
  327.5 67.6 all-gather.9
  397.5 32.8 reduce-scatter.4

commit v4 on v3

--- a/solution.py
+++ b/solution.py
@@ -114,21 +114,15 @@
     return sum(arrived[i].astype(jnp.float32) for i in range(len(arrived))).astype(jnp.bfloat16)
 
 
-def spread(piece):
+def spread(piece, *beside):
     x = lax.axis_index("x")
     pair = in_order(piece, swap(piece, "zh"), "zh", 0)
+    far, after, before = [ring(pair, "x", step) for step in STEPS]
+    far, *beside = fence(far, *beside)
     whole = put(jnp.zeros((RING, *pair.shape), pair.dtype), pair, x)
-    for step in STEPS:
-        whole = put(whole, ring(pair, "x", step), (x - step) % RING)
-    return whole
-
-
-def sum_everywhere(terms):
-    terms = terms + swap(terms, "hd")
-    for axis in ("y", ("zh", "zl"), "x"):
-        far, after, before = [ring(terms, axis, step) for step in STEPS]
-        terms = (terms + far) + (after + before)
-    return terms
+    for step, block in zip(STEPS, (far, after, before)):
+        whole = put(whole, block, (x - step) % RING)
+    return whole, beside
 
 
 def turn(values, cosine, sine):
@@ -325,15 +319,36 @@
                 other_ref[piece] = block
 
 
-def joint_terms_kernel(normed_ref, grad_ref, out_ref):
-    few = out_ref.shape[1]
+def joint_terms_kernel(normed_ref, grad_ref, gains_ref, out_ref):
     team, half = 2 * RING, normed_ref.shape[1] // 2
+    few = half // (8 * team)
     for zl in range(2):
         terms = dot(normed_ref[:, zl * half : (zl + 1) * half], grad_ref[...], (0, 1))
         for place in range(team):
             for piece in range(8):
                 start = (place * 8 + piece) * few
-                out_ref[(piece * 2 + zl) * team + place] = terms[start : start + few].astype(jnp.bfloat16)
+                block = jnp.concatenate([terms[start : start + few], gains_ref[piece]], axis=0)
+                out_ref[(piece * 2 + zl) * team + place] = block.astype(jnp.bfloat16)
+
+
+def joint_sum_kernel(came_ref, out_ref):
+    count, rows, cols = came_ref.shape
+    team = 2 * RING
+    few = rows - 4
+    gains = jnp.zeros((4, cols), jnp.float32)
+    parts = []
+    for place in range(team):
+        total = came_ref[place].astype(jnp.float32)
+        for source in range(1, count // team):
+            total = total + came_ref[source * team + place].astype(jnp.float32)
+        parts.append(total[:few])
+        gains = gains + total[few:]
+    gains = gains[:2] + gains[2:]
+    high = gains.astype(jnp.bfloat16).astype(jnp.float32)
+    parts += [high, gains - high, jnp.zeros((4, cols), jnp.float32)]
+    whole = jnp.concatenate(parts, axis=0)
+    spare = jnp.zeros((whole.shape[0], out_ref.shape[1] - cols), jnp.float32)
+    out_ref[...] = jnp.concatenate([whole, spare], axis=1).astype(jnp.bfloat16)
 
 
 def unpack_ffn_kernel(pieces_ref, gate_ref, up_ref):
@@ -346,8 +361,8 @@
         )
 
 
-def unpack_kernel(pieces_ref, w_down_ref, w_out_ref, w_query_ref, w_key_ref, w_value_ref):
-    team, cols = 2 * RING, pieces_ref.shape[3]
+def unpack_kernel(pieces_ref, w_down_ref, w_out_ref, w_query_ref, w_key_ref, w_value_ref, gains_ref):
+    team, cols = 2 * RING, gains_ref.shape[2]
     down, out, few = w_down_ref.shape[0] // 8, w_out_ref.shape[0] // 8, w_query_ref.shape[0] // 8
     rows = down + out
     down_rows, out_rows, joint_rows = [], [], []
@@ -359,6 +374,8 @@
             out_rows.append(ready[down:])
             heads = [RING * rows + place_of(head) * few for head in range(team)]
             joint_rows.append([piece[start : start + few] for start in heads])
+            gains = piece[RING * rows + team * few :, :cols]
+            gains_ref[x * 2 + zh] = gains[:2] + gains[2:4]
     w_down_ref[...] = jnp.concatenate([down_rows[x * 2 + zh] for zh in range(2) for x in range(RING)], axis=0)
     w_out_ref[...] = jnp.concatenate(out_rows, axis=0)
     targets = (w_query_ref, 0, GROUP * HS), (w_key_ref, GROUP * HS, HS), (w_value_ref, (GROUP + 1) * HS, HS)
@@ -428,14 +445,14 @@
     normed_all = lax.all_gather(normed, TEAM, axis=0, tiled=True)
     my_rows = lambda w: lax.dynamic_slice_in_dim(w, lax.axis_index("x") * few, few, 0)
     gate_up_rows = call(pack_kernel, [((2 * team, 2 * few, ffn), bf16)], [], (my_rows(w_gate), my_rows(w_up)))[0]
-    w_joint, gate_up_rows, grad_in = fence(w_joint, gate_up_rows, out_grad)
+    out_rows = in_order(w_out, swap(w_out, "zl"), "zl", 0)
+    w_out_own = in_order(at(out_rows, hd), swap(at(out_rows, 1 - hd), "hd"), "hd", 0).reshape(heads_width, width)
+    w_joint, w_out_own, gate_up_rows, grad_in = fence(w_joint, w_out_own, gate_up_rows, out_grad)
     w_joint = w_joint.reshape(width, -1)
     grad_all = lax.all_gather(grad_in, TEAM, axis=0, tiled=True)
     gate_up_rows = exchange(gate_up_rows, ("zl", "y", "hd"))
     down_other = jnp.concatenate([ring_z(w_down[: half_ffn // 2], 1), ring_z(w_down[half_ffn // 2 :], 3)])
     w_down_own = in_order(w_down, down_other, "zl", 0).reshape(ffn, width)
-    out_rows = in_order(w_out, swap(w_out, "zl"), "zl", 0)
-    w_out_own = in_order(at(out_rows, hd), swap(at(out_rows, 1 - hd), "hd"), "hd", 0).reshape(heads_width, width)
 
     joint = dot(w_joint, normed_all, (0, 1)).astype(bf16)
     other_kv = swap(joint[heads_width:], "zl")
@@ -494,9 +511,19 @@
     branch_grad = middle_grad.astype(bf16)
     out_part = dot(hidden_last, w_down_own, (1, 0)).astype(bf16)
     column, out_part, down_came = fence(gather_column(branch_grad), out_part, down_came)
+    out_sum = lax.psum_scatter(out_part, TEAM, scatter_dimension=0, tiled=True)
     branch_all = both_columns(column)
     att_grad = dot(w_out_own, branch_all, (1, 1)).astype(bf16)
 
+    out_mine, out_other = call(
+        out_terms_kernel,
+        [((8, held // 8, width), bf16)] * 2,
+        [],
+        (jnp.reshape(hd, (1,)).astype(jnp.int32), att, branch_all),
+    )
+    out_pieces = in_order(out_mine, swap(out_other, "hd"), "hd", 1)
+    att_grad, out_pieces = fence(att_grad, out_pieces)
+    out_came = exchange(out_pieces.reshape(16, held // 8, width), SUMMED)
     q_grad, kv_own, kv_other, qgain_part = call(
         attend_back_kernel,
         [
@@ -514,49 +541,44 @@
         ],
         (half_flag, joint, att_grad, cosine, sine, qgain, att32, lse, q_rot, kt_rot, k_rot, v_nat),
     )
-    out_mine, out_other = call(
-        out_terms_kernel,
-        [((8, held // 8, width), bf16)] * 2,
-        [],
-        (jnp.reshape(hd, (1,)).astype(jnp.int32), att, branch_all),
-    )
-    out_pieces = in_order(out_mine, swap(out_other, "hd"), "hd", 1)
-    out_came = exchange(out_pieces.reshape(16, held // 8, width), SUMMED)
-    kv_other, out_came, gate_up_sum = fence(kv_other, out_came, gate_up_sum)
-    down_mine = sum_x(sum_first(down_came).reshape(4, half_ffn // 8, width))
     gate_up_came = exchange(gate_up_sum, ("zh", "zl") + TEAM)
-    kv_came = swap(kv_other, "zl")
+    kv_came, gate_up_came, att, down_came = fence(swap(kv_other, "zl"), gate_up_came, att, down_came)
     joint_grad, kgain_part = call(
         key_back_kernel,
         [(joint.shape, bf16), ((HS, 1), f32)],
         [],
         (joint, kv_own, kv_came, cosine, sine, kgain, q_grad),
     )
+    normed_part = dot(joint_grad, w_joint, (0, 1))
+    norm_gain_part = jnp.sum(normed_part * normed_all.astype(f32), axis=0) / norm_gain
+    normed_part = normed_part.astype(bf16)
+    gains = [norm_gain_part, ffn_gain_part, jnp.sum(qgain_part, axis=1), kgain_part[:, 0]]
+    joint_width = joint.shape[0]
+    gains = jnp.concatenate([*gains, jnp.zeros((16 * joint_width - 2 * width - 2 * HS,), f32)])
+    gains = gains.reshape(8, 2, joint_width)
+    high = lax.optimization_barrier(gains.astype(bf16)).astype(f32)
     joint_pieces = call(
         joint_terms_kernel,
-        [((16 * team, held // 8, joint.shape[0]), bf16)],
+        [((16 * team, held // 8 + 4, joint_width), bf16)],
         [],
-        (normed_all, joint_grad),
+        (normed_all, joint_grad, jnp.concatenate([high, gains - high], axis=1)),
     )[0]
-    normed_part = dot(joint_grad, w_joint, (0, 1))
-    norm_gain_part = jnp.sum(normed_part * normed_all.astype(f32), axis=0) / norm_gain
-    chip = chip_sum(normed_part.astype(bf16))
-    chip, joint_pieces, gate_up_came, out_part = fence(chip, joint_pieces, gate_up_came, out_part)
-    joint_came = exchange(joint_pieces, SUMMED + TEAM).reshape(16, team, held // 8, -1)
+    joint_pieces, gate_up_came, out_came, normed_part, down_came = fence(
+        joint_pieces, gate_up_came, out_came, normed_part, down_came
+    )
+    joint_came = exchange(joint_pieces, SUMMED + TEAM)
     gate_up_mine = sum_first(gate_up_came.reshape(4, team * few, ffn))
     gate_up_whole = lax.all_gather(gate_up_mine, ("x", "zh"), axis=0, tiled=False)
     gate_up_whole = gate_up_whole.reshape(RING, 2, team, few, ffn)
-    out_sum = lax.psum_scatter(out_part, TEAM, scatter_dimension=0, tiled=True)
+    down_mine = sum_x(sum_first(down_came).reshape(4, half_ffn // 8, width))
+    ready = jnp.concatenate([down_mine, sum_first(out_came)])
+    ready = jnp.concatenate([ready[:, i * quarter : (i + 1) * quarter] for i in range(4)])
+    joint_came, ready, chip = fence(joint_came, ready, chip_sum(normed_part))
+    joint_mine = call(joint_sum_kernel, [((held + 8, quarter), bf16)], [], (joint_came,))[0]
+    pieces, (normed_grad,) = spread(jnp.concatenate([ready, joint_mine]), column_sum(chip))
     output = (middle + out_sum.astype(f32)).astype(bf16)
-    normed_grad = column_sum(chip)
     input_part, _ = rms_backward(tokens32, norm_gain, normed_grad)
     input_grad = middle_grad + input_part
-    joint_came, norm_gain_part = fence(joint_came, norm_gain_part)
-    joint_mine = sum_first(joint_came).reshape(held, -1)
-    joint_mine = jnp.pad(joint_mine, ((0, 0), (0, quarter - joint_mine.shape[1])))
-    ready = jnp.concatenate([down_mine, sum_first(out_came)])
-    ready = [ready[:, i * quarter : (i + 1) * quarter] for i in range(4)]
-    pieces = spread(jnp.concatenate([*ready, joint_mine]))
     block = lambda shape, index: pl.BlockSpec(shape, index)
     w_gate_grad, w_up_grad = pl.pallas_call(
         unpack_ffn_kernel,
@@ -567,12 +589,12 @@
         compiler_params=pltpu.CompilerParams(vmem_limit_bytes=40 * 1024 * 1024),
     )(gate_up_whole)
     shapes = [(half_ffn, width), (held, width)] + [(held, w.shape[1]) for w in (w_query, w_key, w_value)]
-    w_down_grad, w_out_grad, w_query_grad, w_key_grad, w_value_grad = call(
+    shapes.append((8, 2, joint_width))
+    w_down_grad, w_out_grad, w_query_grad, w_key_grad, w_value_grad, gains = call(
         unpack_kernel, [(shape, f32) for shape in shapes], [], (pieces,)
     )
 
-    gains = jnp.concatenate([norm_gain_part, ffn_gain_part, jnp.sum(qgain_part, axis=1), kgain_part[:, 0]])
-    gains = sum_everywhere(gains.reshape(-1, BLOCK)).reshape(-1)
+    gains = gains.reshape(-1)
     return (
         output[None],
         input_grad[None],
@@ -582,7 +604,7 @@
         w_value_grad,
         w_out_grad,
         gains[2 * width : 2 * width + HS],
-        gains[2 * width + HS :],
+        gains[2 * width + HS : 2 * width + 2 * HS],
         gains[width : 2 * width],
         w_gate_grad,
         w_up_grad,

time: 464 us -> 419 us (0.903)
  the two profiles are of different devices: /device:TPU:0 before, /device:TPU:1 now
where the time goes in v4:
time: 419 us; the launch traced here: 412 us
  waiting for transfers between devices  154 us (37%)
  starting transfers between devices  94.9 us (23%)
  matrix products  49.8 us (12%)
  local copies, waits for them, and re-layouts  36.8 us (9%)
  other arithmetic  31.6 us (8%)
  Pallas kernels  28.1 us (7%)
  between operations  15.8 us (4%)
    ppermute x23, waiting for transfers between devices, ring(): lax.ppermute(array, axis, [(i, (i + step) % RING) for i in range(RING)])  70.4 us
    all_to_all x6, waiting for transfers between devices, exchange(): return lax.all_to_all(blocks, axes, split_axis=0, concat_axis=0, tiled=True)  53.8 us
    dot_general x11, matrix products, dot(): lax.dot_general(left, right, (((contract[0],), (contract[1],)), ((), ()))...  49.8 us
    ppermute x23, starting transfers between devices, ring(): lax.ppermute(array, axis, [(i, (i + step) % RING) for i in range(RING)])  39.1 us
    all_to_all x6, starting transfers between devices, exchange(): return lax.all_to_all(blocks, axes, split_axis=0, concat_axis=0, tiled=True)  35.2 us
    ppermute x11, waiting for transfers between devices, swap(): return lax.ppermute(array, axis, [(0, 1), (1, 0)])  28.9 us
    pallas_call x9, Pallas kernels, call(): pl.pallas_call(kernel, out_shape=[jax.ShapeDtypeStruct(shape, dtype) for...  25.2 us
    ppermute x11, starting transfers between devices, swap(): return lax.ppermute(array, axis, [(0, 1), (1, 0)])  20.4 us
  transfers between devices with their start and end apart: 46, of which 22 were waited for; matrix products, arithmetic and copies ran while one was open for 19% of the time, Pallas kernels for 4%

profile of v4, /device:TPU:1, one launch (start us, length us, event | category | flops | bytes accessed | tf_op | source)
XLA Modules:
  0.0 411.6 jit_solution(16470814474550575797)
XLA Ops:
  16.5 5.4 %all-to-all-start = ((bf16[16,96,320]{2,1,0:T(8,128)(2,1)}), bf16[16,96,320]{2,1,0:T(8,128)(2,1)S(1)}, u32[]{:S(2)}, u32[]{:S(2)}) async-start(bf16[16,96,320]{2,1,0:T(8,128)(2,1)} %pad_maximum_fusion.3), calls=%async_computation | async-start | bytes 2359296 | tf_op jit(solution)/shard_map/all_to_all | solution.py:104
  25.1 23.6 %all-to-all-done = bf16[16,96,320]{2,1,0:T(8,128)(2,1)S(1)} async-done(((bf16[16,96,320]{2,1,0:T(8,128)(2,1)}), bf16[16,96,320]{2,1,0:T(8,128)(2,1)S(1)}, u32[]{:S(2)}, u32[]{:S(2)}) %all-to-all-start) | async-done | bytes 983072 | tf_op jit(solution)/shard_map/all_to_all | solution.py:104
  49.7 5.1 %all-to-all-start.1 = ((bf16[16,48,864]{2,1,0:T(8,128)(2,1)}), bf16[16,48,864]{2,1,0:T(8,128)(2,1)S(1)}, u32[]{:S(2)}, u32[]{:S(2)}) async-start(bf16[16,48,864]{2,1,0:T(8,128)(2,1)} %shard_map.228), calls=%async_computation.1 | async-start | bytes 2752512 | tf_op jit(solution)/shard_map/all_to_all | solution.py:104
  54.9 3.8 convolution_convert_fusion.3.own_ref
  61.4 16.0 %collective-permute-done.2.other_ref = bf16[128,1024]{1,0:T(8,128)(2,1)S(1)} collective-permute-done((bf16[128,1024]{1,0:T(8,128)(2,1)S(1)}, bf16[128,1024]{1,0:T(8,128)(2,1)S(1)}, u32[]{:S(2)}, u32[]{:S(2)}) %collective-permute-start.2) | collective-permute-done | bytes 262176 | tf_op jit(solution)/shard_map/ppermute | solution.py:70
  104.1 4.3 %collective-permute-start.7 = (bf16[216,1536]{1,0:T(8,128)(2,1)}, bf16[216,1536]{1,0:T(8,128)(2,1)S(1)}, u32[]{:S(2)}, u32[]{:S(2)}) collective-permute-start(bf16[216,1536]{1,0:T(8,128)(2,1)} %get-tuple-element.150), channel_id=1, source_target_pairs={{0,8},{8,16},{16,24},{24,0},{1,9},{9,17},{17,25},{25,1},{2,10},{10... | collective-permute-start | bytes 1990664 | tf_op jit(solution)/shard_map/ppermute | solution.py:62
  111.3 7.6 %collective-permute-done.5 = bf16[128,1536]{1,0:T(8,128)(2,1)} collective-permute-done((bf16[128,1536]{1,0:T(8,128)(2,1)}, bf16[128,1536]{1,0:T(8,128)(2,1)}, u32[]{:S(2)}, u32[]{:S(2)}) %collective-permute-start.5) | collective-permute-done | bytes 393248 | tf_op jit(solution)/shard_map/ppermute | solution.py:62
  121.9 3.7 collective-permute-done.7
  132.4 9.1 %collective-permute-done.10 = bf16[128,1536]{1,0:T(8,128)(2,1)S(1)} collective-permute-done((bf16[128,1536]{1,0:T(8,128)(2,1)S(1)}, bf16[128,1536]{1,0:T(8,128)(2,1)S(1)}, u32[]{:S(2)}, u32[]{:S(2)}) %collective-permute-start.10) | collective-permute-done | bytes 393248 | tf_op jit(solution)/shard_map/ppermute | solution.py:62
  144.7 7.9 %fusion.39 = f32[1024,864]{1,0:T(8,128)} fusion(bf16[1024,1536]{1,0:T(8,128)(2,1)} %all-gather.8.cloned.1.call-done, bf16[864,1536]{1,0:T(8,128)(2,1)} %bitcast.221), kind=kOutput, calls=%fused_computation.147 | convolution fusion | flops 2717908992 | bytes 9338880 | tf_op jit(solution)/shard_map/dot_general | solution.py:39
  158.9 3.4 fusion.40
  162.3 5.7 %multiply_convert_fusion = (bf16[1024,864]{1,0:T(8,128)(2,1)}, bf16[1024,864]{1,0:T(8,128)(2,1)S(1)}, bf16[1024,864]{1,0:T(8,128)(2,1)S(1)}) fusion(f32[1024,864]{1,0:T(8,128)S(1)} %fusion.40, f32[1024,864]{1,0:T(8,128)S(1)} %copy-done.62, bf16[1024,1536]{1,0:T(8,128)(2,1)S(1)} %bitcast.204, bf16[1536,864]{1,0:T(8,128)(2,1)S(1)} %bitcast.217), kind=kOutput, calls=%fused_computation.5 | convolution fusion | flops 2732064768 | bytes 18186240 | tf_op jit(solution)/shard_map/dot_general | solution.py:39
  168.1 3.5 fusion.41
  171.5 3.7 add_convert_fusion
  181.2 6.7 %shard_map.230 = bf16[4,32,24,864]{3,2,1,0:T(8,128)(2,1)S(1)} custom-call(bf16[1024,1536]{1,0:T(8,128)(2,1)S(1)} %bitcast.205, bf16[1024,864]{1,0:T(8,128)(2,1)S(1)} %get-tuple-element.74.gate_ref, bf16[1024,864]{1,0:T(8,128)(2,1)S(1)} %get-tuple-element.75.up_ref), custom_call_target="tpu_custom_call" | custom-call | flops 1024 | bytes 1024 | tf_op jit(solution)/shard_map/pallas_call | solution.py:392
  198.1 6.4 %convolution_convert_fusion.2 = bf16[864,1536]{1,0:T(8,128)(2,1)} fusion(bf16[1024,864]{1,0:T(8,128)(2,1)S(1)} %copy-done.60, bf16[1024,1536]{1,0:T(8,128)(2,1)} %all-gather.8.cloned.1.call-done), kind=kOutput, calls=%fused_computation.9 | convolution fusion | flops 2719236096 | bytes 7569408 | tf_op jit(solution)/shard_map/dot_general | solution.py:39
  204.5 6.6 %all-to-all-start.2 = ((bf16[4,216,1536]{2,1,0:T(8,128)(2,1)}), bf16[4,216,1536]{2,1,0:T(8,128)(2,1)}, u32[]{:S(2)}, u32[]{:S(2)}) async-start(bf16[4,216,1536]{2,1,0:T(8,128)(2,1)} %bitcast.223), calls=%async_computation.2 | async-start | bytes 5308416 | tf_op jit(solution)/shard_map/all_to_all | solution.py:104
  221.5 4.8 %convolution_convert_fusion.1 = bf16[1024,1536]{1,0:T(8,128)(2,1)} fusion(bf16[1024,864]{1,0:T(8,128)(2,1)S(1)} %copy-done.61, bf16[864,1536]{1,0:T(8,128)(2,1)S(1)} %bitcast.222), kind=kOutput, calls=%fused_computation.4 | convolution fusion | flops 2719481856 | bytes 7569408 | tf_op jit(solution)/shard_map/dot_general | solution.py:39
  229.8 9.3 %collective-permute-done.18 = bf16[128,1536]{1,0:T(8,128)(2,1)S(1)} collective-permute-done((bf16[128,1536]{1,0:T(8,128)(2,1)}, bf16[128,1536]{1,0:T(8,128)(2,1)S(1)}, u32[]{:S(2)}, u32[]{:S(2)}) %collective-permute-start.18) | collective-permute-done | bytes 393248 | tf_op jit(solution)/shard_map/ppermute | solution.py:62
  239.1 4.8 %all-to-all-done.2 = bf16[4,216,1536]{2,1,0:T(8,128)(2,1)} async-done(((bf16[4,216,1536]{2,1,0:T(8,128)(2,1)}), bf16[4,216,1536]{2,1,0:T(8,128)(2,1)}, u32[]{:S(2)}, u32[]{:S(2)}) %all-to-all-start.2) | async-done | bytes 2654240 | tf_op jit(solution)/shard_map/all_to_all | solution.py:104
  251.9 7.7 %all-to-all-start.3 = ((bf16[32,24,864]{2,1,0:T(8,128)(2,1)}), bf16[32,24,864]{2,1,0:T(8,128)(2,1)}, u32[]{:S(2)}, u32[]{:S(2)}) async-start(bf16[32,24,864]{2,1,0:T(8,128)(2,1)} %bitcast.227), calls=%async_computation.5 | async-start | bytes 2752512 | tf_op jit(solution)/shard_map/all_to_all | solution.py:104
  264.0 6.1 %shard_map.232 = (bf16[192,1024]{1,0:T(8,128)(2,1)S(1)}, f32[128,1024]{1,0:T(8,128)S(1)}, bf16[128,1024]{1,0:T(8,128)(2,1)S(1)}, f32[64,256]{1,0:T(8,128)S(1)}) custom-call(s32[1]{0:T(128)} %bitcast.1.half_ref, bf16[320,1024]{1,0:T(8,128)(2,1)S(1)} %copy-done.2, bf16[192,1024]{1,0:T(8,128)(2,1)S(1)} %convolution_convert_fusion.4.grad_ref, ...), custom_call_target="tpu_custom_call" | custom-call | flops 1024 | bytes 1024 | tf_op jit(solution)/shard_map/pallas_call | solution.py:392
  270.1 9.0 %collective-permute-start.22 = (bf16[128,1024]{1,0:T(8,128)(2,1)S(1)}, bf16[128,1024]{1,0:T(8,128)(2,1)S(1)}, u32[]{:S(2)}, u32[]{:S(2)}) collective-permute-start(bf16[128,1024]{1,0:T(8,128)(2,1)S(1)} %get-tuple-element.91), channel_id=1, source_target_pairs={{0,8},{8,0},{1,9},{9,1},{2,10},{10,2},{3,11},{11,3},{4,12},{12,4},... | collective-permute-start | bytes 786440 | tf_op jit(solution)/shard_map/ppermute | solution.py:70
  280.2 4.8 %all-to-all-done.3 = bf16[32,24,864]{2,1,0:T(8,128)(2,1)} async-done(((bf16[32,24,864]{2,1,0:T(8,128)(2,1)}), bf16[32,24,864]{2,1,0:T(8,128)(2,1)}, u32[]{:S(2)}, u32[]{:S(2)}) %all-to-all-start.3) | async-done | bytes 1327136 | tf_op jit(solution)/shard_map/all_to_all | solution.py:104
  284.9 4.5 %all-to-all-start.4 = ((bf16[16,12,1536]{2,1,0:T(8,128)(2,1)}), bf16[16,12,1536]{2,1,0:T(8,128)(2,1)}, u32[]{:S(2)}, u32[]{:S(2)}) async-start(bf16[16,12,1536]{2,1,0:T(8,128)(2,1)} %bitcast.216), calls=%async_computation.6 | async-start | bytes 1572864 | tf_op jit(solution)/shard_map/all_to_all | solution.py:104
  291.0 5.6 %fusion.34 = (bf16[1024,1536]{1,0:T(8,128)(2,1)}, f32[1536]{0:T(1024)S(1)}) fusion(bf16[1024,1536]{1,0:T(8,128)(2,1)} %all-gather.6.cloned.1.call-done.normed_ref, bf16[320,1024]{1,0:T(8,128)(2,1)S(1)} %get-tuple-element.95.grad_ref, bf16[1536,320]{1,0:T(8,128)(2,1)S(1)} %bitcast.230), kind=kOutput, calls=%fused_computation.142 | convolution fusion | flops 1012922880 | bytes 7936000 | tf_op jit(solution)/shard_map/dot_general | solution.py:39
  313.4 5.9 %all-to-all-start.5 = ((bf16[128,16,320]{2,1,0:T(8,128)(2,1)}), bf16[128,16,320]{2,1,0:T(8,128)(2,1)S(1)}, u32[]{:S(2)}, u32[]{:S(2)}) async-start(bf16[128,16,320]{2,1,0:T(8,128)(2,1)} %shard_map.234), calls=%async_computation.7 | async-start | bytes 3145728 | tf_op jit(solution)/shard_map/all_to_all | solution.py:104
  325.4 19.4 %all-to-all-done.5.came_ref = bf16[128,16,320]{2,1,0:T(8,128)(2,1)S(1)} async-done(((bf16[128,16,320]{2,1,0:T(8,128)(2,1)}), bf16[128,16,320]{2,1,0:T(8,128)(2,1)S(1)}, u32[]{:S(2)}, u32[]{:S(2)}) %all-to-all-start.5) | async-done | bytes 1310752 | tf_op jit(solution)/shard_map/all_to_all | solution.py:104
  349.2 3.7 collective-permute-done.27
  359.5 7.2 %collective-permute-done.30 = bf16[128,1536]{1,0:T(8,128)(2,1)S(1)} collective-permute-done((bf16[128,1536]{1,0:T(8,128)(2,1)S(1)}, bf16[128,1536]{1,0:T(8,128)(2,1)S(1)}, u32[]{:S(2)}, u32[]{:S(2)}) %collective-permute-start.30) | collective-permute-done | bytes 393248 | tf_op jit(solution)/shard_map/ppermute | solution.py:62
  367.9 5.3 %collective-permute-done.28 = bf16[2,368,384]{2,1,0:T(8,128)(2,1)S(1)} collective-permute-done((bf16[2,368,384]{2,1,0:T(8,128)(2,1)S(1)}, bf16[2,368,384]{2,1,0:T(8,128)(2,1)S(1)}, u32[]{:S(2)}, u32[]{:S(2)}) %collective-permute-start.28) | collective-permute-done | bytes 565280 | tf_op jit(solution)/shard_map/ppermute | solution.py:62
  373.3 19.3 %collective-permute-done.32 = bf16[2,368,384]{2,1,0:T(8,128)(2,1)S(1)} collective-permute-done((bf16[2,368,384]{2,1,0:T(8,128)(2,1)S(1)}, bf16[2,368,384]{2,1,0:T(8,128)(2,1)S(1)}, u32[]{:S(2)}, u32[]{:S(2)}) %collective-permute-start.32) | collective-permute-done | bytes 565280 | tf_op jit(solution)/shard_map/ppermute | solution.py:62
  (308 shorter events, 155.7 us)
Async XLA Ops:
  7.2 47.6 %all-gather.6.cloned.1.call-start = ((), (), s32[]{:S(2)}) async-start(), calls=%async_computation.8 | async-start | bytes 3538944 | tf_op jit(solution)/shard_map/all_gather | solution.py:445
  16.5 32.2 %all-to-all-start = ((bf16[16,96,320]{2,1,0:T(8,128)(2,1)}), bf16[16,96,320]{2,1,0:T(8,128)(2,1)S(1)}, u32[]{:S(2)}, u32[]{:S(2)}) async-start(bf16[16,96,320]{2,1,0:T(8,128)(2,1)} %pad_maximum_fusion.3), calls=%async_computation | async-start | bytes 2359296 | tf_op jit(solution)/shard_map/all_to_all | solution.py:104
  21.9 122.8 %all-gather.8.cloned.1.call-start = ((), (), s32[]{:S(2)}) async-start(), calls=%async_computation.9 | async-start | bytes 3538944 | tf_op jit(solution)/shard_map/all_gather | solution.py:452
  49.7 36.2 %all-to-all-start.1 = ((bf16[16,48,864]{2,1,0:T(8,128)(2,1)}), bf16[16,48,864]{2,1,0:T(8,128)(2,1)S(1)}, u32[]{:S(2)}, u32[]{:S(2)}) async-start(bf16[16,48,864]{2,1,0:T(8,128)(2,1)} %shard_map.228), calls=%async_computation.1 | async-start | bytes 2752512 | tf_op jit(solution)/shard_map/all_to_all | solution.py:104
  54.8 100.6 %all-gather.12.cloned.1.call-start = ((), (), s32[]{:S(2)}) async-start(), calls=%async_computation.13 | async-start | bytes 6881280 | tf_op jit(solution)/shard_map/all_gather | solution.py:480
  58.8 18.7 %collective-permute-start.2 = (bf16[128,1024]{1,0:T(8,128)(2,1)S(1)}, bf16[128,1024]{1,0:T(8,128)(2,1)S(1)}, u32[]{:S(2)}, u32[]{:S(2)}) collective-permute-start(bf16[128,1024]{1,0:T(8,128)(2,1)S(1)} %slice.154), channel_id=1, source_target_pairs={{0,8},{8,0},{1,9},{9,1},{2,10},{10,2},{3,11},{11,3},{4,12},{12,4},... | collective-permute-start | bytes 786440 | tf_op jit(solution)/shard_map/ppermute | solution.py:70
  91.1 160.8 %reduce-scatter.5.cloned.1.call-start = ((), (), s32[]{:S(2)}) async-start(), calls=%async_computation.11 | async-start | bytes 6881280 | tf_op jit(solution)/shard_map/reduce_scatter | solution.py:504
  97.6 13.7 %collective-permute-start.4 = (bf16[128,1536]{1,0:T(8,128)(2,1)}, bf16[128,1536]{1,0:T(8,128)(2,1)S(1)}, u32[]{:S(2)}, u32[]{:S(2)}) collective-permute-start(bf16[128,1536]{1,0:T(8,128)(2,1)} %get-tuple-element.146), channel_id=1, source_target_pairs={{0,4},{2,6},{4,0},{6,2},{1,5},{3,7},{5,1},{7,3},{8,12},{10,14},{12... | collective-permute-start | bytes 1179656 | tf_op jit(solution)/shard_map/ppermute | solution.py:62
  100.3 18.6 %collective-permute-start.5 = (bf16[128,1536]{1,0:T(8,128)(2,1)}, bf16[128,1536]{1,0:T(8,128)(2,1)}, u32[]{:S(2)}, u32[]{:S(2)}) collective-permute-start(bf16[128,1536]{1,0:T(8,128)(2,1)} %get-tuple-element.148), channel_id=1, source_target_pairs={{0,2},{2,4},{4,6},{6,0},{1,3},{3,5},{5,7},{7,1},{8,10},{10,12},{12... | collective-permute-start | bytes 1179656 | tf_op jit(solution)/shard_map/ppermute | solution.py:62
  100.6 18.3 %collective-permute-start.6 = (bf16[128,1536]{1,0:T(8,128)(2,1)}, bf16[128,1536]{1,0:T(8,128)(2,1)}, u32[]{:S(2)}, u32[]{:S(2)}) collective-permute-start(bf16[128,1536]{1,0:T(8,128)(2,1)} %get-tuple-element.147), channel_id=1, source_target_pairs={{0,6},{2,0},{4,2},{6,4},{1,7},{3,1},{5,3},{7,5},{8,14},{10,8},{12,... | collective-permute-start | bytes 1179656 | tf_op jit(solution)/shard_map/ppermute | solution.py:62
  104.1 21.5 %collective-permute-start.7 = (bf16[216,1536]{1,0:T(8,128)(2,1)}, bf16[216,1536]{1,0:T(8,128)(2,1)S(1)}, u32[]{:S(2)}, u32[]{:S(2)}) collective-permute-start(bf16[216,1536]{1,0:T(8,128)(2,1)} %get-tuple-element.150), channel_id=1, source_target_pairs={{0,8},{8,16},{16,24},{24,0},{1,9},{9,17},{17,25},{25,1},{2,10},{10... | collective-permute-start | bytes 1990664 | tf_op jit(solution)/shard_map/ppermute | solution.py:62
  108.4 17.2 %collective-permute-start.8 = (bf16[216,1536]{1,0:T(8,128)(2,1)}, bf16[216,1536]{1,0:T(8,128)(2,1)}, u32[]{:S(2)}, u32[]{:S(2)}) collective-permute-start(bf16[216,1536]{1,0:T(8,128)(2,1)} %get-tuple-element.149), channel_id=1, source_target_pairs={{0,24},{8,0},{16,8},{24,16},{1,25},{9,1},{17,9},{25,17},{2,26},{10... | collective-permute-start | bytes 1990664 | tf_op jit(solution)/shard_map/ppermute | solution.py:62
  126.9 14.6 %collective-permute-start.10 = (bf16[128,1536]{1,0:T(8,128)(2,1)S(1)}, bf16[128,1536]{1,0:T(8,128)(2,1)S(1)}, u32[]{:S(2)}, u32[]{:S(2)}) collective-permute-start(bf16[128,1536]{1,0:T(8,128)(2,1)S(1)} %get-tuple-element.124), channel_id=1, source_target_pairs={{0,2},{2,4},{4,6},{6,0},{1,3},{3,5},{5,7},{7,1},{8,10},{10,12},{12... | collective-permute-start | bytes 1179656 | tf_op jit(solution)/shard_map/ppermute | solution.py:62
  127.0 14.6 %collective-permute-start.11 = (bf16[128,1536]{1,0:T(8,128)(2,1)S(1)}, bf16[128,1536]{1,0:T(8,128)(2,1)S(1)}, u32[]{:S(2)}, u32[]{:S(2)}) collective-permute-start(bf16[128,1536]{1,0:T(8,128)(2,1)S(1)} %get-tuple-element.124), channel_id=1, source_target_pairs={{0,6},{2,0},{4,2},{6,4},{1,7},{3,1},{5,3},{7,5},{8,14},{10,8},{12,... | collective-permute-start | bytes 1179656 | tf_op jit(solution)/shard_map/ppermute | solution.py:62
  192.7 18.4 %collective-permute-start.14 = (bf16[128,1536]{1,0:T(8,128)(2,1)}, bf16[128,1536]{1,0:T(8,128)(2,1)S(1)}, u32[]{:S(2)}, u32[]{:S(2)}) collective-permute-start(bf16[128,1536]{1,0:T(8,128)(2,1)} %get-tuple-element.143), channel_id=1, source_target_pairs={{0,4},{2,6},{4,0},{6,2},{1,5},{3,7},{5,1},{7,3},{8,12},{10,14},{12... | collective-permute-start | bytes 1179656 | tf_op jit(solution)/shard_map/ppermute | solution.py:62
  195.4 18.6 %collective-permute-start.15 = (bf16[128,1536]{1,0:T(8,128)(2,1)}, bf16[128,1536]{1,0:T(8,128)(2,1)}, u32[]{:S(2)}, u32[]{:S(2)}) collective-permute-start(bf16[128,1536]{1,0:T(8,128)(2,1)} %get-tuple-element.145), channel_id=1, source_target_pairs={{0,2},{2,4},{4,6},{6,0},{1,3},{3,5},{5,7},{7,1},{8,10},{10,12},{12... | collective-permute-start | bytes 1179656 | tf_op jit(solution)/shard_map/ppermute | solution.py:62
  195.7 18.3 %collective-permute-start.16 = (bf16[128,1536]{1,0:T(8,128)(2,1)S(1)}, bf16[128,1536]{1,0:T(8,128)(2,1)}, u32[]{:S(2)}, u32[]{:S(2)}) collective-permute-start(bf16[128,1536]{1,0:T(8,128)(2,1)S(1)} %get-tuple-element.144), channel_id=1, source_target_pairs={{0,6},{2,0},{4,2},{6,4},{1,7},{3,1},{5,3},{7,5},{8,14},{10,8},{12,... | collective-permute-start | bytes 1179656 | tf_op jit(solution)/shard_map/ppermute | solution.py:62
  204.5 39.5 %all-to-all-start.2 = ((bf16[4,216,1536]{2,1,0:T(8,128)(2,1)}), bf16[4,216,1536]{2,1,0:T(8,128)(2,1)}, u32[]{:S(2)}, u32[]{:S(2)}) async-start(bf16[4,216,1536]{2,1,0:T(8,128)(2,1)} %bitcast.223), calls=%async_computation.2 | async-start | bytes 5308416 | tf_op jit(solution)/shard_map/all_to_all | solution.py:104
  211.1 186.0 %reduce-scatter.3.cloned.1.call-start = ((), (), s32[]{:S(2)}) async-start(), calls=%async_computation.10 | async-start | bytes 3538944 | tf_op jit(solution)/shard_map/reduce_scatter | solution.py:514
  218.9 20.2 %collective-permute-start.18 = (bf16[128,1536]{1,0:T(8,128)(2,1)}, bf16[128,1536]{1,0:T(8,128)(2,1)S(1)}, u32[]{:S(2)}, u32[]{:S(2)}) collective-permute-start(bf16[128,1536]{1,0:T(8,128)(2,1)} %get-tuple-element.122), channel_id=1, source_target_pairs={{0,2},{2,4},{4,6},{6,0},{1,3},{3,5},{5,7},{7,1},{8,10},{10,12},{12... | collective-permute-start | bytes 1179656 | tf_op jit(solution)/shard_map/ppermute | solution.py:62
  220.8 18.3 %collective-permute-start.19 = (bf16[128,1536]{1,0:T(8,128)(2,1)}, bf16[128,1536]{1,0:T(8,128)(2,1)S(1)}, u32[]{:S(2)}, u32[]{:S(2)}) collective-permute-start(bf16[128,1536]{1,0:T(8,128)(2,1)} %get-tuple-element.122), channel_id=1, source_target_pairs={{0,6},{2,0},{4,2},{6,4},{1,7},{3,1},{5,3},{7,5},{8,14},{10,8},{12,... | collective-permute-start | bytes 1179656 | tf_op jit(solution)/shard_map/ppermute | solution.py:62
  251.9 33.1 %all-to-all-start.3 = ((bf16[32,24,864]{2,1,0:T(8,128)(2,1)}), bf16[32,24,864]{2,1,0:T(8,128)(2,1)}, u32[]{:S(2)}, u32[]{:S(2)}) async-start(bf16[32,24,864]{2,1,0:T(8,128)(2,1)} %bitcast.227), calls=%async_computation.5 | async-start | bytes 2752512 | tf_op jit(solution)/shard_map/all_to_all | solution.py:104
  270.1 19.4 %collective-permute-start.22 = (bf16[128,1024]{1,0:T(8,128)(2,1)S(1)}, bf16[128,1024]{1,0:T(8,128)(2,1)S(1)}, u32[]{:S(2)}, u32[]{:S(2)}) collective-permute-start(bf16[128,1024]{1,0:T(8,128)(2,1)S(1)} %get-tuple-element.91), channel_id=1, source_target_pairs={{0,8},{8,0},{1,9},{9,1},{2,10},{10,2},{3,11},{11,3},{4,12},{12,4},... | collective-permute-start | bytes 786440 | tf_op jit(solution)/shard_map/ppermute | solution.py:70
  284.9 17.2 %all-to-all-start.4 = ((bf16[16,12,1536]{2,1,0:T(8,128)(2,1)}), bf16[16,12,1536]{2,1,0:T(8,128)(2,1)}, u32[]{:S(2)}, u32[]{:S(2)}) async-start(bf16[16,12,1536]{2,1,0:T(8,128)(2,1)} %bitcast.216), calls=%async_computation.6 | async-start | bytes 1572864 | tf_op jit(solution)/shard_map/all_to_all | solution.py:104
  304.8 18.2 %collective-permute-start.26 = (bf16[4,128,1536]{2,1,0:T(8,128)(2,1)}, bf16[4,128,1536]{2,1,0:T(8,128)(2,1)}, u32[]{:S(2)}, u32[]{:S(2)}) collective-permute-start(bf16[4,128,1536]{2,1,0:T(8,128)(2,1)} %dynamic-slice_bitcast_fusion), channel_id=1, source_target_pairs={{0,1},{1,0},{2,3},{3,2},{4,5},{5,4},{6,7},{7,6},{8,9},{9,8},{10,11... | collective-permute-start | bytes 4718600 | tf_op jit(solution)/shard_map/ppermute | solution.py:70
  313.4 31.4 %all-to-all-start.5 = ((bf16[128,16,320]{2,1,0:T(8,128)(2,1)}), bf16[128,16,320]{2,1,0:T(8,128)(2,1)S(1)}, u32[]{:S(2)}, u32[]{:S(2)}) async-start(bf16[128,16,320]{2,1,0:T(8,128)(2,1)} %shard_map.234), calls=%async_computation.7 | async-start | bytes 3145728 | tf_op jit(solution)/shard_map/all_to_all | solution.py:104
  319.3 80.2 %all-gather.10.cloned.1.call-start = ((), (), s32[]{:S(2)}) async-start(), calls=%async_computation.12 | async-start | bytes 3096576 | tf_op jit(solution)/shard_map/all_gather | solution.py:571
  346.5 20.2 %collective-permute-start.30 = (bf16[128,1536]{1,0:T(8,128)(2,1)S(1)}, bf16[128,1536]{1,0:T(8,128)(2,1)S(1)}, u32[]{:S(2)}, u32[]{:S(2)}) collective-permute-start(bf16[128,1536]{1,0:T(8,128)(2,1)S(1)} %get-tuple-element.142), channel_id=1, source_target_pairs={{0,2},{2,4},{4,6},{6,0},{1,3},{3,5},{5,7},{7,1},{8,10},{10,12},{12... | collective-permute-start | bytes 1179656 | tf_op jit(solution)/shard_map/ppermute | solution.py:62
  347.8 18.9 %collective-permute-start.31 = (bf16[128,1536]{1,0:T(8,128)(2,1)S(1)}, bf16[128,1536]{1,0:T(8,128)(2,1)S(1)}, u32[]{:S(2)}, u32[]{:S(2)}) collective-permute-start(bf16[128,1536]{1,0:T(8,128)(2,1)S(1)} %get-tuple-element.141), channel_id=1, source_target_pairs={{0,6},{2,0},{4,2},{6,4},{1,7},{3,1},{5,3},{7,5},{8,14},{10,8},{12,... | collective-permute-start | bytes 1179656 | tf_op jit(solution)/shard_map/ppermute | solution.py:62
  353.1 20.1 %collective-permute-start.28 = (bf16[2,368,384]{2,1,0:T(8,128)(2,1)S(1)}, bf16[2,368,384]{2,1,0:T(8,128)(2,1)S(1)}, u32[]{:S(2)}, u32[]{:S(2)}) collective-permute-start(bf16[2,368,384]{2,1,0:T(8,128)(2,1)S(1)} %pad_maximum_fusion.7), channel_id=1, source_target_pairs={{0,64},{32,96},{64,0},{96,32},{1,65},{33,97},{65,1},{97,33},{2,66}... | collective-permute-start | bytes 1695752 | tf_op jit(solution)/shard_map/ppermute | solution.py:62
  356.2 36.4 %collective-permute-start.32 = (bf16[2,368,384]{2,1,0:T(8,128)(2,1)S(1)}, bf16[2,368,384]{2,1,0:T(8,128)(2,1)S(1)}, u32[]{:S(2)}, u32[]{:S(2)}) collective-permute-start(bf16[2,368,384]{2,1,0:T(8,128)(2,1)S(1)} %pad_maximum_fusion.7), channel_id=1, source_target_pairs={{0,32},{32,64},{64,96},{96,0},{1,33},{33,65},{65,97},{97,1},{2,34}... | collective-permute-start | bytes 1695752 | tf_op jit(solution)/shard_map/ppermute | solution.py:62
  356.5 36.2 %collective-permute-start.33 = (bf16[2,368,384]{2,1,0:T(8,128)(2,1)S(1)}, bf16[2,368,384]{2,1,0:T(8,128)(2,1)S(1)}, u32[]{:S(2)}, u32[]{:S(2)}) collective-permute-start(bf16[2,368,384]{2,1,0:T(8,128)(2,1)S(1)} %pad_maximum_fusion.7), channel_id=1, source_target_pairs={{0,96},{32,0},{64,32},{96,64},{1,97},{33,1},{65,33},{97,65},{2,98}... | collective-permute-start | bytes 1695752 | tf_op jit(solution)/shard_map/ppermute | solution.py:62
  (77 other events, 537.3 us)
Sparse Core Ops, SparseCore 0:
  10.5 42.4 all-gather.5
  54.7 33.2 all-gather.7
  91.2 64.1 all-gather.11
  190.4 61.4 reduce-scatter.4
  254.1 43.5 reduce-scatter.2
  322.9 69.1 all-gather.9
